TPU v7x, 128 devices: a whole 4x4x4 slice. The times are simulated.
128 devices in a mesh: gz: 4 (over z_lo, core), gy: 8 (over z_hi, x), vec: 4 (over y).
Axes of the slice: x: 4, y: 4, z: 4 (z_hi: 2, z_lo: 2; z = z_hi * 2 + z_lo), core: 2. Of those that a mesh axis runs over, the one named last changes fastest.
Arguments:
- vectors: bfloat16 [256, 3, 32, 16, 128], P('vec', None, 'gz', 'gy'), may hold values from -6 to 6
- links: bfloat16 [3, 3, 3, 32, 16, 128], P(None, None, None, 'gz', 'gy'), may hold values from -4 to 4
- momentum: int32 [3], replicated, may hold values from -5 to 5, as said below
- directions: int32 [3], replicated, may hold values from 0 to 2, each once
Outputs:
- elementals: float32 [4, 2, 256, 256], P(None, None, 'vec')
Inputs may be any that keep to these rules, and one draw needn't show every extreme that they name: `momentum`: one component is -5, another 5. `directions`: each of 0, 1, 2 once.
All inputs are finite; a program needn't handle non-finite values.
Results may differ from a plain program's by a relative error of at most 0.0029.
Values may be sent and summed in bfloat16 or wider, within the bound.
No kernel may reach another device: no remote copies, remote signals or barrier semaphores. Data moves between devices by JAX's collectives and lax.ppermute only.
A program may use at most 128 MiB of HBM per device.

v0:
```python
import math

import jax
import jax.numpy as jnp
from jax import lax
from jax.sharding import PartitionSpec as P


def shifted(value, axis, steps):
    count = lax.axis_size(axis)
    pairs = [(source, (source + steps) % count) for source in range(count)]
    return lax.ppermute(value, axis, pairs)


def with_halo(x, sides, width):
    edges = {}
    for axis, dim in sides:
        size, length = (lax.axis_size(axis), x.shape[dim])
        up = [(i, (i + 1) % size) for i in range(size)]
        last = lax.slice_in_dim(x, length - width, length, axis=dim)
        first = lax.slice_in_dim(x, 0, width, axis=dim)
        edges[dim] = (
            lax.ppermute(last, axis, up),
            lax.ppermute(first, axis, [(b, a) for a, b in up]),
        )
    done = []
    for _, dim in sides:
        low, high = edges[dim]
        around = [(width, width) if d in done else (0, 0) for d in range(x.ndim)]
        x = jnp.concatenate([jnp.pad(low, around), x, jnp.pad(high, around)], axis=dim)
        done.append(dim)
    return x


def split_up(x, dim, size):
    shape = x.shape
    pieces = x.reshape(*shape[:dim], size, shape[dim] // size, *shape[dim + 1 :])
    return jnp.moveaxis(pieces, dim, 0)


def summed_on_arrival(x, axis, dim):
    pieces = split_up(x, dim, lax.axis_size(axis))
    arrived = lax.all_to_all(pieces, axis, split_axis=0, concat_axis=0, tiled=True)
    return arrived.sum(axis=0)


def rows_for(lines, size):
    spare = -lines.shape[0] % size
    if not spare:
        return lines
    return jnp.concatenate([lines, jnp.zeros((spare, *lines.shape[1:]), lines.dtype)])


def laid_out(pieces, dim):
    shape = list(pieces.shape[1:])
    shape[dim] *= pieces.shape[0]
    return jnp.moveaxis(pieces, 0, dim).reshape(shape)


def from_everyone(x, axis):
    copies = jnp.broadcast_to(x, (lax.axis_size(axis), *x.shape))
    return lax.all_to_all(copies, axis, split_axis=0, concat_axis=0, tiled=True)


def gather_directly(x, axis, dim):
    return laid_out(from_everyone(x, axis), dim)


def nested_sum(x, axes):
    lines = x.reshape(-1, x.shape[-1])
    own = summed_on_arrival(rows_for(lines, lax.axis_size(axes)), axes, 0)
    whole = gather_directly(own, axes, 0)
    return whole[: len(lines)].reshape(x.shape)


def apply_link(link_pair, field_pair):
    link_real, link_imag = link_pair
    field_real, field_imag = field_pair
    out_real = 0.0
    out_imag = 0.0
    for column in range(3):
        coeff_real = link_real[:, column][None]
        coeff_imag = link_imag[:, column][None]
        value_real = field_real[:, column][:, None]
        value_imag = field_imag[:, column][:, None]
        out_real = out_real + coeff_real * value_real - coeff_imag * value_imag
        out_imag = out_imag + coeff_real * value_imag + coeff_imag * value_real
    return (out_real, out_imag)


def apply_adjoint(link_pair, field_pair):
    link_real, link_imag = link_pair
    field_real, field_imag = field_pair
    out_real = 0.0
    out_imag = 0.0
    for column in range(3):
        coeff_real = link_real[column][None]
        coeff_imag = link_imag[column][None]
        value_real = field_real[:, column][:, None]
        value_imag = field_imag[:, column][:, None]
        out_real = out_real + coeff_real * value_real + coeff_imag * value_imag
        out_imag = out_imag + coeff_real * value_imag - coeff_imag * value_real
    return (out_real, out_imag)


def covariant(up_pair, down_pair, ahead_pair, behind_pair):
    forward = apply_link(up_pair, ahead_pair)
    backward = apply_adjoint(down_pair, behind_pair)
    return (0.5 * (forward[0] - backward[0]), 0.5 * (forward[1] - backward[1]))


def phase_table(momentum, x_coords, y_coords, z_coords, extent_x, extent_y, extent_z):
    frac_x = (momentum[0] * x_coords % extent_x).astype(jnp.float32) / extent_x
    frac_y = (momentum[1] * y_coords % extent_y).astype(jnp.float32) / extent_y
    frac_z = (momentum[2] * z_coords % extent_z).astype(jnp.float32) / extent_z
    summed = frac_z[:, None, None] + frac_y[None, :, None] + frac_x[None, None, :]
    angle = 2.0 * math.pi * summed
    return (jnp.cos(angle), jnp.sin(angle))


def make_operators(
    field_pair, ahead_list, behind_list, up_list, down_list, directions, cosine, sine
):
    derived = [
        covariant(
            up_list[axis_number],
            down_list[axis_number],
            ahead_list[axis_number],
            behind_list[axis_number],
        )
        for axis_number in range(3)
    ]
    results = []
    for op_slot in range(3):
        chosen = directions[op_slot]
        real_part = jnp.where(
            chosen == 0, derived[0][0], jnp.where(chosen == 1, derived[1][0], derived[2][0])
        )
        imag_part = jnp.where(
            chosen == 0, derived[0][1], jnp.where(chosen == 1, derived[1][1], derived[2][1])
        )
        results.append(jnp.stack([real_part, imag_part], -2).astype(jnp.bfloat16))
    field_real, field_imag = field_pair
    phased_real = field_real * cosine + field_imag * sine
    phased_imag = field_imag * cosine - field_real * sine
    results.append(jnp.stack([phased_real, phased_imag], -2).astype(jnp.bfloat16))
    return jnp.stack(results, 1)


def contract(rows, stacked_left):
    row_count = rows.shape[0]
    flat_rows = rows.reshape(row_count * 4, -1)
    product = lax.dot_general(
        flat_rows, stacked_left, (((1,), (1,)), ((), ())), preferred_element_type=jnp.float32
    )
    return product.reshape(row_count, 4, 2, stacked_left.shape[0] // 2)


def stack_left(six_dims):
    row_count = six_dims.shape[0]
    swapped = jnp.stack([-six_dims[..., 1, :], six_dims[..., 0, :]], -2)
    return jnp.concatenate([six_dims.reshape(row_count, -1), swapped.reshape(row_count, -1)], 0)


def link_parts(link_six):
    widened = link_six.astype(jnp.float32)
    return (widened[..., 0, :], widened[..., 1, :])


def stencil_lists(padded, row_count, slab_depth, height, width):
    widened = padded.astype(jnp.float32).reshape(row_count, 3, slab_depth + 2, height + 2, 2, width)
    pad_real = widened[..., 0, :]
    pad_imag = widened[..., 1, :]
    centre_real = pad_real[:, :, 1:-1, 1:-1]
    centre_imag = pad_imag[:, :, 1:-1, 1:-1]
    ahead_list = [
        (jnp.roll(centre_real, -1, axis=-1), jnp.roll(centre_imag, -1, axis=-1)),
        (pad_real[:, :, 1:-1, 2:], pad_imag[:, :, 1:-1, 2:]),
        (pad_real[:, :, 2:, 1:-1], pad_imag[:, :, 2:, 1:-1]),
    ]
    behind_list = [
        (jnp.roll(centre_real, 1, axis=-1), jnp.roll(centre_imag, 1, axis=-1)),
        (pad_real[:, :, 1:-1, :-2], pad_imag[:, :, 1:-1, :-2]),
        (pad_real[:, :, :-2, 1:-1], pad_imag[:, :, :-2, 1:-1]),
    ]
    return ((centre_real, centre_imag), ahead_list, behind_list)


def body(vectors, links, momentum, directions):
    local_count = vectors.shape[0]
    depth = vectors.shape[2]
    height = vectors.shape[3]
    width = vectors.shape[4] // 2
    links_six = links.reshape(3, 3, 3, depth, height, 2, width)
    x_down = jnp.roll(links_six[0], 1, axis=-1)
    y_link = links_six[1]
    y_rim = shifted(y_link[:, :, :, -1:], "gy", 1)
    y_down = jnp.concatenate([y_rim, y_link[:, :, :, :-1]], 3)
    z_link = links_six[2]
    z_rim = shifted(z_link[:, :, -1:], "gz", 1)
    z_down = jnp.concatenate([z_rim, z_link[:, :, :-1]], 2)
    up_six = [links_six[0], y_link, z_link]
    down_six = [x_down, y_down, z_down]
    extent_y = height * lax.axis_size("gy")
    extent_z = depth * lax.axis_size("gz")
    y_coords = lax.axis_index("gy") * height + jnp.arange(height, dtype=jnp.int32)
    z_coords = lax.axis_index("gz") * depth + jnp.arange(depth, dtype=jnp.int32)
    padded = with_halo(vectors, (("gz", 2), ("gy", 3)), 1)
    centre, ahead_list, behind_list = stencil_lists(padded, local_count, depth, height, width)
    up_list = [link_parts(link_six) for link_six in up_six]
    down_list = [link_parts(link_six) for link_six in down_six]
    cosine, sine = phase_table(
        momentum, jnp.arange(width, dtype=jnp.int32), y_coords, z_coords, width, extent_y, extent_z
    )
    transformed = make_operators(
        centre, ahead_list, behind_list, up_list, down_list, directions, cosine, sine
    )
    transformed_rows = transformed.reshape(local_count, 4, -1)
    left_piece = lax.all_gather(vectors, "vec", axis=0, tiled=True)
    piece_rows = left_piece.shape[0]
    six_dims = left_piece.reshape(piece_rows, 3, depth, height, 2, width)
    terms = contract(transformed_rows, stack_left(six_dims))
    summed = nested_sum(terms, ("gz", "gy"))
    scaled = summed * (1.0 / math.sqrt(width * extent_y * extent_z))
    return jnp.transpose(scaled, (1, 2, 0, 3))


def solution(mesh):
    in_specs = (P("vec", None, "gz", "gy", None), P(None, None, None, "gz", "gy", None), P(), P())
    out_specs = P(None, None, "vec", None)
    return jax.shard_map(body, mesh=mesh, in_specs=in_specs, out_specs=out_specs, check_vma=False)
```

profile of v0, /device:TPU:1, one launch (start us, length us, event | category | flops | bytes accessed | tf_op | source)
XLA Modules:
  0.0 170.1 jit_solution(15549379246333246910)
XLA Ops:
  6.5 1.1 fusion.50
  7.6 1.5 collective-permute-start.2
  9.1 1.7 collective-permute-start.1
  10.8 2.1 %copy.61 = bf16[64,3,8,2,128]{4,2,3,1,0:T(8,128)(2,1)} copy(bf16[64,3,8,2,128]{4,3,2,1,0:T(2,128)(2,1)} %param.4) | data formatting | bytes 1572864 | tf_op args[0]
  13.0 2.0 %fusion.49 = (bf16[64,3,8,1,128]{4,2,3,1,0:T(8,128)(2,1)}, bf16[64,3,8,1,128]{4,2,3,1,0:T(8,128)(2,1)S(1)}) fusion(bf16[64,3,8,2,128]{4,2,3,1,0:T(8,128)(2,1)} %copy.61), kind=kLoop, calls=%fused_computation.172 | loop fusion | bytes 1572864 | tf_op jit(solution)/shard_map/slice | solution.py:20
  14.9 1.2 collective-permute-start
  16.1 4.3 %collective-permute-start.3 = (bf16[64,3,8,1,128]{4,2,3,1,0:T(8,128)(2,1)S(1)}, bf16[64,3,8,1,128]{4,2,3,1,0:T(8,128)(2,1)}, u32[]{:S(2)}, u32[]{:S(2)}) collective-permute-start(bf16[64,3,8,1,128]{4,2,3,1,0:T(8,128)(2,1)S(1)} %get-tuple-element.68), channel_id=1, source_target_pairs={{4,0},{8,4},{12,8},{16,12},{20,16},{24,20},{28,24},{0,28},{5,1},{9... | collective-permute-start | bytes 1179656 | tf_op jit(solution)/shard_map/ppermute | solution.py:24
  32.8 6.8 %collective-permute-done.4 = bf16[3,3,8,1,2,64]{5,3,2,1,4,0:T(2,128)(2,1)S(1)} collective-permute-done((bf16[3,3,8,1,2,64]{5,3,2,1,4,0:T(2,128)(2,1)S(1)}, bf16[3,3,8,1,2,64]{5,3,2,1,4,0:T(2,128)(2,1)S(1)}, u32[]{:S(2)}, u32[]{:S(2)}) %collective-permute-start.4) | collective-permute-done | bytes 18464 | tf_op jit(solution)/shard_map/ppermute | solution.py:12
  40.4 1.5 pad_maximum_fusion.1
  42.2 0.8 concatenate.74
  43.0 2.1 %pad.7 = bf16[64,3,10,1,128]{4,2,3,1,0:T(8,128)(2,1)} pad(bf16[64,3,8,1,128]{4,2,3,1,0:T(8,128)(2,1)} %collective-permute-done, bf16[]{:T(256)} %constant.65.clone.1), padding=0_0x0_0x1_1x0_0x0_0 | pad | bytes 884738 | tf_op jit(solution)/shard_map/jit(_pad)/pad | solution.py:30
  45.1 2.5 %reshape.734 = bf16[64,3,10,1,2,64]{5,4,2,1,0,3:T(2,128)(2,1)S(1)} reshape(bf16[64,3,10,1,128]{4,2,3,1,0:T(8,128)(2,1)} %pad.7) | data formatting | bytes 983040 | tf_op jit(solution)/shard_map/concatenate | solution.py:30
  47.6 2.1 %pad.8 = bf16[64,3,10,1,128]{4,2,3,1,0:T(8,128)(2,1)} pad(bf16[64,3,8,1,128]{4,2,3,1,0:T(8,128)(2,1)} %collective-permute-done.3, bf16[]{:T(256)} %constant.65.clone.1), padding=0_0x0_0x1_1x0_0x0_0 | pad | bytes 884738 | tf_op jit(solution)/shard_map/jit(_pad)/pad | solution.py:30
  49.7 3.2 %reshape.735 = bf16[64,3,10,1,2,64]{5,4,2,1,0,3:T(2,128)(2,1)} reshape(bf16[64,3,10,1,128]{4,2,3,1,0:T(8,128)(2,1)} %pad.8) | data formatting | bytes 983040 | tf_op jit(solution)/shard_map/concatenate | solution.py:30
  52.9 6.6 %maximum_convert_fusion = f32[64,3,10,4,2,64]{5,4,0,3,2,1:T(2,128)S(1)} fusion(bf16[64,3,10,2,2,64]{5,4,0,3,2,1:T(2,128)(2,1)S(1)} %concatenate.74, bf16[64,3,10,1,2,64]{5,4,2,1,0,3:T(2,128)(2,1)S(1)} %reshape.734, bf16[64,3,10,1,2,64]{5,4,2,1,0,3:T(2,128)(2,1)} %reshape.735), kind=kLoop, calls=%fused_computation.5 | loop fusion | flops 5898240 | bytes 5898240 | tf_op jit(solution)/shard_map/convert_element_type | solution.py:171
  59.6 8.3 %fusion.44 = (f32[64,3,10,4,1,64]{5,4,0,3,2,1:T(1,128)S(1)}, f32[64,3,10,4,1,64]{5,4,0,3,2,1:T(1,128)S(1)}) fusion(f32[64,3,10,4,2,64]{5,4,0,3,2,1:T(2,128)S(1)} %maximum_convert_fusion), kind=kLoop, calls=%fused_computation.167 | loop fusion | bytes 7864320 | tf_op jit(solution)/shard_map/slice | solution.py:173
  67.9 1.0 slice_bitcast_fusion.23
  70.2 1.0 slice_bitcast_fusion.22
  72.4 0.9 fusion.19
  73.6 0.9 fusion.15
  74.7 8.4 %fusion.5 = (bf16[64,1,3,8,2,1,64]{6,0,4,3,2,5,1:T(8,128)(2,1)S(1)}, bf16[64,3,8,2,1,64]{5,0,3,2,1,4:T(8,128)(2,1)S(1)}, bf16[64,3,8,2,1,64]{5,0,3,2,1,4:T(8,128)(2,1)S(1)}, bf16[64,3,8,2,1,64]{5,0,3,2,1,4:T(8,128)(2,1)S(1)}) fusion(pred[]{:T(512)} %bitcast.29, pred[]{:T(512)} %bitcast, f32[64,8,2,64]{3,0,2,1:T(8,128)S(1)} %get-tuple-element.38, ...), kind=kLoop, calls=%fused_computation.40 | loop fusion | flops 15138816 | bytes 11452418 | tf_op jit(solution)/shard_map/stack | solution.py:142
  83.3 8.2 %fusion.4 = (bf16[64,1,3,8,2,1,64]{6,0,4,3,2,5,1:T(8,128)(2,1)S(1)}, bf16[64,3,8,2,1,64]{5,0,3,2,1,4:T(8,128)(2,1)S(1)}, bf16[64,3,8,2,1,64]{5,0,3,2,1,4:T(8,128)(2,1)S(1)}, bf16[64,3,8,2,1,64]{5,0,3,2,1,4:T(8,128)(2,1)S(1)}) fusion(pred[]{:T(512)} %bitcast.29, pred[]{:T(512)} %bitcast, f32[64,8,2,64]{3,0,2,1:T(8,128)S(1)} %get-tuple-element.26, ...), kind=kLoop, calls=%fused_computation.39 | loop fusion | flops 15138816 | bytes 11452418 | tf_op jit(solution)/shard_map/stack | solution.py:142
  92.1 2.2 %maximum_maximum_fusion = bf16[64,4,3,8,2,2,64]{6,0,4,3,2,5,1:T(8,128)(2,1)S(1)} fusion(bf16[64,1,3,8,2,1,64]{6,0,4,3,2,5,1:T(8,128)(2,1)S(1)} %get-tuple-element.14, bf16[64,1,3,8,2,1,64]{6,0,4,3,2,5,1:T(8,128)(2,1)S(1)} %get-tuple-element.13, bf16[64,1,3,8,2,1,64]{6,0,4,3,2,5,1:T(8,128)(2,1)S(1)} %get-tuple-element.66, ...), kind=kLoop, calls=%fused_computation | loop fusion | flops 11010048 | bytes 6291456 | tf_op jit(solution)/shard_map/stack | solution.py:147
  94.3 15.6 %copy.81 = bf16[64,4,3,8,2,2,64]{6,5,4,3,2,1,0:T(2,128)(2,1)} copy(bf16[64,4,3,8,2,2,64]{6,0,4,3,2,5,1:T(8,128)(2,1)S(1)} %maximum_maximum_fusion) | data formatting | bytes 6291456 | tf_op jit(solution)/shard_map/stack | solution.py:147
  109.8 9.1 %reshape_reshape.7 = bf16[256,6144]{1,0:T(8,128)(2,1)} reshape(bf16[64,4,3,8,2,2,64]{6,5,4,3,2,1,0:T(2,128)(2,1)} %copy.81) | data formatting | bytes 6291456 | tf_op jit(solution)/shard_map/reshape;reshape | solution.py:152
  118.9 3.8 %copy.83 = bf16[256,3,8,2,128]{0,4,3,2,1:T(8,128)(2,1)S(1)} copy(bf16[256,3,8,2,128]{4,2,3,1,0:T(8,128)(2,1)} %all-gather.2.cloned.1.call-done) | data formatting | bytes 6291456 | tf_op jit(solution)/shard_map/all_gather | solution.py:219
  123.3 1.6 copy-done.1
  124.9 3.5 %fusion = f32[256,512]{1,0:T(8,128)} fusion(bf16[256,6144]{1,0:T(8,128)(2,1)S(1)} %copy-done.1, bf16[256,6144]{0,1:T(8,128)(2,1)S(1)} %bitcast.209, bf16[256,6144]{0,1:T(8,128)(2,1)S(1)} %bitcast.208), kind=kOutput, calls=%fused_computation.1 | convolution fusion | flops 1623195648 | bytes 9961472 | tf_op jit(solution)/shard_map/dot_general | solution.py:153
  128.4 1.1 reshape_reshape_reshape.3
  129.6 16.6 %all_to_all.10 = f32[32,16,256]{2,1,0:T(8,128)S(1)} all-to-all(f32[32,16,256]{2,1,0:T(8,128)S(1)} %reshape_reshape_reshape.3), channel_id=1, replica_groups=mesh['gz'=4,'gy'=8,'vec'=4] {'gz','gy'}, dimensions={0} | all-to-all | bytes 1048576 | tf_op jit(solution)/shard_map/all_to_all | solution.py:43
  146.3 15.7 %all_to_all.11 = f32[32,16,256]{2,1,0:T(8,128)S(1)} all-to-all(f32[32,16,256]{2,1,0:T(8,128)S(1)} %broadcast_in_dim.2), channel_id=1, replica_groups=mesh['gz'=4,'gy'=8,'vec'=4] {'gz','gy'}, dimensions={0} | all-to-all | bytes 1048576 | tf_op jit(solution)/shard_map/all_to_all | solution.py:62
  162.3 1.0 copy.85
  (125 shorter events, 13.7 us)
Async XLA Ops:
  6.5 112.4 %all-gather.2.cloned.1.call-start = ((), (), s32[]{:S(2)}) async-start(), calls=%async_computation.2 | async-start | bytes 3932160 | tf_op jit(solution)/shard_map/all_gather | solution.py:219
  7.6 32.8 %collective-permute-start.2 = (bf16[64,3,1,2,128]{4,3,2,1,0:T(2,128)(2,1)S(1)}, bf16[64,3,1,2,128]{4,3,2,1,0:T(2,128)(2,1)S(1)}, u32[]{:S(2)}, u32[]{:S(2)}) collective-permute-start(bf16[64,3,1,2,128]{4,3,2,1,0:T(2,128)(2,1)S(1)} %get-tuple-element.70), channel_id=1, source_target_pairs={{32,0},{64,32},{96,64},{0,96},{33,1},{65,33},{97,65},{1,97},{34,2}... | collective-permute-start | bytes 294920 | tf_op jit(solution)/shard_map/ppermute | solution.py:24
  9.1 31.3 %collective-permute-start.1 = (bf16[64,3,1,2,128]{4,3,2,1,0:T(2,128)(2,1)S(1)}, bf16[64,3,1,2,128]{4,3,2,1,0:T(2,128)(2,1)S(1)}, u32[]{:S(2)}, u32[]{:S(2)}) collective-permute-start(bf16[64,3,1,2,128]{4,3,2,1,0:T(2,128)(2,1)S(1)} %get-tuple-element.69), channel_id=1, source_target_pairs={{0,32},{32,64},{64,96},{96,0},{1,33},{33,65},{65,97},{97,1},{2,34}... | collective-permute-start | bytes 294920 | tf_op jit(solution)/shard_map/ppermute | solution.py:23
  12.9 7.5 %copy-start.30 = (bf16[3,3,3,8,2,128]{5,4,3,2,1,0:T(2,128)(2,1)S(1)}, bf16[3,3,3,8,2,128]{5,4,3,2,1,0:T(2,128)(2,1)}, u32[]{:S(2)}) copy-start(bf16[3,3,3,8,2,128]{5,4,3,2,1,0:T(2,128)(2,1)} %param.5) | copy-start | bytes 331780
  12.9 8.9 %copy-start.31 = (s32[3]{0:T(128)S(1)}, s32[3]{0:T(128)}, u32[]{:S(2)}) copy-start(s32[3]{0:T(128)} %param.6) | copy-start | bytes 40
  14.9 28.1 %collective-permute-start = (bf16[64,3,8,1,128]{4,2,3,1,0:T(8,128)(2,1)}, bf16[64,3,8,1,128]{4,2,3,1,0:T(8,128)(2,1)}, u32[]{:S(2)}, u32[]{:S(2)}) collective-permute-start(bf16[64,3,8,1,128]{4,2,3,1,0:T(8,128)(2,1)} %get-tuple-element.67), channel_id=1, source_target_pairs={{0,4},{4,8},{8,12},{12,16},{16,20},{20,24},{24,28},{28,0},{1,5},{5... | collective-permute-start | bytes 1179656 | tf_op jit(solution)/shard_map/ppermute | solution.py:23
  16.1 31.5 %collective-permute-start.3 = (bf16[64,3,8,1,128]{4,2,3,1,0:T(8,128)(2,1)S(1)}, bf16[64,3,8,1,128]{4,2,3,1,0:T(8,128)(2,1)}, u32[]{:S(2)}, u32[]{:S(2)}) collective-permute-start(bf16[64,3,8,1,128]{4,2,3,1,0:T(8,128)(2,1)S(1)} %get-tuple-element.68), channel_id=1, source_target_pairs={{4,0},{8,4},{12,8},{16,12},{20,16},{24,20},{28,24},{0,28},{5,1},{9... | collective-permute-start | bytes 1179656 | tf_op jit(solution)/shard_map/ppermute | solution.py:24
  20.6 11.1 %collective-permute-start.5 = (bf16[3,3,1,2,2,64]{5,3,2,1,4,0:T(2,128)(2,1)S(1)}, bf16[3,3,1,2,2,64]{5,3,2,1,4,0:T(2,128)(2,1)S(1)}, u32[]{:S(2)}, u32[]{:S(2)}) collective-permute-start(bf16[3,3,1,2,2,64]{5,3,2,1,4,0:T(2,128)(2,1)S(1)} %copy.97), channel_id=1, source_target_pairs={{0,32},{32,64},{64,96},{96,0},{1,33},{33,65},{65,97},{97,1},{2,34}... | collective-permute-start | bytes 13832 | tf_op jit(solution)/shard_map/ppermute | solution.py:12
  21.6 5.5 %copy-start.32 = (s32[3]{0:T(128)S(1)}, s32[3]{0:T(128)}, u32[]{:S(2)}) copy-start(s32[3]{0:T(128)} %param.7) | copy-start | bytes 40
  23.5 16.9 %copy-start = (bf16[64,3,8,2,128]{4,3,2,1,0:T(2,128)(2,1)S(1)}, bf16[64,3,8,2,128]{4,3,2,1,0:T(2,128)(2,1)}, u32[]{:S(2)}) copy-start(bf16[64,3,8,2,128]{4,3,2,1,0:T(2,128)(2,1)} %param.4) | copy-start | bytes 2359300
  31.7 7.8 %collective-permute-start.4 = (bf16[3,3,8,1,2,64]{5,3,2,1,4,0:T(2,128)(2,1)S(1)}, bf16[3,3,8,1,2,64]{5,3,2,1,4,0:T(2,128)(2,1)S(1)}, u32[]{:S(2)}, u32[]{:S(2)}) collective-permute-start(bf16[3,3,8,1,2,64]{5,3,2,1,4,0:T(2,128)(2,1)S(1)} %copy.95), channel_id=1, source_target_pairs={{0,4},{4,8},{8,12},{12,16},{16,20},{20,24},{24,28},{28,0},{1,5},{5... | collective-permute-start | bytes 55304 | tf_op jit(solution)/shard_map/ppermute | solution.py:12
  73.3 1.2 copy-start.2
  73.3 1.2 copy-start.3
  73.3 1.2 copy-start.4
  73.3 1.2 copy-start.5
  73.3 1.2 copy-start.6
  73.3 1.2 copy-start.7
  73.3 1.2 copy-start.8
  73.3 1.2 copy-start.9
  73.4 1.2 copy-start.10
  73.4 1.2 copy-start.11
  73.4 1.2 copy-start.12
  73.4 1.2 copy-start.13
  73.4 1.2 copy-start.14
  73.4 1.2 copy-start.15
  73.4 1.2 copy-start.16
  73.4 1.2 copy-start.17
  73.4 1.2 copy-start.18
  73.4 1.2 copy-start.19
  73.5 1.2 copy-start.20
  73.5 1.2 copy-start.21
  123.0 1.9 %copy-start.1 = (bf16[256,6144]{1,0:T(8,128)(2,1)S(1)}, bf16[256,6144]{1,0:T(8,128)(2,1)}, u32[]{:S(2)}) copy-start(bf16[256,6144]{1,0:T(8,128)(2,1)} %reshape_reshape.7) | copy-start | bytes 9437188
  (8 other events, 9.3 us)
Sparse Core Ops, SparseCore 0:
  13.1 40.9 all-gather.1
where the time goes:
time: 171 us; the launch traced here: 170 us
  local copies, waits for them, and re-layouts  67 us (39%)
  other arithmetic  32.9 us (19%)
  blocking collectives  32.3 us (19%)
  between operations  18 us (11%)
  starting transfers between devices  9.57 us (6%)
  waiting for transfers between devices  6.81 us (4%)
  matrix products  3.55 us (2%)
    another operation x4, other arithmetic, make_operators(): results.append(jnp.stack([real_part, imag_part], -2).astype(jnp.bfloat16))  16.8 us
    all_to_all x1, blocking collectives, summed_on_arrival(): lax.all_to_all(pieces, axis, split_axis=0, concat_axis=0, tiled=True)  16.6 us
    all_to_all x1, blocking collectives, from_everyone(): return lax.all_to_all(copies, axis, split_axis=0, concat_axis=0, tiled=True)  15.7 us
    another operation x1, local copies, waits for them, and re-layouts, make_operators(): return jnp.stack(results, 1)  15.6 us
    another operation x1, local copies, waits for them, and re-layouts, contract(): flat_rows = rows.reshape(row_count * 4, -1)  9.08 us
    slice x1, local copies, waits for them, and re-layouts, stencil_lists(): pad_imag = widened[..., 1, :]  8.34 us
    ppermute x2, waiting for transfers between devices, shifted(): return lax.ppermute(value, axis, pairs)  6.79 us
    concatenate x4, local copies, waits for them, and re-layouts, with_halo(): jnp.concatenate([jnp.pad(low, around), x, jnp.pad(high, around)], axis=dim)  6.76 us
  transfers between devices with their start and end apart: 7, of which 1 were waited for; matrix products, arithmetic and copies ran while one was open for 53% of the time, Pallas kernels for 0%

commit v1 on v0

v1 whole, which is shorter than its diff:
```python
import functools
import math

import jax
import jax.numpy as jnp
from jax import lax
from jax.experimental import pallas as pl
from jax.experimental.pallas import tpu as pltpu
from jax.sharding import PartitionSpec as P

F32 = jnp.float32
BF16 = jnp.bfloat16
VMEM = pl.BlockSpec(memory_space=pltpu.VMEM)
SMEM = pl.BlockSpec(memory_space=pltpu.SMEM)

NV = 64
COL = 3
DZ = 8
HY = 2
LANES = 128
HALF = 64
NZY = DZ * HY
NK = COL * NZY
KDIM = NK * LANES


def params(limit):
    return pltpu.CompilerParams(vmem_limit_bytes=limit * 1024 * 1024)


def shape(dims, dtype):
    return jax.ShapeDtypeStruct(dims, dtype)


def prepare_kernel(v_ref, l_ref, vt_ref, y0_ref, y1_ref, z0_ref, z1_ref, wide, lwide):
    wide[...] = v_ref[...].astype(F32)
    lwide[0:432, :] = l_ref[...].astype(F32)
    lwide[432:576, :] = jnp.zeros((144, LANES), F32)
    for k in range(NK):
        tile = wide[pl.ds(k, NV, stride=NK), :].astype(BF16)
        c, z, y = k // NZY, (k % NZY) // HY, k % HY
        vt_ref[k] = tile
        if y == 0:
            y0_ref[c * DZ + z] = tile
        else:
            y1_ref[c * DZ + z] = tile
        if z == 0:
            z0_ref[c * HY + y] = tile
        if z == DZ - 1:
            z1_ref[c * HY + y] = tile
    rim = lwide[pl.ds(9 * NZY + 1, 72, stride=HY), :]
    rim = jnp.concatenate([rim, jnp.zeros((56, LANES), F32)], 0).astype(BF16)
    y1_ref[24] = rim[0:64]
    y1_ref[25] = rim[64:128]
    low = lwide[pl.ds(18 * NZY + 14, 16, stride=NZY), :]
    high = lwide[pl.ds(18 * NZY + 15, 16, stride=NZY), :]
    rest = jnp.zeros((32, LANES), F32)
    z1_ref[6] = jnp.concatenate([low, high, rest], 0).astype(BF16)


def prepare(rows, link_rows):
    return pl.pallas_call(
        prepare_kernel,
        out_shape=(
            shape((NK, NV, LANES), BF16),
            shape((24, NV, LANES), BF16),
            shape((26, NV, LANES), BF16),
            shape((6, NV, LANES), BF16),
            shape((7, NV, LANES), BF16),
        ),
        in_specs=[VMEM] * 2,
        out_specs=(VMEM,) * 5,
        scratch_shapes=[pltpu.VMEM((NV * NK, LANES), F32), pltpu.VMEM((576, LANES), F32)],
        compiler_params=params(16),
        cost_estimate=pl.CostEstimate(flops=0, bytes_accessed=3000000, transcendentals=0),
        name="prepare",
    )(rows, link_rows)


def stencil_kernel(
    dirs_ref, vt_ref, yp_ref, ym_ref, zp_ref, zm_ref, l_ref, cos_ref, sin_ref, w_ref,
    ext, exts, lwide, real, imag, upr, upi, dnr, dni,
):
    lane = lax.broadcasted_iota(jnp.int32, (1, LANES), 1)
    first = lane < HALF
    sign = jnp.where(first, -1.0, 1.0).astype(F32)

    def put(c, z, y, tile):
        wide = tile.astype(F32)
        ext[c, z, y] = wide
        exts[c, z, y] = pltpu.roll(wide, HALF, 1)

    for c in range(COL):
        for z in range(DZ):
            for y in range(HY):
                put(c, z + 1, y + 1, vt_ref[(c * DZ + z) * HY + y])
            put(c, z + 1, HY + 1, yp_ref[c * DZ + z])
            put(c, z + 1, 0, ym_ref[c * DZ + z])
        for y in range(HY):
            put(c, DZ + 1, y + 1, zp_ref[c * HY + y])
            put(c, 0, y + 1, zm_ref[c * HY + y])

    def coefficients(rows):
        half = rows * 0.5
        swapped = pltpu.roll(half, HALF, 1)
        return jnp.where(first, half, swapped), jnp.where(first, swapped, half)

    lwide[0:432, :] = l_ref[...].astype(F32)
    lwide[432:504, :] = jnp.concatenate([ym_ref[24], ym_ref[25]], 0).astype(F32)[0:72]
    zrim = zm_ref[6].astype(F32)
    lwide[504:520, :] = zrim[0:16]
    lwide[520:536, :] = zrim[16:32]
    re, im = coefficients(lwide[...])
    real[...] = re
    imag[...] = im
    for zy in range(NZY):
        z, y = zy // HY, zy % HY
        pick = pl.ds(zy, 27, stride=NZY)
        upr[zy, 0:27, :] = real[pick, :]
        upi[zy, 0:27, :] = imag[pick, :] * sign
        pick = pl.ds(zy, 9, stride=NZY)
        dnr[zy, 0:9, :] = pltpu.roll(real[pick, :], 1, 1)
        dni[zy, 0:9, :] = pltpu.roll(imag[pick, :], 1, 1) * sign
        pick = pl.ds(432 + z, 9, stride=DZ) if y == 0 else pl.ds(9 * NZY + zy - 1, 9, stride=NZY)
        dnr[zy, 9:18, :] = real[pick, :]
        dni[zy, 9:18, :] = imag[pick, :] * sign
        pick = pl.ds(504 + 16 * y, 9) if z == 0 else pl.ds(18 * NZY + zy - HY, 9, stride=NZY)
        dnr[zy, 18:27, :] = real[pick, :]
        dni[zy, 18:27, :] = imag[pick, :] * sign

    slots = [
        sum(jnp.where(dirs_ref[o] == mu, o, 0) for o in range(3)).astype(jnp.int32)
        for mu in range(3)
    ]
    wrap_up = (lane == HALF - 1) | (lane == LANES - 1)
    wrap_down = (lane == 0) | (lane == HALF)

    def site(zy, carry):
        z = lax.div(zy, HY) + 1
        y = lax.rem(zy, HY) + 1
        def neighbour(mu, c, step):
            if mu == 1:
                return ext[c, z, y + step], exts[c, z, y + step]
            if mu == 2:
                return ext[c, z + step, y], exts[c, z + step, y]
            here, swap = ext[c, z, y], exts[c, z, y]
            a = pltpu.roll(here, (-step) % LANES, 1)
            b = pltpu.roll(swap, (-step) % LANES, 1)
            wrap = wrap_up if step == 1 else wrap_down
            return jnp.where(wrap, b, a), jnp.where(wrap, a, b)

        for mu in range(3):
            out = [None] * 3
            for c in range(COL):
                here, swap = neighbour(mu, c, 1)
                for r in range(3):
                    at = mu * 9 + r * 3 + c
                    term = here * upr[zy, at:at + 1, :] + swap * upi[zy, at:at + 1, :]
                    out[r] = term if out[r] is None else out[r] + term
            for c in range(COL):
                here, swap = neighbour(mu, c, -1)
                for r in range(3):
                    at = mu * 9 + c * 3 + r
                    term = here * dnr[zy, at:at + 1, :] - swap * dni[zy, at:at + 1, :]
                    out[r] = out[r] - term
            for r in range(3):
                column = pl.multiple_of((r * NZY + zy) * LANES, LANES)
                w_ref[slots[mu], :, pl.ds(column, LANES)] = out[r].astype(BF16)
        cosine = cos_ref[pl.ds(zy, 1), :]
        sine = sin_ref[pl.ds(zy, 1), :]
        for c in range(COL):
            column = pl.multiple_of((c * NZY + zy) * LANES, LANES)
            phased = ext[c, z, y] * cosine + exts[c, z, y] * sine
            w_ref[3, :, pl.ds(column, LANES)] = phased.astype(BF16)
        return carry

    lax.fori_loop(0, NZY, site, 0)


def stencil(directions, vt, yp, ym, zp, zm, link_rows, cosine, sine):
    table = pltpu.VMEM((NZY, 32, LANES), F32)
    return pl.pallas_call(
        stencil_kernel,
        out_shape=shape((4, NV, KDIM), BF16),
        in_specs=[SMEM] + [VMEM] * 8,
        out_specs=VMEM,
        scratch_shapes=[
            pltpu.VMEM((COL, DZ + 2, HY + 2, NV, LANES), F32),
            pltpu.VMEM((COL, DZ + 2, HY + 2, NV, LANES), F32),
            pltpu.VMEM((536, LANES), F32),
            pltpu.VMEM((536, LANES), F32),
            pltpu.VMEM((536, LANES), F32),
            table,
            table,
            table,
            table,
        ],
        compiler_params=params(24),
        cost_estimate=pl.CostEstimate(flops=60000000, bytes_accessed=6000000, transcendentals=0),
        name="stencil",
    )(directions, vt, yp, ym, zp, zm, link_rows, cosine, sine)


def contract_kernel(counts, core_ref, w_ref, *refs):
    blocks = refs[: len(counts)]
    keep_ref, send_ref, wide, right, product = refs[len(counts):]
    total = sum(counts)
    lane = lax.broadcasted_iota(jnp.int32, (1, LANES), 1)
    sign = jnp.where(lane < HALF, -1.0, 1.0).astype(F32)
    start = 0
    for block, count in zip(blocks, counts):
        wide[0:count * NK, :] = block[...].astype(F32)
        for k in range(NK):
            tile = wide[pl.ds(k, count, stride=NK), :]
            swap = pltpu.roll(tile, HALF, 1) * sign
            right[start:start + count, k * LANES:(k + 1) * LANES] = tile.astype(BF16)
            right[total + start:total + start + count, k * LANES:(k + 1) * LANES] = swap.astype(BF16)
        start += count
    left = w_ref[...].reshape(4 * NV, KDIM)
    dots = lax.dot_general(left, right[...], (((1,), (1,)), ((), ())), preferred_element_type=F32)
    product[...] = dots.reshape(2, 2 * NV, 2 * total)
    mine = core_ref[0]
    keep_ref[...] = product[mine]
    send_ref[...] = product[1 - mine]


def contract(core, w, blocks):
    counts = tuple(b.shape[0] // NK for b in blocks)
    total = sum(counts)
    out = shape((2 * NV, 2 * total), F32)
    return pl.pallas_call(
        functools.partial(contract_kernel, counts),
        out_shape=(out, out),
        in_specs=[SMEM] + [VMEM] * (1 + len(blocks)),
        out_specs=(VMEM, VMEM),
        scratch_shapes=[
            pltpu.VMEM((NV * NK, LANES), F32),
            pltpu.VMEM((2 * total, KDIM), BF16),
            pltpu.VMEM((2, 2 * NV, 2 * total), F32),
        ],
        compiler_params=params(32),
        cost_estimate=pl.CostEstimate(
            flops=2 * 256 * 2 * total * KDIM, bytes_accessed=4000000, transcendentals=0
        ),
        name="contract",
    )(core, w, *blocks)


def finish_kernel(scale, where_ref, a0_ref, a1_ref, b0_ref, b1_ref, out_ref):
    shift, core = where_ref[0], where_ref[1]
    a = [a0_ref[...], a1_ref[...]]
    b = [b0_ref[...], b1_ref[...]]
    for ch in range(2):
        for part in range(2):
            near = a[ch][:, part * 192:(part + 1) * 192]
            far = b[ch][:, part * 64:(part + 1) * 64]
            line = jnp.concatenate([near[:, 0:128], far, near[:, 128:192]], 1) * scale
            line = pltpu.roll(line, shift, 1)
            at = 2 * (core if ch == 0 else 1 - core)
            out_ref[at, part] = line[0:NV]
            out_ref[at + 1, part] = line[NV:2 * NV]


def finish(where, near_mine, near_other, far_mine, far_other, scale):
    return pl.pallas_call(
        functools.partial(finish_kernel, scale),
        out_shape=shape((4, 2, NV, 256), F32),
        in_specs=[SMEM] + [VMEM] * 4,
        out_specs=VMEM,
        compiler_params=params(16),
        cost_estimate=pl.CostEstimate(flops=200000, bytes_accessed=1000000, transcendentals=0),
        name="finish",
    )(where, near_mine, near_other, far_mine, far_other)


def permuted(value, axis, target):
    size = lax.axis_size(axis)
    return lax.ppermute(value, axis, [(source, target(source)) for source in range(size)])


def four_sum(own, axis_opposite, axis_side, axis_other):
    wide = [t.astype(F32) for t in (own, axis_opposite, axis_side, axis_other)]
    return (wide[0] + wide[1]) + (wide[2] + wide[3])


def body(vectors, links, momentum, directions):
    vec = lax.axis_index("vec")
    rows = vectors.reshape(NV * NK, LANES)
    link_rows = links.reshape(27 * NZY, LANES)
    mid = NV * NK // 2
    ring_up = lambda v: permuted(v, "vec", lambda s: (s + 1) % 4)
    ring_down = lambda v: permuted(v, "vec", lambda s: (s - 1) % 4)
    low, high = rows[:mid], rows[mid:]
    prev_low = ring_up(low)
    next_high = ring_down(high)
    prev_high = ring_up(high)
    next_low = ring_down(low)
    far_low = ring_up(prev_low)
    far_high = ring_down(next_high)

    vt, y0, y1, z0, z1 = prepare(rows, link_rows)
    yp = permuted(y0, "gy", lambda s: (s - 1) % 8)
    ym = permuted(y1, "gy", lambda s: (s + 1) % 8)
    zp = permuted(z0, "gz", lambda s: (s - 1) % 4)
    zm = permuted(z1, "gz", lambda s: (s + 1) % 4)

    width, extent_y, extent_z = HALF, 16, 32
    x = jnp.arange(LANES, dtype=jnp.int32) % HALF
    zy = jnp.arange(NZY, dtype=jnp.int32)
    y = lax.axis_index("gy") * HY + zy % HY
    z = lax.axis_index("gz") * DZ + zy // HY
    frac_x = (momentum[0] * x % width).astype(F32) / width
    frac_y = (momentum[1] * y % extent_y).astype(F32) / extent_y
    frac_z = (momentum[2] * z % extent_z).astype(F32) / extent_z
    angle = 2.0 * math.pi * ((frac_z + frac_y)[:, None] + frac_x[None, :])
    cosine = jnp.cos(angle)
    sine = jnp.sin(angle) * jnp.where(jnp.arange(LANES) < HALF, 1.0, -1.0).astype(F32)

    w = stencil(directions, vt, yp, ym, zp, zm, link_rows, cosine, sine)

    core = lax.axis_index("gz") % 2
    core_ref = core.reshape(1).astype(jnp.int32)
    near_keep, near_send = contract(core_ref, w, [rows, next_low, next_high, prev_low, prev_high])
    far_keep, far_send = contract(core_ref, w, [far_low, far_high])

    mate = lambda v: permuted(v, "gz", lambda s: s ^ 1)
    along_x = lambda v, step: permuted(v, "gy", lambda s: (s // 4) * 4 + (s + step) % 4)

    def summed(keep, send):
        chip = (keep + mate(send)).astype(BF16)
        row = four_sum(chip, along_x(chip, 2), along_x(chip, 1), along_x(chip, 3)).astype(BF16)
        far = permuted(row, "gy", lambda s: s ^ 4)
        side = permuted(row, "gz", lambda s: s ^ 2)
        both = permuted(row, ("gz", "gy"), lambda s: s ^ 20)
        plane = four_sum(row, far, side, both)
        return plane, mate(plane)

    near, near_other = summed(near_keep, near_send)
    far, far_other = summed(far_keep, far_send)
    where = jnp.stack([vec * HALF, core]).astype(jnp.int32)
    scale = 1.0 / math.sqrt(width * extent_y * extent_z)
    return finish(where, near, near_other, far, far_other, scale)


def solution(mesh):
    in_specs = (P("vec", None, "gz", "gy", None), P(None, None, None, "gz", "gy", None), P(), P())
    out_specs = P(None, None, "vec", None)
    return jax.shard_map(body, mesh=mesh, in_specs=in_specs, out_specs=out_specs, check_vma=False)
```

time: 171 us -> 92.7 us (0.54)
  local copies, waits for them, and re-layouts: 67 us -> 15.9 us
  blocking collectives: 32.3 us -> 0 us
  other arithmetic: 32.9 us -> 3.14 us
  starting transfers between devices: 9.57 us -> 37.3 us
  Pallas kernels: 0 us -> 18.4 us
  between operations: 18 us -> 0.18 us
  waiting for transfers between devices: 6.81 us -> 17.3 us
  matrix products: 3.55 us -> 0 us
    all_to_all x2 -> x0, blocking collectives: 32.3 us -> none  [the longest x1 16.6 us: summed_on_arrival(): lax.all_to_all(pieces, axis, split_axis=0, concat_axis=0, tiled=True)]
    ppermute x6 -> x26, starting transfers between devices: 9.57 us -> 37.3 us  [permuted(): lax.ppermute(value, axis, [(source, target(source)) for source in range(s...]
    another operation x3 -> x0, local copies, waits for them, and re-layouts: 25.8 us -> none  [the longest x1 15.6 us: make_operators(): return jnp.stack(results, 1)]
    another operation x7 -> x1, other arithmetic: 19.8 us -> 0.07 us  [body(): where = jnp.stack([vec * HALF, core]).astype(jnp.int32)]
    pallas_call x0 -> x5, Pallas kernels: none -> 18.4 us  [the longest x2 8.24 us: contract(): pl.pallas_call(functools.partial(contract_kernel, counts), out_shape=(out...]
    slice x14 -> x2, local copies, waits for them, and re-layouts: 15.3 us -> 2.79 us  [the longest x1 1.43 us: body(): low, high = (rows[:mid], rows[mid:])]
    ppermute x6 -> x26, waiting for transfers between devices: 6.8 us -> 17.3 us  [permuted(): lax.ppermute(value, axis, [(source, target(source)) for source in range(s...]
    unnamed x73 -> x34, local copies, waits for them, and re-layouts: 4.04 us -> 13.1 us
  transfers between devices with their start and end apart: 7 -> 26, of which waited for: 1 -> 5; matrix products, arithmetic and copies ran while one was open for 53% -> 6% of each run, Pallas kernels for 0% -> 17%
where the time goes in v1:
time: 92.7 us; the launch traced here: 92.1 us
  starting transfers between devices  37.3 us (40%)
  Pallas kernels  18.4 us (20%)
  waiting for transfers between devices  17.3 us (19%)
  local copies, waits for them, and re-layouts  15.9 us (17%)
  other arithmetic  3.14 us (3%)
    ppermute x26, starting transfers between devices, permuted(): lax.ppermute(value, axis, [(source, target(source)) for source in range(s...  37.3 us
    ppermute x26, waiting for transfers between devices, permuted(): lax.ppermute(value, axis, [(source, target(source)) for source in range(s...  17.3 us
    unnamed x34, local copies, waits for them, and re-layouts  13.1 us
    pallas_call x2, Pallas kernels, contract(): pl.pallas_call(functools.partial(contract_kernel, counts), out_shape=(out...  8.24 us
    pallas_call x1, Pallas kernels, stencil(): pl.pallas_call(stencil_kernel, out_shape=shape((4, NV, KDIM), BF16), in_s...  7.78 us
  transfers between devices with their start and end apart: 26, of which 5 were waited for; matrix products, arithmetic and copies ran while one was open for 6% of the time, Pallas kernels for 17%

profile of v1, /device:TPU:1, one launch (start us, length us, event | category | flops | bytes accessed | tf_op | source)
XLA Modules:
  0.0 92.1 jit_solution(9250078759276054216)
XLA Ops:
  0.0 1.1 %copy-done = bf16[64,3,8,2,128]{4,3,2,1,0:T(2,128)(2,1)S(1)} copy-done((bf16[64,3,8,2,128]{4,3,2,1,0:T(2,128)(2,1)S(1)}, bf16[64,3,8,2,128]{4,3,2,1,0:T(2,128)(2,1)}, u32[]{:S(2)}) %copy-start) | copy-done | bytes 786456
  1.1 0.9 copy-done.4
  2.6 6.7 %collective-permute-start = (bf16[24,64,128]{2,1,0:T(8,128)(2,1)S(1)}, bf16[24,64,128]{2,1,0:T(8,128)(2,1)S(1)}, u32[]{:S(2)}, u32[]{:S(2)}) collective-permute-start(bf16[24,64,128]{2,1,0:T(8,128)(2,1)S(1)} %get-tuple-element.15), channel_id=1, source_target_pairs={{0,28},{4,0},{8,4},{12,8},{16,12},{20,16},{24,20},{28,24},{1,29},{... | collective-permute-start | bytes 1179656 | tf_op jit(solution)/shard_map/ppermute | solution.py:278
  9.3 1.4 %fusion.16 = (bf16[32,3,8,2,128]{4,3,2,1,0:T(2,128)(2,1)}, bf16[32,3,8,2,128]{4,3,2,1,0:T(2,128)(2,1)}) fusion(bf16[64,3,8,2,128]{4,3,2,1,0:T(2,128)(2,1)S(1)} %copy-done), kind=kLoop, calls=%fused_computation.41 | loop fusion | bytes 1572864 | tf_op jit(solution)/shard_map/slice | solution.py:293
  10.7 1.3 %collective-permute-start.6 = (bf16[1536,128]{1,0:T(8,128)(2,1)}, bf16[1536,128]{1,0:T(8,128)(2,1)S(1)}, u32[]{:S(2)}, u32[]{:S(2)}) collective-permute-start(bf16[1536,128]{1,0:T(8,128)(2,1)} %bitcast.7), channel_id=1, source_target_pairs={{0,1},{1,2},{2,3},{3,0},{4,5},{5,6},{6,7},{7,4},{8,9},{9,10},{10,1... | collective-permute-start | bytes 1179656 | tf_op jit(solution)/shard_map/ppermute | solution.py:278
  12.0 1.4 %collective-permute-start.5 = (bf16[1536,128]{1,0:T(8,128)(2,1)}, bf16[1536,128]{1,0:T(8,128)(2,1)}, u32[]{:S(2)}, u32[]{:S(2)}) collective-permute-start(bf16[1536,128]{1,0:T(8,128)(2,1)} %bitcast.8), channel_id=1, source_target_pairs={{0,3},{1,0},{2,1},{3,2},{4,7},{5,4},{6,5},{7,6},{8,11},{9,8},{10,9... | collective-permute-start | bytes 1179656 | tf_op jit(solution)/shard_map/ppermute | solution.py:278
  13.5 2.1 %collective-permute-start.3 = (bf16[7,64,128]{2,1,0:T(8,128)(2,1)S(1)}, bf16[7,64,128]{2,1,0:T(8,128)(2,1)S(1)}, u32[]{:S(2)}, u32[]{:S(2)}) collective-permute-start(bf16[7,64,128]{2,1,0:T(8,128)(2,1)S(1)} %get-tuple-element.18), channel_id=1, source_target_pairs={{0,32},{32,64},{64,96},{96,0},{1,33},{33,65},{65,97},{97,1},{2,34}... | collective-permute-start | bytes 344072 | tf_op jit(solution)/shard_map/ppermute | solution.py:278
  15.6 1.4 %fusion.17 = (s32[1]{0:T(128)}, s32[1]{0:T(128)}, s32[1]{0:T(128)}) fusion(s32[3]{0:T(128)} %param.6), kind=kLoop, calls=%fused_computation.42 | loop fusion | bytes 24 | tf_op jit(solution)/shard_map/slice | solution.py:314
  16.9 3.1 %collective-permute-done.2.zp_ref = bf16[6,64,128]{2,1,0:T(8,128)(2,1)S(1)} collective-permute-done((bf16[6,64,128]{2,1,0:T(8,128)(2,1)S(1)}, bf16[6,64,128]{2,1,0:T(8,128)(2,1)S(1)}, u32[]{:S(2)}, u32[]{:S(2)}) %collective-permute-start.2) | collective-permute-done | bytes 98336 | tf_op jit(solution)/shard_map/ppermute | solution.py:278
  20.6 1.5 %collective-permute-start.4 = (bf16[1536,128]{1,0:T(8,128)(2,1)}, bf16[1536,128]{1,0:T(8,128)(2,1)}, u32[]{:S(2)}, u32[]{:S(2)}) collective-permute-start(bf16[1536,128]{1,0:T(8,128)(2,1)} %bitcast.7), channel_id=1, source_target_pairs={{0,3},{1,0},{2,1},{3,2},{4,7},{5,4},{6,5},{7,6},{8,11},{9,8},{10,9... | collective-permute-start | bytes 1179656 | tf_op jit(solution)/shard_map/ppermute | solution.py:278
  23.6 1.3 %fusion.7 = f32[16]{0:T(128)S(1)} fusion(s32[]{:T(128)S(6)} %mul.58, s32[]{:T(128)} %bitcast.5, s32[]{:T(128)S(6)} %mul.55, s32[]{:T(128)} %bitcast.4), kind=kLoop, calls=%fused_computation.31 | loop fusion | flops 688 | bytes 80 | tf_op jit(solution)/shard_map/add | solution.py:315
  25.5 2.7 %collective-permute-start.17 = (bf16[1536,128]{1,0:T(8,128)(2,1)}, bf16[1536,128]{1,0:T(8,128)(2,1)}, u32[]{:S(2)}, u32[]{:S(2)}) collective-permute-start(bf16[1536,128]{1,0:T(8,128)(2,1)} %collective-permute-done.5.refs_2_), channel_id=1, source_target_pairs={{0,3},{1,0},{2,1},{3,2},{4,7},{5,4},{6,5},{7,6},{8,11},{9,8},{10,9... | collective-permute-start | bytes 1179656 | tf_op jit(solution)/shard_map/ppermute | solution.py:278
  28.4 10.2 %collective-permute-done.1.ym_ref = bf16[26,64,128]{2,1,0:T(8,128)(2,1)S(1)} collective-permute-done((bf16[26,64,128]{2,1,0:T(8,128)(2,1)S(1)}, bf16[26,64,128]{2,1,0:T(8,128)(2,1)S(1)}, u32[]{:S(2)}, u32[]{:S(2)}) %collective-permute-start.1) | collective-permute-done | bytes 426016 | tf_op jit(solution)/shard_map/ppermute | solution.py:278
  39.4 1.1 %copy-done.3 = bf16[48,64,128]{2,1,0:T(8,128)(2,1)S(1)} copy-done((bf16[48,64,128]{2,1,0:T(8,128)(2,1)S(1)}, bf16[48,64,128]{2,1,0:T(8,128)(2,1)}, u32[]{:S(2)}) %copy-start.3) | copy-done | bytes 786456
  41.4 1.0 %copy-done.7 = bf16[26,64,128]{2,1,0:T(8,128)(2,1)S(1)} copy-done((bf16[26,64,128]{2,1,0:T(8,128)(2,1)S(1)}, bf16[26,64,128]{2,1,0:T(8,128)(2,1)}, u32[]{:S(2)}) %copy-start.7) | copy-done | bytes 426008
  42.4 1.0 %copy-done.9 = bf16[24,64,128]{2,1,0:T(8,128)(2,1)S(1)} copy-done((bf16[24,64,128]{2,1,0:T(8,128)(2,1)S(1)}, bf16[24,64,128]{2,1,0:T(8,128)(2,1)}, u32[]{:S(2)}) %copy-start.9) | copy-done | bytes 393240
  43.4 0.9 copy-done.13
  45.9 7.8 %stencil.1.w_ref = bf16[4,64,6144]{2,1,0:T(8,128)(2,1)S(1)} custom-call(s32[3]{0:T(128)S(1)} %copy-done.16, bf16[48,64,128]{2,1,0:T(8,128)(2,1)S(1)} %copy-done.3, bf16[24,64,128]{2,1,0:T(8,128)(2,1)S(1)} %copy-done.9, bf16[26,64,128]{2,1,0:T(8,128)(2,1)S(1)} %copy-done.7, bf16[6,64,128]{2,1,0:T(8,128)(2,1)S(1)} %copy-done.15, ...), custom_call_target="tpu_custom_call" | custom-call | flops 60000000 | bytes 6000000 | tf_op jit(solution)/shard_map/stencil/pallas_call | solution.py:182
  53.7 1.1 %copy-done.1 = bf16[64,3,8,2,128]{4,3,2,1,0:T(2,128)(2,1)S(1)} copy-done((bf16[64,3,8,2,128]{4,3,2,1,0:T(2,128)(2,1)S(1)}, bf16[64,3,8,2,128]{4,3,2,1,0:T(2,128)(2,1)}, u32[]{:S(2)}) %copy-start.1) | copy-done | bytes 786456
  54.8 5.7 %contract.2 = (f32[128,384]{1,0:T(8,128)S(1)}, f32[128,384]{1,0:T(8,128)}) custom-call(s32[1]{0:T(128)} %bitcast.1.core_ref, bf16[4,64,6144]{2,1,0:T(8,128)(2,1)S(1)} %stencil.1.w_ref, bf16[3072,128]{1,0:T(8,128)(2,1)S(1)} %bitcast.10, bf16[1536,128]{1,0:T(8,128)(2,1)} %collective-permute-done.4.refs_1_, bf16[1536,128]{1,0:T(8,128)(2,1)} %collective-permute-done.5.refs_2_, ...), custom_call_target="tpu_custom_call" | custom-call | flops 1207959552 | bytes 4000000 | tf_op jit(solution)/shard_map/contract/pallas_call | solution.py:231
  61.2 2.6 %contract.3 = (f32[128,128]{1,0:T(8,128)S(1)}, f32[128,128]{1,0:T(8,128)S(1)}) custom-call(s32[1]{0:T(128)} %bitcast.1.core_ref, bf16[4,64,6144]{2,1,0:T(8,128)(2,1)S(1)} %stencil.1.w_ref, bf16[1536,128]{1,0:T(8,128)(2,1)} %collective-permute-done.16.refs_0_, bf16[1536,128]{1,0:T(8,128)(2,1)} %collective-permute-done.17.refs_1_), custom_call_target="tpu_custom_call" | custom-call | flops 402653184 | bytes 4000000 | tf_op jit(solution)/shard_map/contract/pallas_call | solution.py:231
  64.4 0.9 %add_convert_fusion.1 = bf16[128,384]{1,0:T(8,128)(2,1)S(1)} fusion(f32[128,384]{1,0:T(8,128)S(1)} %copy-done.11, f32[128,384]{1,0:T(8,128)} %collective-permute-done.8), kind=kLoop, calls=%fused_computation.2 | loop fusion | flops 98304 | bytes 491520 | tf_op jit(solution)/shard_map/convert_element_type | solution.py:330
  65.3 2.3 %collective-permute-start.11 = (bf16[128,384]{1,0:T(8,128)(2,1)S(1)}, bf16[128,384]{1,0:T(8,128)(2,1)S(1)}, u32[]{:S(2)}, u32[]{:S(2)}) collective-permute-start(bf16[128,384]{1,0:T(8,128)(2,1)S(1)} %add_convert_fusion.1), channel_id=1, source_target_pairs={{0,12},{4,0},{8,4},{12,8},{16,28},{20,16},{24,20},{28,24},{1,13},{... | collective-permute-start | bytes 294920 | tf_op jit(solution)/shard_map/ppermute | solution.py:278
  67.6 1.3 %collective-permute-start.9 = (bf16[128,384]{1,0:T(8,128)(2,1)S(1)}, bf16[128,384]{1,0:T(8,128)(2,1)S(1)}, u32[]{:S(2)}, u32[]{:S(2)}) collective-permute-start(bf16[128,384]{1,0:T(8,128)(2,1)S(1)} %add_convert_fusion.1), channel_id=1, source_target_pairs={{0,8},{4,12},{8,0},{12,4},{16,24},{20,28},{24,16},{28,20},{1,9},{5... | collective-permute-start | bytes 294920 | tf_op jit(solution)/shard_map/ppermute | solution.py:278
  68.9 1.5 %collective-permute-start.21 = (bf16[128,128]{1,0:T(8,128)(2,1)S(1)}, bf16[128,128]{1,0:T(8,128)(2,1)S(1)}, u32[]{:S(2)}, u32[]{:S(2)}) collective-permute-start(bf16[128,128]{1,0:T(8,128)(2,1)S(1)} %add_convert_fusion.3), channel_id=1, source_target_pairs={{0,12},{4,0},{8,4},{12,8},{16,28},{20,16},{24,20},{28,24},{1,13},{... | collective-permute-start | bytes 98312 | tf_op jit(solution)/shard_map/ppermute | solution.py:278
  71.0 1.7 %collective-permute-start.19 = (bf16[128,128]{1,0:T(8,128)(2,1)S(1)}, bf16[128,128]{1,0:T(8,128)(2,1)S(1)}, u32[]{:S(2)}, u32[]{:S(2)}) collective-permute-start(bf16[128,128]{1,0:T(8,128)(2,1)S(1)} %add_convert_fusion.3), channel_id=1, source_target_pairs={{0,8},{4,12},{8,0},{12,4},{16,24},{20,28},{24,16},{28,20},{1,9},{5... | collective-permute-start | bytes 98312 | tf_op jit(solution)/shard_map/ppermute | solution.py:278
  72.7 2.5 %collective-permute-done.10 = bf16[128,384]{1,0:T(8,128)(2,1)S(1)} collective-permute-done((bf16[128,384]{1,0:T(8,128)(2,1)S(1)}, bf16[128,384]{1,0:T(8,128)(2,1)S(1)}, u32[]{:S(2)}, u32[]{:S(2)}) %collective-permute-start.10) | collective-permute-done | bytes 98336 | tf_op jit(solution)/shard_map/ppermute | solution.py:278
  76.2 3.0 %collective-permute-start.12 = (bf16[128,384]{1,0:T(8,128)(2,1)S(1)}, bf16[128,384]{1,0:T(8,128)(2,1)S(1)}, u32[]{:S(2)}, u32[]{:S(2)}) collective-permute-start(bf16[128,384]{1,0:T(8,128)(2,1)S(1)} %add_convert_fusion), channel_id=1, source_target_pairs={{0,16},{4,20},{8,24},{12,28},{16,0},{20,4},{24,8},{28,12},{1,17},{... | collective-permute-start | bytes 294920 | tf_op jit(solution)/shard_map/ppermute | solution.py:278
  80.0 3.2 %collective-permute-start.22 = (bf16[128,128]{1,0:T(8,128)(2,1)S(1)}, bf16[128,128]{1,0:T(8,128)(2,1)S(1)}, u32[]{:S(2)}, u32[]{:S(2)}) collective-permute-start(bf16[128,128]{1,0:T(8,128)(2,1)S(1)} %add_convert_fusion.2), channel_id=1, source_target_pairs={{0,16},{4,20},{8,24},{12,28},{16,0},{20,4},{24,8},{28,12},{1,17},{... | collective-permute-start | bytes 98312 | tf_op jit(solution)/shard_map/ppermute | solution.py:278
  83.2 3.4 %collective-permute-start.15 = (f32[128,384]{1,0:T(8,128)S(1)}, f32[128,384]{1,0:T(8,128)S(1)}, u32[]{:S(2)}, u32[]{:S(2)}) collective-permute-start(f32[128,384]{1,0:T(8,128)S(1)} %add_add_fusion.a0_ref), channel_id=1, source_target_pairs={{0,32},{32,0},{64,96},{96,64},{1,33},{33,1},{65,97},{97,65},{2,34}... | collective-permute-start | bytes 589832 | tf_op jit(solution)/shard_map/ppermute | solution.py:278
  86.6 2.8 %collective-permute-start.25 = (f32[128,128]{1,0:T(8,128)S(1)}, f32[128,128]{1,0:T(8,128)S(1)}, u32[]{:S(2)}, u32[]{:S(2)}) collective-permute-start(f32[128,128]{1,0:T(8,128)S(1)} %add_add_fusion.1.b0_ref), channel_id=1, source_target_pairs={{0,32},{32,0},{64,96},{96,64},{1,33},{33,1},{65,97},{97,65},{2,34}... | collective-permute-start | bytes 196616 | tf_op jit(solution)/shard_map/ppermute | solution.py:278
  90.4 1.8 %finish.1 = f32[4,2,64,256]{3,2,1,0:T(8,128)} custom-call(s32[2]{0:T(128)S(1)} %pad_add_fusion.where_ref, f32[128,384]{1,0:T(8,128)S(1)} %add_add_fusion.a0_ref, f32[128,384]{1,0:T(8,128)S(1)} %collective-permute-done.15.a1_ref, f32[128,128]{1,0:T(8,128)S(1)} %add_add_fusion.1.b0_ref, f32[128,128]{1,0:T(8,128)S(1)} %collective-permute-done.25.b1_ref), custom_call_target="tpu_custom_call" | custom-call | flops 200000 | bytes 1000000 | tf_op jit(solution)/shard_map/finish/pallas_call | solution.py:265
  (71 shorter events, 11.3 us)
Async XLA Ops:
  0.0 1.1 %copy-start = (bf16[64,3,8,2,128]{4,3,2,1,0:T(2,128)(2,1)S(1)}, bf16[64,3,8,2,128]{4,3,2,1,0:T(2,128)(2,1)}, u32[]{:S(2)}) copy-start(bf16[64,3,8,2,128]{4,3,2,1,0:T(2,128)(2,1)} %param.4) | copy-start | bytes 2359300
  2.6 8.1 %copy-start.2 = (bf16[48,64,128]{2,1,0:T(8,128)(2,1)}, bf16[48,64,128]{2,1,0:T(8,128)(2,1)S(1)}, u32[]{:S(2)}) copy-start(bf16[48,64,128]{2,1,0:T(8,128)(2,1)S(1)} %get-tuple-element.14.vt_ref) | copy-start | bytes 2359300
  2.6 20.2 %collective-permute-start = (bf16[24,64,128]{2,1,0:T(8,128)(2,1)S(1)}, bf16[24,64,128]{2,1,0:T(8,128)(2,1)S(1)}, u32[]{:S(2)}, u32[]{:S(2)}) collective-permute-start(bf16[24,64,128]{2,1,0:T(8,128)(2,1)S(1)} %get-tuple-element.15), channel_id=1, source_target_pairs={{0,28},{4,0},{8,4},{12,8},{16,12},{20,16},{24,20},{28,24},{1,29},{... | collective-permute-start | bytes 1179656 | tf_op jit(solution)/shard_map/ppermute | solution.py:278
  10.7 14.7 %collective-permute-start.6 = (bf16[1536,128]{1,0:T(8,128)(2,1)}, bf16[1536,128]{1,0:T(8,128)(2,1)S(1)}, u32[]{:S(2)}, u32[]{:S(2)}) collective-permute-start(bf16[1536,128]{1,0:T(8,128)(2,1)} %bitcast.7), channel_id=1, source_target_pairs={{0,1},{1,2},{2,3},{3,0},{4,5},{5,6},{6,7},{7,4},{8,9},{9,10},{10,1... | collective-permute-start | bytes 1179656 | tf_op jit(solution)/shard_map/ppermute | solution.py:278
  12.0 13.5 %collective-permute-start.5 = (bf16[1536,128]{1,0:T(8,128)(2,1)}, bf16[1536,128]{1,0:T(8,128)(2,1)}, u32[]{:S(2)}, u32[]{:S(2)}) collective-permute-start(bf16[1536,128]{1,0:T(8,128)(2,1)} %bitcast.8), channel_id=1, source_target_pairs={{0,3},{1,0},{2,1},{3,2},{4,7},{5,4},{6,5},{7,6},{8,11},{9,8},{10,9... | collective-permute-start | bytes 1179656 | tf_op jit(solution)/shard_map/ppermute | solution.py:278
  13.5 8.7 %collective-permute-start.3 = (bf16[7,64,128]{2,1,0:T(8,128)(2,1)S(1)}, bf16[7,64,128]{2,1,0:T(8,128)(2,1)S(1)}, u32[]{:S(2)}, u32[]{:S(2)}) collective-permute-start(bf16[7,64,128]{2,1,0:T(8,128)(2,1)S(1)} %get-tuple-element.18), channel_id=1, source_target_pairs={{0,32},{32,64},{64,96},{96,0},{1,33},{33,65},{65,97},{97,1},{2,34}... | collective-permute-start | bytes 344072 | tf_op jit(solution)/shard_map/ppermute | solution.py:278
  15.6 4.4 %collective-permute-start.2 = (bf16[6,64,128]{2,1,0:T(8,128)(2,1)S(1)}, bf16[6,64,128]{2,1,0:T(8,128)(2,1)S(1)}, u32[]{:S(2)}, u32[]{:S(2)}) collective-permute-start(bf16[6,64,128]{2,1,0:T(8,128)(2,1)S(1)} %get-tuple-element.17), channel_id=1, source_target_pairs={{0,96},{32,0},{64,32},{96,64},{1,97},{33,1},{65,33},{97,65},{2,98}... | collective-permute-start | bytes 294920 | tf_op jit(solution)/shard_map/ppermute | solution.py:278
  20.6 33.0 %collective-permute-start.4 = (bf16[1536,128]{1,0:T(8,128)(2,1)}, bf16[1536,128]{1,0:T(8,128)(2,1)}, u32[]{:S(2)}, u32[]{:S(2)}) collective-permute-start(bf16[1536,128]{1,0:T(8,128)(2,1)} %bitcast.7), channel_id=1, source_target_pairs={{0,3},{1,0},{2,1},{3,2},{4,7},{5,4},{6,5},{7,6},{8,11},{9,8},{10,9... | collective-permute-start | bytes 1179656 | tf_op jit(solution)/shard_map/ppermute | solution.py:278
  22.8 30.9 %collective-permute-start.7 = (bf16[1536,128]{1,0:T(8,128)(2,1)}, bf16[1536,128]{1,0:T(8,128)(2,1)}, u32[]{:S(2)}, u32[]{:S(2)}) collective-permute-start(bf16[1536,128]{1,0:T(8,128)(2,1)} %bitcast.8), channel_id=1, source_target_pairs={{0,1},{1,2},{2,3},{3,0},{4,5},{5,6},{6,7},{7,4},{8,9},{9,10},{10,1... | collective-permute-start | bytes 1179656 | tf_op jit(solution)/shard_map/ppermute | solution.py:278
  23.6 15.1 %collective-permute-start.1 = (bf16[26,64,128]{2,1,0:T(8,128)(2,1)S(1)}, bf16[26,64,128]{2,1,0:T(8,128)(2,1)S(1)}, u32[]{:S(2)}, u32[]{:S(2)}) collective-permute-start(bf16[26,64,128]{2,1,0:T(8,128)(2,1)S(1)} %get-tuple-element.16), channel_id=1, source_target_pairs={{0,4},{4,8},{8,12},{12,16},{16,20},{20,24},{24,28},{28,0},{1,5},{5... | collective-permute-start | bytes 1277960 | tf_op jit(solution)/shard_map/ppermute | solution.py:278
  25.4 35.7 %collective-permute-start.16 = (bf16[1536,128]{1,0:T(8,128)(2,1)S(1)}, bf16[1536,128]{1,0:T(8,128)(2,1)}, u32[]{:S(2)}, u32[]{:S(2)}) collective-permute-start(bf16[1536,128]{1,0:T(8,128)(2,1)S(1)} %collective-permute-done.6.refs_3_), channel_id=1, source_target_pairs={{0,1},{1,2},{2,3},{3,0},{4,5},{5,6},{6,7},{7,4},{8,9},{9,10},{10,1... | collective-permute-start | bytes 1179656 | tf_op jit(solution)/shard_map/ppermute | solution.py:278
  25.5 35.6 %collective-permute-start.17 = (bf16[1536,128]{1,0:T(8,128)(2,1)}, bf16[1536,128]{1,0:T(8,128)(2,1)}, u32[]{:S(2)}, u32[]{:S(2)}) collective-permute-start(bf16[1536,128]{1,0:T(8,128)(2,1)} %collective-permute-done.5.refs_2_), channel_id=1, source_target_pairs={{0,3},{1,0},{2,1},{3,2},{4,7},{5,4},{6,5},{7,6},{8,11},{9,8},{10,9... | collective-permute-start | bytes 1179656 | tf_op jit(solution)/shard_map/ppermute | solution.py:278
  39.4 1.1 %copy-start.3 = (bf16[48,64,128]{2,1,0:T(8,128)(2,1)S(1)}, bf16[48,64,128]{2,1,0:T(8,128)(2,1)}, u32[]{:S(2)}) copy-start(bf16[48,64,128]{2,1,0:T(8,128)(2,1)} %copy-done.2) | copy-start | bytes 2359300
  41.4 1.0 %copy-start.7 = (bf16[26,64,128]{2,1,0:T(8,128)(2,1)S(1)}, bf16[26,64,128]{2,1,0:T(8,128)(2,1)}, u32[]{:S(2)}) copy-start(bf16[26,64,128]{2,1,0:T(8,128)(2,1)} %copy-done.6) | copy-start | bytes 1277956
  53.7 1.1 %copy-start.1 = (bf16[64,3,8,2,128]{4,3,2,1,0:T(2,128)(2,1)S(1)}, bf16[64,3,8,2,128]{4,3,2,1,0:T(2,128)(2,1)}, u32[]{:S(2)}) copy-start(bf16[64,3,8,2,128]{4,3,2,1,0:T(2,128)(2,1)} %param.4) | copy-start | bytes 2359300
  61.2 3.2 %collective-permute-start.8 = (f32[128,384]{1,0:T(8,128)}, f32[128,384]{1,0:T(8,128)}, u32[]{:S(2)}, u32[]{:S(2)}) collective-permute-start(f32[128,384]{1,0:T(8,128)} %get-tuple-element.20), channel_id=1, source_target_pairs={{0,32},{32,0},{64,96},{96,64},{1,33},{33,1},{65,97},{97,65},{2,34}... | collective-permute-start | bytes 589832 | tf_op jit(solution)/shard_map/ppermute | solution.py:278
  61.2 3.2 %copy-start.11 = (f32[128,384]{1,0:T(8,128)S(1)}, f32[128,384]{1,0:T(8,128)}, u32[]{:S(2)}) copy-start(f32[128,384]{1,0:T(8,128)} %copy-done.10) | copy-start | bytes 589828
  63.8 5.1 %collective-permute-start.18 = (f32[128,128]{1,0:T(8,128)S(1)}, f32[128,128]{1,0:T(8,128)S(1)}, u32[]{:S(2)}, u32[]{:S(2)}) collective-permute-start(f32[128,128]{1,0:T(8,128)S(1)} %get-tuple-element.22), channel_id=1, source_target_pairs={{0,32},{32,0},{64,96},{96,64},{1,33},{33,1},{65,97},{97,65},{2,34}... | collective-permute-start | bytes 196616 | tf_op jit(solution)/shard_map/ppermute | solution.py:278
  65.3 5.7 %collective-permute-start.11 = (bf16[128,384]{1,0:T(8,128)(2,1)S(1)}, bf16[128,384]{1,0:T(8,128)(2,1)S(1)}, u32[]{:S(2)}, u32[]{:S(2)}) collective-permute-start(bf16[128,384]{1,0:T(8,128)(2,1)S(1)} %add_convert_fusion.1), channel_id=1, source_target_pairs={{0,12},{4,0},{8,4},{12,8},{16,28},{20,16},{24,20},{28,24},{1,13},{... | collective-permute-start | bytes 294920 | tf_op jit(solution)/shard_map/ppermute | solution.py:278
  67.6 7.6 %collective-permute-start.10 = (bf16[128,384]{1,0:T(8,128)(2,1)S(1)}, bf16[128,384]{1,0:T(8,128)(2,1)S(1)}, u32[]{:S(2)}, u32[]{:S(2)}) collective-permute-start(bf16[128,384]{1,0:T(8,128)(2,1)S(1)} %add_convert_fusion.1), channel_id=1, source_target_pairs={{0,4},{4,8},{8,12},{12,0},{16,20},{20,24},{24,28},{28,16},{1,5},{5... | collective-permute-start | bytes 294920 | tf_op jit(solution)/shard_map/ppermute | solution.py:278
  67.6 7.6 %collective-permute-start.9 = (bf16[128,384]{1,0:T(8,128)(2,1)S(1)}, bf16[128,384]{1,0:T(8,128)(2,1)S(1)}, u32[]{:S(2)}, u32[]{:S(2)}) collective-permute-start(bf16[128,384]{1,0:T(8,128)(2,1)S(1)} %add_convert_fusion.1), channel_id=1, source_target_pairs={{0,8},{4,12},{8,0},{12,4},{16,24},{20,28},{24,16},{28,20},{1,9},{5... | collective-permute-start | bytes 294920 | tf_op jit(solution)/shard_map/ppermute | solution.py:278
  68.9 7.3 %collective-permute-start.21 = (bf16[128,128]{1,0:T(8,128)(2,1)S(1)}, bf16[128,128]{1,0:T(8,128)(2,1)S(1)}, u32[]{:S(2)}, u32[]{:S(2)}) collective-permute-start(bf16[128,128]{1,0:T(8,128)(2,1)S(1)} %add_convert_fusion.3), channel_id=1, source_target_pairs={{0,12},{4,0},{8,4},{12,8},{16,28},{20,16},{24,20},{28,24},{1,13},{... | collective-permute-start | bytes 98312 | tf_op jit(solution)/shard_map/ppermute | solution.py:278
  70.3 8.9 %collective-permute-start.20 = (bf16[128,128]{1,0:T(8,128)(2,1)S(1)}, bf16[128,128]{1,0:T(8,128)(2,1)S(1)}, u32[]{:S(2)}, u32[]{:S(2)}) collective-permute-start(bf16[128,128]{1,0:T(8,128)(2,1)S(1)} %add_convert_fusion.3), channel_id=1, source_target_pairs={{0,4},{4,8},{8,12},{12,0},{16,20},{20,24},{24,28},{28,16},{1,5},{5... | collective-permute-start | bytes 98312 | tf_op jit(solution)/shard_map/ppermute | solution.py:278
  71.0 8.2 %collective-permute-start.19 = (bf16[128,128]{1,0:T(8,128)(2,1)S(1)}, bf16[128,128]{1,0:T(8,128)(2,1)S(1)}, u32[]{:S(2)}, u32[]{:S(2)}) collective-permute-start(bf16[128,128]{1,0:T(8,128)(2,1)S(1)} %add_convert_fusion.3), channel_id=1, source_target_pairs={{0,8},{4,12},{8,0},{12,4},{16,24},{20,28},{24,16},{28,20},{1,9},{5... | collective-permute-start | bytes 98312 | tf_op jit(solution)/shard_map/ppermute | solution.py:278
  75.2 4.8 %collective-permute-start.14 = (bf16[128,384]{1,0:T(8,128)(2,1)S(1)}, bf16[128,384]{1,0:T(8,128)(2,1)S(1)}, u32[]{:S(2)}, u32[]{:S(2)}) collective-permute-start(bf16[128,384]{1,0:T(8,128)(2,1)S(1)} %add_convert_fusion), channel_id=1, source_target_pairs={{0,80},{4,84},{8,88},{12,92},{16,64},{20,68},{24,72},{28,76},{32,1... | collective-permute-start | bytes 294920 | tf_op jit(solution)/shard_map/ppermute | solution.py:278
  75.3 7.8 %collective-permute-start.13 = (bf16[128,384]{1,0:T(8,128)(2,1)S(1)}, bf16[128,384]{1,0:T(8,128)(2,1)S(1)}, u32[]{:S(2)}, u32[]{:S(2)}) collective-permute-start(bf16[128,384]{1,0:T(8,128)(2,1)S(1)} %add_convert_fusion), channel_id=1, source_target_pairs={{0,64},{32,96},{64,0},{96,32},{1,65},{33,97},{65,1},{97,33},{2,66}... | collective-permute-start | bytes 294920 | tf_op jit(solution)/shard_map/ppermute | solution.py:278
  76.2 7.0 %collective-permute-start.12 = (bf16[128,384]{1,0:T(8,128)(2,1)S(1)}, bf16[128,384]{1,0:T(8,128)(2,1)S(1)}, u32[]{:S(2)}, u32[]{:S(2)}) collective-permute-start(bf16[128,384]{1,0:T(8,128)(2,1)S(1)} %add_convert_fusion), channel_id=1, source_target_pairs={{0,16},{4,20},{8,24},{12,28},{16,0},{20,4},{24,8},{28,12},{1,17},{... | collective-permute-start | bytes 294920 | tf_op jit(solution)/shard_map/ppermute | solution.py:278
  79.2 7.4 %collective-permute-start.24 = (bf16[128,128]{1,0:T(8,128)(2,1)S(1)}, bf16[128,128]{1,0:T(8,128)(2,1)S(1)}, u32[]{:S(2)}, u32[]{:S(2)}) collective-permute-start(bf16[128,128]{1,0:T(8,128)(2,1)S(1)} %add_convert_fusion.2), channel_id=1, source_target_pairs={{0,80},{4,84},{8,88},{12,92},{16,64},{20,68},{24,72},{28,76},{32,1... | collective-permute-start | bytes 98312 | tf_op jit(solution)/shard_map/ppermute | solution.py:278
  79.4 7.2 %collective-permute-start.23 = (bf16[128,128]{1,0:T(8,128)(2,1)S(1)}, bf16[128,128]{1,0:T(8,128)(2,1)S(1)}, u32[]{:S(2)}, u32[]{:S(2)}) collective-permute-start(bf16[128,128]{1,0:T(8,128)(2,1)S(1)} %add_convert_fusion.2), channel_id=1, source_target_pairs={{0,64},{32,96},{64,0},{96,32},{1,65},{33,97},{65,1},{97,33},{2,66}... | collective-permute-start | bytes 98312 | tf_op jit(solution)/shard_map/ppermute | solution.py:278
  80.0 6.6 %collective-permute-start.22 = (bf16[128,128]{1,0:T(8,128)(2,1)S(1)}, bf16[128,128]{1,0:T(8,128)(2,1)S(1)}, u32[]{:S(2)}, u32[]{:S(2)}) collective-permute-start(bf16[128,128]{1,0:T(8,128)(2,1)S(1)} %add_convert_fusion.2), channel_id=1, source_target_pairs={{0,16},{4,20},{8,24},{12,28},{16,0},{20,4},{24,8},{28,12},{1,17},{... | collective-permute-start | bytes 98312 | tf_op jit(solution)/shard_map/ppermute | solution.py:278
  83.2 7.2 %collective-permute-start.15 = (f32[128,384]{1,0:T(8,128)S(1)}, f32[128,384]{1,0:T(8,128)S(1)}, u32[]{:S(2)}, u32[]{:S(2)}) collective-permute-start(f32[128,384]{1,0:T(8,128)S(1)} %add_add_fusion.a0_ref), channel_id=1, source_target_pairs={{0,32},{32,0},{64,96},{96,64},{1,33},{33,1},{65,97},{97,65},{2,34}... | collective-permute-start | bytes 589832 | tf_op jit(solution)/shard_map/ppermute | solution.py:278
  86.6 3.7 %collective-permute-start.25 = (f32[128,128]{1,0:T(8,128)S(1)}, f32[128,128]{1,0:T(8,128)S(1)}, u32[]{:S(2)}, u32[]{:S(2)}) collective-permute-start(f32[128,128]{1,0:T(8,128)S(1)} %add_add_fusion.1.b0_ref), channel_id=1, source_target_pairs={{0,32},{32,0},{64,96},{96,64},{1,33},{33,1},{65,97},{97,65},{2,34}... | collective-permute-start | bytes 196616 | tf_op jit(solution)/shard_map/ppermute | solution.py:278
  (11 other events, 8.7 us)

commit v2 on v1

v2 whole, which is shorter than its diff:
```python
import functools
import math

import jax
import jax.numpy as jnp
from jax import lax
from jax.experimental import pallas as pl
from jax.experimental.pallas import tpu as pltpu
from jax.sharding import PartitionSpec as P

F32 = jnp.float32
BF16 = jnp.bfloat16
VMEM = pl.BlockSpec(memory_space=pltpu.VMEM)
SMEM = pl.BlockSpec(memory_space=pltpu.SMEM)
ANY = pl.BlockSpec(memory_space=pl.ANY)
HBM = pl.BlockSpec(memory_space=pltpu.HBM)

NV = 64
COL = 3
DZ = 8
HY = 2
LANES = 128
HALF = 64
NZY = DZ * HY
EXT_X, EXT_Y, EXT_Z = 64, 16, 32
NK = COL * NZY
KDIM = NK * LANES


def params(limit):
    return pltpu.CompilerParams(vmem_limit_bytes=limit * 1024 * 1024)


def shape(dims, dtype):
    return jax.ShapeDtypeStruct(dims, dtype)


def fetch(sources, targets, sem):
    copies = [
        pltpu.make_async_copy(source, target, sem.at[i])
        for i, (source, target) in enumerate(zip(sources, targets))
    ]
    for copy in copies:
        copy.start()
    return copies


def prepare_kernel(rows, lrows, y0_ref, y1_ref, z0_ref, z1_ref, wide, lwide):
    wide[...] = rows[...].astype(F32)
    lwide[0:432, :] = lrows[...].astype(F32)
    lwide[432:576, :] = jnp.zeros((144, LANES), F32)
    for k in range(NK):
        tile = wide[pl.ds(k, NV, stride=NK), :].astype(BF16)
        c, z, y = k // NZY, (k % NZY) // HY, k % HY
        if y == 0:
            y0_ref[c * DZ + z] = tile
        else:
            y1_ref[c * DZ + z] = tile
        if z == 0:
            z0_ref[c * HY + y] = tile
        if z == DZ - 1:
            z1_ref[c * HY + y] = tile
    rim = lwide[pl.ds(9 * NZY + 1, 72, stride=HY), :]
    rim = jnp.concatenate([rim, jnp.zeros((56, LANES), F32)], 0).astype(BF16)
    y1_ref[24] = rim[0:64]
    y1_ref[25] = rim[64:128]
    low = lwide[pl.ds(18 * NZY + 14, 16, stride=NZY), :]
    high = lwide[pl.ds(18 * NZY + 15, 16, stride=NZY), :]
    rest = jnp.zeros((32, LANES), F32)
    z1_ref[6] = jnp.concatenate([low, high, rest], 0).astype(BF16)


def prepare(rows, link_rows):
    return pl.pallas_call(
        prepare_kernel,
        out_shape=(
            shape((24, NV, LANES), BF16),
            shape((26, NV, LANES), BF16),
            shape((6, NV, LANES), BF16),
            shape((7, NV, LANES), BF16),
        ),
        in_specs=[VMEM] * 2,
        out_specs=(VMEM,) * 4,
        scratch_shapes=[
            pltpu.VMEM((NV * NK, LANES), F32),
            pltpu.VMEM((576, LANES), F32),
        ],
        compiler_params=params(6),
        cost_estimate=pl.CostEstimate(flops=2000000000, bytes_accessed=3000000, transcendentals=0),
        name="prepare",
    )(rows, link_rows)


def line_coefficients(rows, first):
    half = rows * 0.5
    swapped = pltpu.roll(half, HALF, 1)
    return jnp.where(first, half, swapped), jnp.where(first, swapped, half)


def lane_masks():
    lane = lax.broadcasted_iota(jnp.int32, (1, LANES), 1)
    return lane, lane < HALF, jnp.where(lane < HALF, -1.0, 1.0).astype(F32)


def derivative(mu, neighbour, tables, zy, store):
    upr, upi, dnr, dni = tables
    out = [None] * 3
    for c in range(COL):
        here, swap = neighbour(c, 1)
        for r in range(3):
            at = mu * 9 + r * 3 + c
            term = here * upr[zy, at:at + 1, :] + swap * upi[zy, at:at + 1, :]
            out[r] = term if out[r] is None else out[r] + term
    for c in range(COL):
        here, swap = neighbour(c, -1)
        for r in range(3):
            at = mu * 9 + c * 3 + r
            term = here * dnr[zy, at:at + 1, :] - swap * dni[zy, at:at + 1, :]
            out[r] = out[r] - term
    for r in range(3):
        store(r, out[r].astype(BF16))


def local_kernel(
    momentum_ref, v_ref, l_ref, w_ref, ext, exts, upr, upi, dnr, dni,
    wide, lwide, real, imag, cos_ref, sin_ref,
):
    lane, first, sign = lane_masks()
    at = lax.broadcasted_iota(jnp.int32, (NZY, LANES), 0)
    x = lax.broadcasted_iota(jnp.int32, (NZY, LANES), 1) & (HALF - 1)
    y = lax.axis_index("gy").astype(jnp.int32) * HY + (at & (HY - 1))
    z = lax.axis_index("gz").astype(jnp.int32) * DZ + (at >> 1)
    frac_x = ((momentum_ref[0] * x) & (EXT_X - 1)).astype(F32) / EXT_X
    frac_y = ((momentum_ref[1] * y) & (EXT_Y - 1)).astype(F32) / EXT_Y
    frac_z = ((momentum_ref[2] * z) & (EXT_Z - 1)).astype(F32) / EXT_Z
    angle = 2.0 * math.pi * (frac_z + frac_y + frac_x)
    cos_ref[...] = jnp.cos(angle)
    sin_ref[...] = -sign * jnp.sin(angle)

    wide[...] = v_ref[...].astype(F32)
    for c in range(COL):
        for z in range(DZ):
            for y in range(HY):
                tile = wide[pl.ds((c * DZ + z) * HY + y, NV, stride=NK), :]
                ext[c, z + 1, y + 1] = tile
                exts[c, z + 1, y + 1] = pltpu.roll(tile, HALF, 1)

    lwide[...] = l_ref[...].astype(F32)
    re, im = line_coefficients(lwide[...], first)
    real[...] = re
    imag[...] = im
    for zy in range(NZY):
        z, y = zy // HY, zy % HY
        pick = pl.ds(zy, 27, stride=NZY)
        upr[zy, 0:27, :] = real[pick, :]
        upi[zy, 0:27, :] = imag[pick, :] * sign
        pick = pl.ds(zy, 9, stride=NZY)
        dnr[zy, 0:9, :] = pltpu.roll(real[pick, :], 1, 1)
        dni[zy, 0:9, :] = pltpu.roll(imag[pick, :], 1, 1) * sign
        if y:
            pick = pl.ds(9 * NZY + zy - 1, 9, stride=NZY)
            dnr[zy, 9:18, :] = real[pick, :]
            dni[zy, 9:18, :] = imag[pick, :] * sign
        if z:
            pick = pl.ds(18 * NZY + zy - HY, 9, stride=NZY)
            dnr[zy, 18:27, :] = real[pick, :]
            dni[zy, 18:27, :] = imag[pick, :] * sign

    wrap_up = (lane == HALF - 1) | (lane == LANES - 1)
    wrap_down = (lane == 0) | (lane == HALF)

    def site(zy, carry):
        z = lax.div(zy, HY) + 1
        y = lax.rem(zy, HY) + 1

        def neighbour(c, step):
            here, swap = ext[c, z, y], exts[c, z, y]
            a = pltpu.roll(here, (-step) % LANES, 1)
            b = pltpu.roll(swap, (-step) % LANES, 1)
            wrap = wrap_up if step == 1 else wrap_down
            return jnp.where(wrap, b, a), jnp.where(wrap, a, b)

        def store(r, value):
            column = pl.multiple_of((r * NZY + zy) * LANES, LANES)
            w_ref[0, :, pl.ds(column, LANES)] = value

        derivative(0, neighbour, (upr, upi, dnr, dni), zy, store)
        cosine = cos_ref[pl.ds(zy, 1), :]
        sine = sin_ref[pl.ds(zy, 1), :]
        for c in range(COL):
            column = pl.multiple_of((c * NZY + zy) * LANES, LANES)
            phased = ext[c, z, y] * cosine + exts[c, z, y] * sine
            w_ref[1, :, pl.ds(column, LANES)] = phased.astype(BF16)
        return carry

    lax.fori_loop(0, NZY, site, 0)


EXTENDED = (COL, DZ + 2, HY + 2, NV, LANES)
TABLE = (NZY, 32, LANES)


def local_terms(momentum, rows, link_rows):
    line = pltpu.VMEM((27 * NZY, LANES), F32)
    return pl.pallas_call(
        local_kernel,
        out_shape=(shape((4, NV, KDIM), BF16),)
        + (shape(EXTENDED, F32),) * 2
        + (shape(TABLE, F32),) * 4,
        in_specs=[SMEM] + [VMEM] * 2,
        out_specs=(VMEM,) * 7,
        scratch_shapes=[
            pltpu.VMEM((NV * NK, LANES), F32),
            line,
            line,
            line,
            pltpu.VMEM((NZY, LANES), F32),
            pltpu.VMEM((NZY, LANES), F32),
        ],
        compiler_params=params(8),
        cost_estimate=pl.CostEstimate(flops=6000000000, bytes_accessed=6000000, transcendentals=0),
        name="local_terms",
    )(momentum, rows, link_rows)


def border_kernel(
    local_ref, e_ref, s_ref, upr, upi, r_ref, i_ref, yp_ref, ym_ref, zp_ref, zm_ref,
    w_ref, ext, exts, dnr, dni, lwide, real, imag,
):
    lane, first, sign = lane_masks()

    def put(c, z, y, tile):
        tile = tile.astype(F32)
        ext[c, z, y] = tile
        exts[c, z, y] = pltpu.roll(tile, HALF, 1)

    for c in range(COL):
        for z in range(DZ):
            put(c, z + 1, HY + 1, yp_ref[c * DZ + z])
            put(c, z + 1, 0, ym_ref[c * DZ + z])
        for y in range(HY):
            put(c, DZ + 1, y + 1, zp_ref[c * HY + y])
            put(c, 0, y + 1, zm_ref[c * HY + y])

    lwide[0:128, :] = jnp.concatenate([ym_ref[24], ym_ref[25]], 0).astype(F32)
    lwide[128:192, :] = zm_ref[6].astype(F32)
    re, im = line_coefficients(lwide[...], first)
    real[...] = re
    imag[...] = im * sign
    for z in range(DZ):
        pick = pl.ds(z, 9, stride=DZ)
        dnr[z * HY, 9:18, :] = real[pick, :]
        dni[z * HY, 9:18, :] = imag[pick, :]
    for y in range(HY):
        pick = pl.ds(128 + 16 * y, 9)
        dnr[y, 18:27, :] = real[pick, :]
        dni[y, 18:27, :] = imag[pick, :]

    def site(zy, carry):
        z = lax.div(zy, HY) + 1
        y = lax.rem(zy, HY) + 1
        for mu in (1, 2):

            def neighbour(c, step):
                at = (c, z, y + step) if mu == 1 else (c, z + step, y)
                return ext[at], exts[at]

            def store(r, value):
                column = pl.multiple_of((r * NZY + zy) * LANES, LANES)
                w_ref[mu + 1, :, pl.ds(column, LANES)] = value

            derivative(mu, neighbour, (upr, upi, dnr, dni), zy, store)
        return carry

    lax.fori_loop(0, NZY, site, 0)


def border_terms(w, ext, exts, upr, upi, dnr, dni, yp, ym, zp, zm):
    line = pltpu.VMEM((192, LANES), F32)
    return pl.pallas_call(
        border_kernel,
        out_shape=(shape((4, NV, KDIM), BF16),)
        + (shape(EXTENDED, F32),) * 2
        + (shape(TABLE, F32),) * 2,
        in_specs=[VMEM] * 11,
        out_specs=(VMEM,) * 5,
        input_output_aliases={0: 0, 1: 1, 2: 2, 5: 3, 6: 4},
        scratch_shapes=[line, line, line],
        compiler_params=params(4),
        cost_estimate=pl.CostEstimate(flops=6000000000, bytes_accessed=6000000, transcendentals=0),
        name="border_terms",
    )(w, ext, exts, upr, upi, dnr, dni, yp, ym, zp, zm)[0]


def fill_right(counts, blocks, wide, right):
    total = sum(counts)
    lane, first, sign = lane_masks()
    start = 0
    for block, count in zip(blocks, counts):
        wide[0:count * NK, :] = block[...].astype(F32)
        for k in range(NK):
            tile = wide[pl.ds(k, count, stride=NK), :]
            swap = pltpu.roll(tile, HALF, 1) * sign
            right[start:start + count, k * LANES:(k + 1) * LANES] = tile.astype(BF16)
            right[total + start:total + start + count, k * LANES:(k + 1) * LANES] = swap.astype(BF16)
        start += count


def dot_halves(w_ref, right, keep_ref, send_ref, product):
    left = w_ref[...].reshape(4 * NV, KDIM)
    dots = lax.dot_general(left, right[...], (((1,), (1,)), ((), ())), preferred_element_type=F32)
    product[...] = dots.reshape(2, 2 * NV, dots.shape[1])
    mine = lax.axis_index("gz").astype(jnp.int32) & 1
    keep_ref[...] = product[mine]
    send_ref[...] = product[1 - mine]


def right_kernel(counts, *refs):
    n = len(counts)
    fill_right(counts, refs[:n], refs[n + 1], refs[n])


def right_side(blocks):
    counts = tuple(b.shape[0] // NK for b in blocks)
    return pl.pallas_call(
        functools.partial(right_kernel, counts),
        out_shape=shape((2 * sum(counts), KDIM), BF16),
        in_specs=[VMEM] * len(blocks),
        out_specs=VMEM,
        scratch_shapes=[pltpu.VMEM((max(counts) * NK, LANES), F32)],
        compiler_params=params(4),
        cost_estimate=pl.CostEstimate(flops=2000000000, bytes_accessed=4000000, transcendentals=0),
        name="right_side",
    )(*blocks)


def near_kernel(w_ref, right_ref, keep_ref, send_ref, product):
    dot_halves(w_ref, right_ref, keep_ref, send_ref, product)


def far_kernel(counts, w_ref, *refs):
    n = len(counts)
    keep_ref, send_ref, wide, right, product = refs[n:]
    fill_right(counts, refs[:n], wide, right)
    dot_halves(w_ref, right, keep_ref, send_ref, product)


def contract_near(w, right):
    columns = right.shape[0]
    out = shape((2 * NV, columns), F32)
    return pl.pallas_call(
        near_kernel,
        out_shape=(out, out),
        in_specs=[VMEM] * 2,
        out_specs=(VMEM, VMEM),
        scratch_shapes=[pltpu.VMEM((2, 2 * NV, columns), F32)],
        compiler_params=params(4),
        cost_estimate=pl.CostEstimate(
            flops=2 * 256 * columns * KDIM, bytes_accessed=4000000, transcendentals=0
        ),
        name="contract_near",
    )(w, right)


def contract_far(w, blocks):
    counts = tuple(b.shape[0] // NK for b in blocks)
    columns = 2 * sum(counts)
    out = shape((2 * NV, columns), F32)
    return pl.pallas_call(
        functools.partial(far_kernel, counts),
        out_shape=(out, out),
        in_specs=[VMEM] * (1 + len(blocks)),
        out_specs=(VMEM, VMEM),
        scratch_shapes=[
            pltpu.VMEM((max(counts) * NK, LANES), F32),
            pltpu.VMEM((columns, KDIM), BF16),
            pltpu.VMEM((2, 2 * NV, columns), F32),
        ],
        compiler_params=params(5),
        cost_estimate=pl.CostEstimate(
            flops=2 * 256 * columns * KDIM, bytes_accessed=4000000, transcendentals=0
        ),
        name="contract_far",
    )(w, *blocks)


def finish_kernel(scale, dirs_ref, mine_ref, other_ref, out_ref):
    shift = lax.axis_index("vec").astype(jnp.int32) * HALF
    core = lax.axis_index("gz").astype(jnp.int32) & 1
    slots = [
        sum(jnp.where(dirs_ref[o] == mu, o, 0) for o in range(3)).astype(jnp.int32)
        for mu in range(3)
    ]
    for ch, rows_ref in enumerate((mine_ref, other_ref)):
        rows = rows_ref[...]
        for part in range(2):
            near = rows[:, part * 192:(part + 1) * 192]
            far = rows[:, 384 + part * 64:384 + (part + 1) * 64]
            line = jnp.concatenate([near[:, 0:128], far, near[:, 128:192]], 1) * scale
            line = pltpu.roll(line, shift, 1)
            half = core if ch == 0 else 1 - core
            out_ref[jnp.where(half == 0, slots[0], slots[1]), part] = line[0:NV]
            out_ref[jnp.where(half == 0, 3, slots[2]), part] = line[NV:2 * NV]


def finish(directions, mine, other, scale):
    return pl.pallas_call(
        functools.partial(finish_kernel, scale),
        out_shape=shape((4, 2, NV, 256), F32),
        in_specs=[SMEM] + [VMEM] * 2,
        out_specs=VMEM,
        compiler_params=params(16),
        cost_estimate=pl.CostEstimate(flops=200000, bytes_accessed=1000000, transcendentals=0),
        name="finish",
    )(directions, mine, other)


def permuted(value, axis, target):
    size = lax.axis_size(axis)
    return lax.ppermute(value, axis, [(source, target(source)) for source in range(size)])


def four_sum(own, axis_opposite, axis_side, axis_other):
    wide = [t.astype(F32) for t in (own, axis_opposite, axis_side, axis_other)]
    return (wide[0] + wide[1]) + (wide[2] + wide[3])


def body(vectors, links, momentum, directions):
    rows = vectors.reshape(NV * NK, LANES)
    link_rows = links.reshape(27 * NZY, LANES)
    mid = NV * NK // 2
    prev = permuted(rows, "vec", lambda s: (s + 1) % 4)
    next_ = permuted(rows, "vec", lambda s: (s - 1) % 4)

    y0, y1, z0, z1 = prepare(rows, link_rows)
    yp = permuted(y0, "gy", lambda s: (s - 1) % 8)
    ym = permuted(y1, "gy", lambda s: (s + 1) % 8)
    prev, next_, zz = lax.optimization_barrier((prev, next_, z1))
    zp = permuted(z0, "gz", lambda s: (s - 1) % 4)
    z1, zp = lax.optimization_barrier((zz, zp))
    zm = permuted(z1, "gz", lambda s: (s + 1) % 4)
    partial = local_terms(momentum, rows, link_rows)

    far_low = permuted(prev[:mid], "vec", lambda s: (s + 1) % 4)
    far_high = permuted(next_[mid:], "vec", lambda s: (s - 1) % 4)

    right = right_side([rows, next_, prev])
    w = border_terms(*partial, yp, ym, zp, zm)

    mate = lambda v: permuted(v, "gz", lambda s: s ^ 1)
    along_x = lambda v, step: permuted(v, "gy", lambda s: (s // 4) * 4 + (s + step) % 4)

    def row_sum(keep, send):
        chip = (keep + mate(send)).astype(BF16)
        return four_sum(chip, along_x(chip, 2), along_x(chip, 1), along_x(chip, 3)).astype(BF16)

    near = row_sum(*contract_near(w, right))
    far = row_sum(*contract_far(w, [far_low, far_high]))
    row = jnp.concatenate([near, far], 1)
    across = permuted(row, "gy", lambda s: s ^ 4)
    side = permuted(row, "gz", lambda s: s ^ 2)
    both = permuted(row, ("gz", "gy"), lambda s: s ^ 20)
    plane = four_sum(row, across, side, both)
    scale = 1.0 / math.sqrt(EXT_X * EXT_Y * EXT_Z)
    return finish(directions, plane, mate(plane), scale)


def solution(mesh):
    in_specs = (P("vec", None, "gz", "gy", None), P(None, None, None, "gz", "gy", None), P(), P())
    out_specs = P(None, None, "vec", None)
    return jax.shard_map(body, mesh=mesh, in_specs=in_specs, out_specs=out_specs, check_vma=False)
```

time: 92.7 us -> 63.3 us (0.68)
  local copies, waits for them, and re-layouts: 15.9 us -> 2.13 us
  starting transfers between devices: 37.3 us -> 32 us
  waiting for transfers between devices: 17.3 us -> 13.1 us
  other arithmetic: 3.14 us -> 0.19 us
  Pallas kernels: 18.4 us -> 15.7 us
    unnamed x34 -> x12, local copies, waits for them, and re-layouts: 13.1 us -> 2.08 us
    ppermute x26 -> x20, starting transfers between devices: 37.3 us -> 32 us  [permuted(): lax.ppermute(value, axis, [(source, target(source)) for source in range(s...]
    ppermute x26 -> x20, waiting for transfers between devices: 17.3 us -> 13.1 us  [permuted(): lax.ppermute(value, axis, [(source, target(source)) for source in range(s...]
    slice x2, local copies, waits for them, and re-layouts: 2.79 us -> 0.05 us  [the longest x1 0.03 us: body(): far_low = permuted(prev[:mid], 'vec', lambda s: (s + 1) % 4)]
    pallas_call x4 -> x6, Pallas kernels: 16.6 us -> 13.9 us  [the longest x1 4.85 us: local_terms(): pl.pallas_call(local_kernel, out_shape=(shape((4, NV, KDIM), BF16),) + (s...]
    add x1 -> x0, other arithmetic: 1.29 us -> none  [body(): angle = 2.0 * math.pi * ((frac_z + frac_y)[:, None] + frac_x[None, :])]
  transfers between devices with their start and end apart: 26 -> 20, of which waited for: 5 -> 8; matrix products, arithmetic and copies ran while one was open for 6% -> 0% of each run, Pallas kernels for 17% -> 22%
where the time goes in v2:
time: 63.3 us; the launch traced here: 63.2 us
  starting transfers between devices  32 us (51%)
  Pallas kernels  15.7 us (25%)
  waiting for transfers between devices  13.1 us (21%)
  local copies, waits for them, and re-layouts  2.13 us (3%)
    ppermute x20, starting transfers between devices, permuted(): lax.ppermute(value, axis, [(source, target(source)) for source in range(s...  32 us
    ppermute x20, waiting for transfers between devices, permuted(): lax.ppermute(value, axis, [(source, target(source)) for source in range(s...  13.1 us
    pallas_call x1, Pallas kernels, local_terms(): pl.pallas_call(local_kernel, out_shape=(shape((4, NV, KDIM), BF16),) + (s...  4.85 us
    pallas_call x1, Pallas kernels, border_terms(): pl.pallas_call(border_kernel, out_shape=(shape((4, NV, KDIM), BF16),) + (...  3.06 us
    pallas_call x1, Pallas kernels, right_side(): pl.pallas_call(functools.partial(right_kernel, counts), out_shape=shape((...  2.15 us
    unnamed x12, local copies, waits for them, and re-layouts  2.08 us
    pallas_call x1, Pallas kernels, contract_near(): pl.pallas_call(near_kernel, out_shape=(out, out), in_specs=[VMEM] * 2, ou...  1.87 us
    pallas_call x1, Pallas kernels, finish(): pl.pallas_call(functools.partial(finish_kernel, scale), out_shape=shape((...  1.76 us
  transfers between devices with their start and end apart: 20, of which 8 were waited for; matrix products, arithmetic and copies ran while one was open for 0% of the time, Pallas kernels for 22%

profile of v2, /device:TPU:1, one launch (start us, length us, event | category | flops | bytes accessed | tf_op | source)
XLA Modules:
  0.0 63.2 jit_solution(3267061403124424300)
XLA Ops:
  0.0 2.1 %collective-permute-start.2 = (bf16[3072,128]{1,0:T(8,128)(2,1)}, bf16[3072,128]{1,0:T(8,128)(2,1)S(1)}, u32[]{:S(2)}, u32[]{:S(2)}) collective-permute-start(bf16[3072,128]{1,0:T(8,128)(2,1)} %bitcast.2), channel_id=1, source_target_pairs={{0,1},{1,2},{2,3},{3,0},{4,5},{5,6},{6,7},{7,4},{8,9},{9,10},{10,1... | collective-permute-start | bytes 2359304 | tf_op jit(solution)/shard_map/ppermute | solution.py:420
  2.1 1.5 %collective-permute-start.3 = (bf16[3072,128]{1,0:T(8,128)(2,1)}, bf16[3072,128]{1,0:T(8,128)(2,1)S(1)}, u32[]{:S(2)}, u32[]{:S(2)}) collective-permute-start(bf16[3072,128]{1,0:T(8,128)(2,1)} %bitcast.3), channel_id=1, source_target_pairs={{0,3},{1,0},{2,1},{3,2},{4,7},{5,4},{6,5},{7,6},{8,11},{9,8},{10,9... | collective-permute-start | bytes 2359304 | tf_op jit(solution)/shard_map/ppermute | solution.py:420
  3.6 1.2 %copy-done.1 = bf16[64,3,8,2,128]{4,3,2,1,0:T(2,128)(2,1)S(1)} copy-done((bf16[64,3,8,2,128]{4,3,2,1,0:T(2,128)(2,1)S(1)}, bf16[64,3,8,2,128]{4,3,2,1,0:T(2,128)(2,1)}, u32[]{:S(2)}) %copy-start.1) | copy-done | bytes 786456
  4.8 0.9 %copy-done.3 = bf16[3,3,3,8,2,128]{5,4,3,2,1,0:T(2,128)(2,1)S(1)} copy-done((bf16[3,3,3,8,2,128]{5,4,3,2,1,0:T(2,128)(2,1)S(1)}, bf16[3,3,3,8,2,128]{5,4,3,2,1,0:T(2,128)(2,1)}, u32[]{:S(2)}) %copy-start.3) | copy-done | bytes 110616
  5.7 0.6 prepare.1
  6.3 1.1 %collective-permute-start.4 = (bf16[6,64,128]{2,1,0:T(8,128)(2,1)S(1)}, bf16[6,64,128]{2,1,0:T(8,128)(2,1)S(1)}, u32[]{:S(2)}, u32[]{:S(2)}) collective-permute-start(bf16[6,64,128]{2,1,0:T(8,128)(2,1)S(1)} %get-tuple-element.37), channel_id=1, source_target_pairs={{0,96},{32,0},{64,32},{96,64},{1,97},{33,1},{65,33},{97,65},{2,98}... | collective-permute-start | bytes 294920 | tf_op jit(solution)/shard_map/ppermute | solution.py:420
  7.4 1.3 %collective-permute-start.1 = (bf16[26,64,128]{2,1,0:T(8,128)(2,1)S(1)}, bf16[26,64,128]{2,1,0:T(8,128)(2,1)S(1)}, u32[]{:S(2)}, u32[]{:S(2)}) collective-permute-start(bf16[26,64,128]{2,1,0:T(8,128)(2,1)S(1)} %get-tuple-element.34), channel_id=1, source_target_pairs={{0,4},{4,8},{8,12},{12,16},{16,20},{20,24},{24,28},{28,0},{1,5},{5... | collective-permute-start | bytes 1277960 | tf_op jit(solution)/shard_map/ppermute | solution.py:420
  8.7 4.6 %collective-permute-start = (bf16[24,64,128]{2,1,0:T(8,128)(2,1)S(1)}, bf16[24,64,128]{2,1,0:T(8,128)(2,1)S(1)}, u32[]{:S(2)}, u32[]{:S(2)}) collective-permute-start(bf16[24,64,128]{2,1,0:T(8,128)(2,1)S(1)} %get-tuple-element.33), channel_id=1, source_target_pairs={{0,28},{4,0},{8,4},{12,8},{16,12},{20,16},{24,20},{28,24},{1,29},{... | collective-permute-start | bytes 1179656 | tf_op jit(solution)/shard_map/ppermute | solution.py:420
  13.3 4.8 %local_terms.1 = (bf16[4,64,6144]{2,1,0:T(8,128)(2,1)S(1)}, f32[3,10,4,64,128]{4,3,2,1,0:T(8,128)S(1)}, f32[3,10,4,64,128]{4,3,2,1,0:T(8,128)S(1)}, f32[16,32,12...) custom-call(s32[3]{0:T(128)S(1)} %copy-done.5, ...), custom_call_target="tpu_custom_call" | custom-call | flops 6000000000 | bytes 6000000 | tf_op jit(solution)/shard_map/local_terms/pallas_call | solution.py:205
  18.1 2.8 %collective-permute-done.2.refs_2_ = bf16[3072,128]{1,0:T(8,128)(2,1)S(1)} collective-permute-done((bf16[3072,128]{1,0:T(8,128)(2,1)}, bf16[3072,128]{1,0:T(8,128)(2,1)S(1)}, u32[]{:S(2)}, u32[]{:S(2)}) %collective-permute-start.2) | collective-permute-done | bytes 786464 | tf_op jit(solution)/shard_map/ppermute | solution.py:420
  20.9 2.9 %collective-permute-start.5 = (bf16[7,64,128]{2,1,0:T(8,128)(2,1)S(1)}, bf16[7,64,128]{2,1,0:T(8,128)(2,1)S(1)}, u32[]{:S(2)}, u32[]{:S(2)}) collective-permute-start(bf16[7,64,128]{2,1,0:T(8,128)(2,1)S(1)} %get-tuple-element.39), channel_id=1, source_target_pairs={{0,32},{32,64},{64,96},{96,0},{1,33},{33,65},{65,97},{97,1},{2,34}... | collective-permute-start | bytes 344072 | tf_op jit(solution)/shard_map/ppermute | solution.py:420
  23.9 1.4 %collective-permute-start.10 = (bf16[1536,128]{1,0:T(8,128)(2,1)S(1)}, bf16[1536,128]{1,0:T(8,128)(2,1)S(1)}, u32[]{:S(2)}, u32[]{:S(2)}) collective-permute-start(bf16[1536,128]{1,0:T(8,128)(2,1)S(1)} %slice.6), channel_id=1, source_target_pairs={{0,1},{1,2},{2,3},{3,0},{4,5},{5,6},{6,7},{7,4},{8,9},{9,10},{10,1... | collective-permute-start | bytes 1179656 | tf_op jit(solution)/shard_map/ppermute | solution.py:420
  25.2 1.5 %collective-permute-start.11 = (bf16[1536,128]{1,0:T(8,128)(2,1)S(1)}, bf16[1536,128]{1,0:T(8,128)(2,1)S(1)}, u32[]{:S(2)}, u32[]{:S(2)}) collective-permute-start(bf16[1536,128]{1,0:T(8,128)(2,1)S(1)} %slice.7), channel_id=1, source_target_pairs={{0,3},{1,0},{2,1},{3,2},{4,7},{5,4},{6,5},{7,6},{8,11},{9,8},{10,9... | collective-permute-start | bytes 1179656 | tf_op jit(solution)/shard_map/ppermute | solution.py:420
  26.8 2.1 %right_side.1.right_ref = bf16[384,6144]{1,0:T(8,128)(2,1)S(1)} custom-call(bf16[3072,128]{1,0:T(8,128)(2,1)S(1)} %bitcast.6, bf16[3072,128]{1,0:T(8,128)(2,1)S(1)} %collective-permute-done.3.refs_1_, bf16[3072,128]{1,0:T(8,128)(2,1)S(1)} %collective-permute-done.2.refs_2_), custom_call_target="tpu_custom_call" | custom-call | flops 2000000000 | bytes 4000000 | tf_op jit(solution)/shard_map/right_side/pallas_call | solution.py:325
  28.9 3.1 %border_terms.1 = (bf16[4,64,6144]{2,1,0:T(8,128)(2,1)S(1)}, f32[3,10,4,64,128]{4,3,2,1,0:T(8,128)S(1)}, f32[3,10,4,64,128]{4,3,2,1,0:T(8,128)S(1)}, f32[16,32,128]{2,1,0:T(8,128)S(1)}, f32[16,32,128]{2,1,0:T(8,128)S(1)}) custom-call(bf16[4,64,6144]{2,1,0:T(8,128)(2,1)S(1)} %get-tuple-elem, ...), custom_call_target="tpu_custom_call", output_to_operand_aliasing={{0}: (0, {}), {1}: (1, {}), {2}: (2, {}), {3}: (5, {}), {4}... | custom-call | flops 6000000000 | bytes 6000000 | tf_op jit(solution)/shard_map/border_terms/pallas_call | solution.py:280
  32.0 1.9 %contract_near.1 = (f32[128,384]{1,0:T(8,128)S(1)}, f32[128,384]{1,0:T(8,128)S(1)}) custom-call(bf16[4,64,6144]{2,1,0:T(8,128)(2,1)S(1)} %get-tuple-element.40.w_ref, bf16[384,6144]{1,0:T(8,128)(2,1)S(1)} %right_side.1.right_ref), custom_call_target="tpu_custom_call" | custom-call | flops 1207959552 | bytes 4000000 | tf_op jit(solution)/shard_map/contract_near/pallas_call | solution.py:351
  34.0 0.9 %collective-permute-done.10.refs_0_ = bf16[1536,128]{1,0:T(8,128)(2,1)S(1)} collective-permute-done((bf16[1536,128]{1,0:T(8,128)(2,1)S(1)}, bf16[1536,128]{1,0:T(8,128)(2,1)S(1)}, u32[]{:S(2)}, u32[]{:S(2)}) %collective-permute-start.10) | collective-permute-done | bytes 393248 | tf_op jit(solution)/shard_map/ppermute | solution.py:420
  34.9 0.5 collective-permute-done.11.refs_1_
  35.4 1.4 %contract_far.1 = (f32[128,128]{1,0:T(8,128)S(1)}, f32[128,128]{1,0:T(8,128)S(1)}) custom-call(bf16[4,64,6144]{2,1,0:T(8,128)(2,1)S(1)} %get-tuple-element.40.w_ref, bf16[1536,128]{1,0:T(8,128)(2,1)S(1)} %collective-permute-done.10.refs_0_, bf16[1536,128]{1,0:T(8,128)(2,1)S(1)} %collective-permute-done.11.refs_1_), custom_call_target="tpu_custom_call" | custom-call | flops 402653184 | bytes 4000000 | tf_op jit(solution)/shard_map/contract_far/pallas_call | solution.py:369
  36.9 2.8 %collective-permute-start.7 = (bf16[128,384]{1,0:T(8,128)(2,1)S(1)}, bf16[128,384]{1,0:T(8,128)(2,1)S(1)}, u32[]{:S(2)}, u32[]{:S(2)}) collective-permute-start(bf16[128,384]{1,0:T(8,128)(2,1)S(1)} %add_convert_fusion.1), channel_id=1, source_target_pairs={{0,8},{4,12},{8,0},{12,4},{16,24},{20,28},{24,16},{28,20},{1,9},{5... | collective-permute-start | bytes 294920 | tf_op jit(solution)/shard_map/ppermute | solution.py:420
  40.1 2.4 %collective-permute-start.9 = (bf16[128,384]{1,0:T(8,128)(2,1)S(1)}, bf16[128,384]{1,0:T(8,128)(2,1)S(1)}, u32[]{:S(2)}, u32[]{:S(2)}) collective-permute-start(bf16[128,384]{1,0:T(8,128)(2,1)S(1)} %add_convert_fusion.1), channel_id=1, source_target_pairs={{0,12},{4,0},{8,4},{12,8},{16,28},{20,16},{24,20},{28,24},{1,13},{... | collective-permute-start | bytes 294920 | tf_op jit(solution)/shard_map/ppermute | solution.py:420
  42.6 0.6 collective-permute-start.14
  43.1 2.2 %collective-permute-start.15 = (bf16[128,128]{1,0:T(8,128)(2,1)S(1)}, bf16[128,128]{1,0:T(8,128)(2,1)S(1)}, u32[]{:S(2)}, u32[]{:S(2)}) collective-permute-start(bf16[128,128]{1,0:T(8,128)(2,1)S(1)} %add_convert_fusion.3), channel_id=1, source_target_pairs={{0,12},{4,0},{8,4},{12,8},{16,28},{20,16},{24,20},{28,24},{1,13},{... | collective-permute-start | bytes 98312 | tf_op jit(solution)/shard_map/ppermute | solution.py:420
  45.4 1.5 %collective-permute-done.13 = bf16[128,128]{1,0:T(8,128)(2,1)S(1)} collective-permute-done((bf16[128,128]{1,0:T(8,128)(2,1)S(1)}, bf16[128,128]{1,0:T(8,128)(2,1)S(1)}, u32[]{:S(2)}, u32[]{:S(2)}) %collective-permute-start.13) | collective-permute-done | bytes 32800 | tf_op jit(solution)/shard_map/ppermute | solution.py:420
  47.0 3.9 %collective-permute-start.16 = (bf16[128,512]{1,0:T(8,128)(2,1)S(1)}, bf16[128,512]{1,0:T(8,128)(2,1)S(1)}, u32[]{:S(2)}, u32[]{:S(2)}) collective-permute-start(bf16[128,512]{1,0:T(8,128)(2,1)S(1)} %pad_maximum_fusion), channel_id=1, source_target_pairs={{0,16},{4,20},{8,24},{12,28},{16,0},{20,4},{24,8},{28,12},{1,17},{... | collective-permute-start | bytes 393224 | tf_op jit(solution)/shard_map/ppermute | solution.py:420
  50.9 0.4 collective-permute-start.17
  51.3 1.9 %collective-permute-done.16 = bf16[128,512]{1,0:T(8,128)(2,1)S(1)} collective-permute-done((bf16[128,512]{1,0:T(8,128)(2,1)S(1)}, bf16[128,512]{1,0:T(8,128)(2,1)S(1)}, u32[]{:S(2)}, u32[]{:S(2)}) %collective-permute-start.16) | collective-permute-done | bytes 131104 | tf_op jit(solution)/shard_map/ppermute | solution.py:420
  53.3 2.4 %collective-permute-done.17 = bf16[128,512]{1,0:T(8,128)(2,1)S(1)} collective-permute-done((bf16[128,512]{1,0:T(8,128)(2,1)S(1)}, bf16[128,512]{1,0:T(8,128)(2,1)S(1)}, u32[]{:S(2)}, u32[]{:S(2)}) %collective-permute-start.17) | collective-permute-done | bytes 131104 | tf_op jit(solution)/shard_map/ppermute | solution.py:420
  55.7 1.8 %collective-permute-done.18 = bf16[128,512]{1,0:T(8,128)(2,1)S(1)} collective-permute-done((bf16[128,512]{1,0:T(8,128)(2,1)S(1)}, bf16[128,512]{1,0:T(8,128)(2,1)S(1)}, u32[]{:S(2)}, u32[]{:S(2)}) %collective-permute-start.18) | collective-permute-done | bytes 131104 | tf_op jit(solution)/shard_map/ppermute | solution.py:420
  57.5 2.7 %collective-permute-start.19 = (f32[128,512]{1,0:T(8,128)S(1)}, f32[128,512]{1,0:T(8,128)S(1)}, u32[]{:S(2)}, u32[]{:S(2)}) collective-permute-start(f32[128,512]{1,0:T(8,128)S(1)} %add_add_fusion.mine_ref), channel_id=1, source_target_pairs={{0,32},{32,0},{64,96},{96,64},{1,33},{33,1},{65,97},{97,65},{2,34}... | collective-permute-start | bytes 786440 | tf_op jit(solution)/shard_map/ppermute | solution.py:420
  60.2 1.2 %collective-permute-done.19.other_ref = f32[128,512]{1,0:T(8,128)S(1)} collective-permute-done((f32[128,512]{1,0:T(8,128)S(1)}, f32[128,512]{1,0:T(8,128)S(1)}, u32[]{:S(2)}, u32[]{:S(2)}) %collective-permute-start.19) | collective-permute-done | bytes 262176 | tf_op jit(solution)/shard_map/ppermute | solution.py:420
  61.4 1.8 %finish.1 = f32[4,2,64,256]{3,2,1,0:T(8,128)} custom-call(s32[3]{0:T(128)S(1)} %copy-done, f32[128,512]{1,0:T(8,128)S(1)} %add_add_fusion.mine_ref, f32[128,512]{1,0:T(8,128)S(1)} %collective-permute-done.19.other_ref), custom_call_target="tpu_custom_call" | custom-call | flops 200000 | bytes 1000000 | tf_op jit(solution)/shard_map/finish/pallas_call | solution.py:407
  (35 shorter events, 0.9 us)
Async XLA Ops:
  0.0 13.3 %copy-start.5 = (s32[3]{0:T(128)S(1)}, s32[3]{0:T(128)}, u32[]{:S(2)}) copy-start(s32[3]{0:T(128)} %momentum_ref.1) | copy-start | bytes 40
  0.0 20.9 %collective-permute-start.2 = (bf16[3072,128]{1,0:T(8,128)(2,1)}, bf16[3072,128]{1,0:T(8,128)(2,1)S(1)}, u32[]{:S(2)}, u32[]{:S(2)}) collective-permute-start(bf16[3072,128]{1,0:T(8,128)(2,1)} %bitcast.2), channel_id=1, source_target_pairs={{0,1},{1,2},{2,3},{3,0},{4,5},{5,6},{6,7},{7,4},{8,9},{9,10},{10,1... | collective-permute-start | bytes 2359304 | tf_op jit(solution)/shard_map/ppermute | solution.py:420
  2.1 18.8 %collective-permute-start.3 = (bf16[3072,128]{1,0:T(8,128)(2,1)}, bf16[3072,128]{1,0:T(8,128)(2,1)S(1)}, u32[]{:S(2)}, u32[]{:S(2)}) collective-permute-start(bf16[3072,128]{1,0:T(8,128)(2,1)} %bitcast.3), channel_id=1, source_target_pairs={{0,3},{1,0},{2,1},{3,2},{4,7},{5,4},{6,5},{7,6},{8,11},{9,8},{10,9... | collective-permute-start | bytes 2359304 | tf_op jit(solution)/shard_map/ppermute | solution.py:420
  3.6 1.2 %copy-start.1 = (bf16[64,3,8,2,128]{4,3,2,1,0:T(2,128)(2,1)S(1)}, bf16[64,3,8,2,128]{4,3,2,1,0:T(2,128)(2,1)}, u32[]{:S(2)}) copy-start(bf16[64,3,8,2,128]{4,3,2,1,0:T(2,128)(2,1)} %param.4) | copy-start | bytes 2359300
  4.8 0.9 %copy-start.3 = (bf16[3,3,3,8,2,128]{5,4,3,2,1,0:T(2,128)(2,1)S(1)}, bf16[3,3,3,8,2,128]{5,4,3,2,1,0:T(2,128)(2,1)}, u32[]{:S(2)}) copy-start(bf16[3,3,3,8,2,128]{5,4,3,2,1,0:T(2,128)(2,1)} %param.5) | copy-start | bytes 331780
  5.7 7.6 %copy-start.2 = (bf16[64,3,8,2,128]{4,3,2,1,0:T(2,128)(2,1)S(1)}, bf16[64,3,8,2,128]{4,3,2,1,0:T(2,128)(2,1)}, u32[]{:S(2)}) copy-start(bf16[64,3,8,2,128]{4,3,2,1,0:T(2,128)(2,1)} %param.4) | copy-start | bytes 2359300
  5.7 7.6 %copy-start.4 = (bf16[3,3,3,8,2,128]{5,4,3,2,1,0:T(2,128)(2,1)S(1)}, bf16[3,3,3,8,2,128]{5,4,3,2,1,0:T(2,128)(2,1)}, u32[]{:S(2)}) copy-start(bf16[3,3,3,8,2,128]{5,4,3,2,1,0:T(2,128)(2,1)} %param.5) | copy-start | bytes 331780
  6.3 14.6 %collective-permute-start.4 = (bf16[6,64,128]{2,1,0:T(8,128)(2,1)S(1)}, bf16[6,64,128]{2,1,0:T(8,128)(2,1)S(1)}, u32[]{:S(2)}, u32[]{:S(2)}) collective-permute-start(bf16[6,64,128]{2,1,0:T(8,128)(2,1)S(1)} %get-tuple-element.37), channel_id=1, source_target_pairs={{0,96},{32,0},{64,32},{96,64},{1,97},{33,1},{65,33},{97,65},{2,98}... | collective-permute-start | bytes 294920 | tf_op jit(solution)/shard_map/ppermute | solution.py:420
  7.4 21.5 %collective-permute-start.1 = (bf16[26,64,128]{2,1,0:T(8,128)(2,1)S(1)}, bf16[26,64,128]{2,1,0:T(8,128)(2,1)S(1)}, u32[]{:S(2)}, u32[]{:S(2)}) collective-permute-start(bf16[26,64,128]{2,1,0:T(8,128)(2,1)S(1)} %get-tuple-element.34), channel_id=1, source_target_pairs={{0,4},{4,8},{8,12},{12,16},{16,20},{20,24},{24,28},{28,0},{1,5},{5... | collective-permute-start | bytes 1277960 | tf_op jit(solution)/shard_map/ppermute | solution.py:420
  8.7 20.2 %collective-permute-start = (bf16[24,64,128]{2,1,0:T(8,128)(2,1)S(1)}, bf16[24,64,128]{2,1,0:T(8,128)(2,1)S(1)}, u32[]{:S(2)}, u32[]{:S(2)}) collective-permute-start(bf16[24,64,128]{2,1,0:T(8,128)(2,1)S(1)} %get-tuple-element.33), channel_id=1, source_target_pairs={{0,28},{4,0},{8,4},{12,8},{16,12},{20,16},{24,20},{28,24},{1,29},{... | collective-permute-start | bytes 1179656 | tf_op jit(solution)/shard_map/ppermute | solution.py:420
  20.9 8.0 %collective-permute-start.5 = (bf16[7,64,128]{2,1,0:T(8,128)(2,1)S(1)}, bf16[7,64,128]{2,1,0:T(8,128)(2,1)S(1)}, u32[]{:S(2)}, u32[]{:S(2)}) collective-permute-start(bf16[7,64,128]{2,1,0:T(8,128)(2,1)S(1)} %get-tuple-element.39), channel_id=1, source_target_pairs={{0,32},{32,64},{64,96},{96,0},{1,33},{33,65},{65,97},{97,1},{2,34}... | collective-permute-start | bytes 344072 | tf_op jit(solution)/shard_map/ppermute | solution.py:420
  23.9 11.1 %collective-permute-start.10 = (bf16[1536,128]{1,0:T(8,128)(2,1)S(1)}, bf16[1536,128]{1,0:T(8,128)(2,1)S(1)}, u32[]{:S(2)}, u32[]{:S(2)}) collective-permute-start(bf16[1536,128]{1,0:T(8,128)(2,1)S(1)} %slice.6), channel_id=1, source_target_pairs={{0,1},{1,2},{2,3},{3,0},{4,5},{5,6},{6,7},{7,4},{8,9},{9,10},{10,1... | collective-permute-start | bytes 1179656 | tf_op jit(solution)/shard_map/ppermute | solution.py:420
  25.2 10.1 %collective-permute-start.11 = (bf16[1536,128]{1,0:T(8,128)(2,1)S(1)}, bf16[1536,128]{1,0:T(8,128)(2,1)S(1)}, u32[]{:S(2)}, u32[]{:S(2)}) collective-permute-start(bf16[1536,128]{1,0:T(8,128)(2,1)S(1)} %slice.7), channel_id=1, source_target_pairs={{0,3},{1,0},{2,1},{3,2},{4,7},{5,4},{6,5},{7,6},{8,11},{9,8},{10,9... | collective-permute-start | bytes 1179656 | tf_op jit(solution)/shard_map/ppermute | solution.py:420
  33.9 27.5 %copy-start = (s32[3]{0:T(128)S(1)}, s32[3]{0:T(128)}, u32[]{:S(2)}) copy-start(s32[3]{0:T(128)} %dirs_ref.1) | copy-start | bytes 40
  33.9 3.0 %collective-permute-start.6 = (f32[128,384]{1,0:T(8,128)S(1)}, f32[128,384]{1,0:T(8,128)S(1)}, u32[]{:S(2)}, u32[]{:S(2)}) collective-permute-start(f32[128,384]{1,0:T(8,128)S(1)} %get-tuple-element.44), channel_id=1, source_target_pairs={{0,32},{32,0},{64,96},{96,64},{1,33},{33,1},{65,97},{97,65},{2,34}... | collective-permute-start | bytes 589832 | tf_op jit(solution)/shard_map/ppermute | solution.py:420
  36.8 5.6 %collective-permute-start.12 = (f32[128,128]{1,0:T(8,128)S(1)}, f32[128,128]{1,0:T(8,128)S(1)}, u32[]{:S(2)}, u32[]{:S(2)}) collective-permute-start(f32[128,128]{1,0:T(8,128)S(1)} %get-tuple-element.46), channel_id=1, source_target_pairs={{0,32},{32,0},{64,96},{96,64},{1,33},{33,1},{65,97},{97,65},{2,34}... | collective-permute-start | bytes 196616 | tf_op jit(solution)/shard_map/ppermute | solution.py:420
  36.9 6.2 %collective-permute-start.7 = (bf16[128,384]{1,0:T(8,128)(2,1)S(1)}, bf16[128,384]{1,0:T(8,128)(2,1)S(1)}, u32[]{:S(2)}, u32[]{:S(2)}) collective-permute-start(bf16[128,384]{1,0:T(8,128)(2,1)S(1)} %add_convert_fusion.1), channel_id=1, source_target_pairs={{0,8},{4,12},{8,0},{12,4},{16,24},{20,28},{24,16},{28,20},{1,9},{5... | collective-permute-start | bytes 294920 | tf_op jit(solution)/shard_map/ppermute | solution.py:420
  39.8 5.5 %collective-permute-start.8 = (bf16[128,384]{1,0:T(8,128)(2,1)S(1)}, bf16[128,384]{1,0:T(8,128)(2,1)S(1)}, u32[]{:S(2)}, u32[]{:S(2)}) collective-permute-start(bf16[128,384]{1,0:T(8,128)(2,1)S(1)} %add_convert_fusion.1), channel_id=1, source_target_pairs={{0,4},{4,8},{8,12},{12,0},{16,20},{20,24},{24,28},{28,16},{1,5},{5... | collective-permute-start | bytes 294920 | tf_op jit(solution)/shard_map/ppermute | solution.py:420
  40.1 5.2 %collective-permute-start.9 = (bf16[128,384]{1,0:T(8,128)(2,1)S(1)}, bf16[128,384]{1,0:T(8,128)(2,1)S(1)}, u32[]{:S(2)}, u32[]{:S(2)}) collective-permute-start(bf16[128,384]{1,0:T(8,128)(2,1)S(1)} %add_convert_fusion.1), channel_id=1, source_target_pairs={{0,12},{4,0},{8,4},{12,8},{16,28},{20,16},{24,20},{28,24},{1,13},{... | collective-permute-start | bytes 294920 | tf_op jit(solution)/shard_map/ppermute | solution.py:420
  42.5 4.5 %collective-permute-start.13 = (bf16[128,128]{1,0:T(8,128)(2,1)S(1)}, bf16[128,128]{1,0:T(8,128)(2,1)S(1)}, u32[]{:S(2)}, u32[]{:S(2)}) collective-permute-start(bf16[128,128]{1,0:T(8,128)(2,1)S(1)} %add_convert_fusion.3), channel_id=1, source_target_pairs={{0,8},{4,12},{8,0},{12,4},{16,24},{20,28},{24,16},{28,20},{1,9},{5... | collective-permute-start | bytes 98312 | tf_op jit(solution)/shard_map/ppermute | solution.py:420
  42.6 4.4 %collective-permute-start.14 = (bf16[128,128]{1,0:T(8,128)(2,1)S(1)}, bf16[128,128]{1,0:T(8,128)(2,1)S(1)}, u32[]{:S(2)}, u32[]{:S(2)}) collective-permute-start(bf16[128,128]{1,0:T(8,128)(2,1)S(1)} %add_convert_fusion.3), channel_id=1, source_target_pairs={{0,4},{4,8},{8,12},{12,0},{16,20},{20,24},{24,28},{28,16},{1,5},{5... | collective-permute-start | bytes 98312 | tf_op jit(solution)/shard_map/ppermute | solution.py:420
  43.1 3.8 %collective-permute-start.15 = (bf16[128,128]{1,0:T(8,128)(2,1)S(1)}, bf16[128,128]{1,0:T(8,128)(2,1)S(1)}, u32[]{:S(2)}, u32[]{:S(2)}) collective-permute-start(bf16[128,128]{1,0:T(8,128)(2,1)S(1)} %add_convert_fusion.3), channel_id=1, source_target_pairs={{0,12},{4,0},{8,4},{12,8},{16,28},{20,16},{24,20},{28,24},{1,13},{... | collective-permute-start | bytes 98312 | tf_op jit(solution)/shard_map/ppermute | solution.py:420
  47.0 6.3 %collective-permute-start.16 = (bf16[128,512]{1,0:T(8,128)(2,1)S(1)}, bf16[128,512]{1,0:T(8,128)(2,1)S(1)}, u32[]{:S(2)}, u32[]{:S(2)}) collective-permute-start(bf16[128,512]{1,0:T(8,128)(2,1)S(1)} %pad_maximum_fusion), channel_id=1, source_target_pairs={{0,16},{4,20},{8,24},{12,28},{16,0},{20,4},{24,8},{28,12},{1,17},{... | collective-permute-start | bytes 393224 | tf_op jit(solution)/shard_map/ppermute | solution.py:420
  50.9 4.7 %collective-permute-start.17 = (bf16[128,512]{1,0:T(8,128)(2,1)S(1)}, bf16[128,512]{1,0:T(8,128)(2,1)S(1)}, u32[]{:S(2)}, u32[]{:S(2)}) collective-permute-start(bf16[128,512]{1,0:T(8,128)(2,1)S(1)} %pad_maximum_fusion), channel_id=1, source_target_pairs={{0,64},{32,96},{64,0},{96,32},{1,65},{33,97},{65,1},{97,33},{2,66}... | collective-permute-start | bytes 393224 | tf_op jit(solution)/shard_map/ppermute | solution.py:420
  51.3 6.1 %collective-permute-start.18 = (bf16[128,512]{1,0:T(8,128)(2,1)S(1)}, bf16[128,512]{1,0:T(8,128)(2,1)S(1)}, u32[]{:S(2)}, u32[]{:S(2)}) collective-permute-start(bf16[128,512]{1,0:T(8,128)(2,1)S(1)} %pad_maximum_fusion), channel_id=1, source_target_pairs={{0,80},{4,84},{8,88},{12,92},{16,64},{20,68},{24,72},{28,76},{32,1... | collective-permute-start | bytes 393224 | tf_op jit(solution)/shard_map/ppermute | solution.py:420
  57.5 3.9 %collective-permute-start.19 = (f32[128,512]{1,0:T(8,128)S(1)}, f32[128,512]{1,0:T(8,128)S(1)}, u32[]{:S(2)}, u32[]{:S(2)}) collective-permute-start(f32[128,512]{1,0:T(8,128)S(1)} %add_add_fusion.mine_ref), channel_id=1, source_target_pairs={{0,32},{32,0},{64,96},{96,64},{1,33},{33,1},{65,97},{97,65},{2,34}... | collective-permute-start | bytes 786440 | tf_op jit(solution)/shard_map/ppermute | solution.py:420

commit v3 on v2

--- a/solution.py
+++ b/solution.py
@@ -435,9 +435,8 @@
     y0, y1, z0, z1 = prepare(rows, link_rows)
     yp = permuted(y0, "gy", lambda s: (s - 1) % 8)
     ym = permuted(y1, "gy", lambda s: (s + 1) % 8)
-    prev, next_, zz = lax.optimization_barrier((prev, next_, z1))
     zp = permuted(z0, "gz", lambda s: (s - 1) % 4)
-    z1, zp = lax.optimization_barrier((zz, zp))
+    z1, zp = lax.optimization_barrier((z1, zp))
     zm = permuted(z1, "gz", lambda s: (s + 1) % 4)
     partial = local_terms(momentum, rows, link_rows)
 
@@ -445,18 +444,19 @@
     far_high = permuted(next_[mid:], "vec", lambda s: (s - 1) % 4)
 
     right = right_side([rows, next_, prev])
+    yp, right = lax.optimization_barrier((yp, right))
     w = border_terms(*partial, yp, ym, zp, zm)
 
     mate = lambda v: permuted(v, "gz", lambda s: s ^ 1)
     along_x = lambda v, step: permuted(v, "gy", lambda s: (s // 4) * 4 + (s + step) % 4)
 
-    def row_sum(keep, send):
-        chip = (keep + mate(send)).astype(BF16)
-        return four_sum(chip, along_x(chip, 2), along_x(chip, 1), along_x(chip, 3)).astype(BF16)
-
-    near = row_sum(*contract_near(w, right))
-    far = row_sum(*contract_far(w, [far_low, far_high]))
-    row = jnp.concatenate([near, far], 1)
+    def chip_sum(keep, send):
+        return (keep + mate(send)).astype(BF16)
+
+    near = chip_sum(*contract_near(w, right))
+    far = chip_sum(*contract_far(w, [far_low, far_high]))
+    chip = jnp.concatenate([near, far], 1)
+    row = four_sum(chip, along_x(chip, 2), along_x(chip, 1), along_x(chip, 3)).astype(BF16)
     across = permuted(row, "gy", lambda s: s ^ 4)
     side = permuted(row, "gz", lambda s: s ^ 2)
     both = permuted(row, ("gz", "gy"), lambda s: s ^ 20)

time: 63.3 us -> 61.8 us (0.976)
  starting transfers between devices: 32 us -> 27 us
  waiting for transfers between devices: 13.1 us -> 16.6 us
    ppermute x20 -> x17, starting transfers between devices: 32 us -> 27 us  [permuted(): lax.ppermute(value, axis, [(source, target(source)) for source in range(s...]
    ppermute x20 -> x17, waiting for transfers between devices: 13.1 us -> 16.6 us  [permuted(): lax.ppermute(value, axis, [(source, target(source)) for source in range(s...]
  transfers between devices with their start and end apart: 20 -> 17, of which waited for: 8 -> 10; matrix products, arithmetic and copies ran while one was open for 0% -> 0% of each run, Pallas kernels for 22% -> 23%
where the time goes in v3:
time: 61.8 us; the launch traced here: 61.6 us
  starting transfers between devices  27 us (44%)
  waiting for transfers between devices  16.6 us (27%)
  Pallas kernels  15.7 us (25%)
  local copies, waits for them, and re-layouts  2.13 us (3%)
    ppermute x17, starting transfers between devices, permuted(): lax.ppermute(value, axis, [(source, target(source)) for source in range(s...  27 us
    ppermute x17, waiting for transfers between devices, permuted(): lax.ppermute(value, axis, [(source, target(source)) for source in range(s...  16.6 us
    pallas_call x1, Pallas kernels, local_terms(): pl.pallas_call(local_kernel, out_shape=(shape((4, NV, KDIM), BF16),) + (s...  4.85 us
    pallas_call x1, Pallas kernels, border_terms(): pl.pallas_call(border_kernel, out_shape=(shape((4, NV, KDIM), BF16),) + (...  3.06 us
    pallas_call x1, Pallas kernels, right_side(): pl.pallas_call(functools.partial(right_kernel, counts), out_shape=shape((...  2.15 us
    unnamed x12, local copies, waits for them, and re-layouts  2.08 us
    pallas_call x1, Pallas kernels, contract_near(): pl.pallas_call(near_kernel, out_shape=(out, out), in_specs=[VMEM] * 2, ou...  1.87 us
    pallas_call x1, Pallas kernels, finish(): pl.pallas_call(functools.partial(finish_kernel, scale), out_shape=shape((...  1.76 us
  transfers between devices with their start and end apart: 17, of which 10 were waited for; matrix products, arithmetic and copies ran while one was open for 0% of the time, Pallas kernels for 23%

profile of v3, /device:TPU:1, one launch (start us, length us, event | category | flops | bytes accessed | tf_op | source)
XLA Modules:
  0.0 61.6 jit_solution(10404087292445583814)
XLA Ops:
  0.0 2.1 %collective-permute-start.2 = (bf16[3072,128]{1,0:T(8,128)(2,1)}, bf16[3072,128]{1,0:T(8,128)(2,1)S(1)}, u32[]{:S(2)}, u32[]{:S(2)}) collective-permute-start(bf16[3072,128]{1,0:T(8,128)(2,1)} %bitcast.2), channel_id=1, source_target_pairs={{0,1},{1,2},{2,3},{3,0},{4,5},{5,6},{6,7},{7,4},{8,9},{9,10},{10,1... | collective-permute-start | bytes 2359304 | tf_op jit(solution)/shard_map/ppermute | solution.py:420
  2.1 1.5 %collective-permute-start.1 = (bf16[3072,128]{1,0:T(8,128)(2,1)}, bf16[3072,128]{1,0:T(8,128)(2,1)S(1)}, u32[]{:S(2)}, u32[]{:S(2)}) collective-permute-start(bf16[3072,128]{1,0:T(8,128)(2,1)} %bitcast.3), channel_id=1, source_target_pairs={{0,3},{1,0},{2,1},{3,2},{4,7},{5,4},{6,5},{7,6},{8,11},{9,8},{10,9... | collective-permute-start | bytes 2359304 | tf_op jit(solution)/shard_map/ppermute | solution.py:420
  3.6 1.2 %copy-done.1 = bf16[64,3,8,2,128]{4,3,2,1,0:T(2,128)(2,1)S(1)} copy-done((bf16[64,3,8,2,128]{4,3,2,1,0:T(2,128)(2,1)S(1)}, bf16[64,3,8,2,128]{4,3,2,1,0:T(2,128)(2,1)}, u32[]{:S(2)}) %copy-start.1) | copy-done | bytes 786456
  4.8 0.9 %copy-done.3 = bf16[3,3,3,8,2,128]{5,4,3,2,1,0:T(2,128)(2,1)S(1)} copy-done((bf16[3,3,3,8,2,128]{5,4,3,2,1,0:T(2,128)(2,1)S(1)}, bf16[3,3,3,8,2,128]{5,4,3,2,1,0:T(2,128)(2,1)}, u32[]{:S(2)}) %copy-start.3) | copy-done | bytes 110616
  5.7 0.6 prepare.1
  6.3 1.1 %collective-permute-start.4 = (bf16[6,64,128]{2,1,0:T(8,128)(2,1)S(1)}, bf16[6,64,128]{2,1,0:T(8,128)(2,1)S(1)}, u32[]{:S(2)}, u32[]{:S(2)}) collective-permute-start(bf16[6,64,128]{2,1,0:T(8,128)(2,1)S(1)} %get-tuple-element.36), channel_id=1, source_target_pairs={{0,96},{32,0},{64,32},{96,64},{1,97},{33,1},{65,33},{97,65},{2,98}... | collective-permute-start | bytes 294920 | tf_op jit(solution)/shard_map/ppermute | solution.py:420
  7.4 5.9 %collective-permute-start = (bf16[24,64,128]{2,1,0:T(8,128)(2,1)S(1)}, bf16[24,64,128]{2,1,0:T(8,128)(2,1)S(1)}, u32[]{:S(2)}, u32[]{:S(2)}) collective-permute-start(bf16[24,64,128]{2,1,0:T(8,128)(2,1)S(1)} %get-tuple-element.32), channel_id=1, source_target_pairs={{0,28},{4,0},{8,4},{12,8},{16,12},{20,16},{24,20},{28,24},{1,29},{... | collective-permute-start | bytes 1179656 | tf_op jit(solution)/shard_map/ppermute | solution.py:420
  13.3 4.8 %local_terms.1 = (bf16[4,64,6144]{2,1,0:T(8,128)(2,1)S(1)}, f32[3,10,4,64,128]{4,3,2,1,0:T(8,128)S(1)}, f32[3,10,4,64,128]{4,3,2,1,0:T(8,128)S(1)}, f32[16,32,12...) custom-call(s32[3]{0:T(128)S(1)} %copy-done.5, ...), custom_call_target="tpu_custom_call" | custom-call | flops 6000000000 | bytes 6000000 | tf_op jit(solution)/shard_map/local_terms/pallas_call | solution.py:205
  18.1 1.1 %collective-permute-start.5 = (bf16[7,64,128]{2,1,0:T(8,128)(2,1)S(1)}, bf16[7,64,128]{2,1,0:T(8,128)(2,1)S(1)}, u32[]{:S(2)}, u32[]{:S(2)}) collective-permute-start(bf16[7,64,128]{2,1,0:T(8,128)(2,1)S(1)} %get-tuple-element.38), channel_id=1, source_target_pairs={{0,32},{32,64},{64,96},{96,0},{1,33},{33,65},{65,97},{97,1},{2,34}... | collective-permute-start | bytes 344072 | tf_op jit(solution)/shard_map/ppermute | solution.py:420
  19.2 1.7 %collective-permute-done.2.refs_2_ = bf16[3072,128]{1,0:T(8,128)(2,1)S(1)} collective-permute-done((bf16[3072,128]{1,0:T(8,128)(2,1)}, bf16[3072,128]{1,0:T(8,128)(2,1)S(1)}, u32[]{:S(2)}, u32[]{:S(2)}) %collective-permute-start.2) | collective-permute-done | bytes 786464 | tf_op jit(solution)/shard_map/ppermute | solution.py:420
  21.0 2.7 %collective-permute-start.8 = (bf16[1536,128]{1,0:T(8,128)(2,1)S(1)}, bf16[1536,128]{1,0:T(8,128)(2,1)S(1)}, u32[]{:S(2)}, u32[]{:S(2)}) collective-permute-start(bf16[1536,128]{1,0:T(8,128)(2,1)S(1)} %slice.9), channel_id=1, source_target_pairs={{0,3},{1,0},{2,1},{3,2},{4,7},{5,4},{6,5},{7,6},{8,11},{9,8},{10,9... | collective-permute-start | bytes 1179656 | tf_op jit(solution)/shard_map/ppermute | solution.py:420
  23.8 2.1 %right_side.1.right_ref = bf16[384,6144]{1,0:T(8,128)(2,1)S(1)} custom-call(bf16[3072,128]{1,0:T(8,128)(2,1)S(1)} %bitcast.6, bf16[3072,128]{1,0:T(8,128)(2,1)S(1)} %collective-permute-done.1.refs_1_, bf16[3072,128]{1,0:T(8,128)(2,1)S(1)} %collective-permute-done.2.refs_2_), custom_call_target="tpu_custom_call" | custom-call | flops 2000000000 | bytes 4000000 | tf_op jit(solution)/shard_map/right_side/pallas_call | solution.py:325
  25.9 1.4 %collective-permute-done.3.ym_ref = bf16[26,64,128]{2,1,0:T(8,128)(2,1)S(1)} collective-permute-done((bf16[26,64,128]{2,1,0:T(8,128)(2,1)S(1)}, bf16[26,64,128]{2,1,0:T(8,128)(2,1)S(1)}, u32[]{:S(2)}, u32[]{:S(2)}) %collective-permute-start.3) | collective-permute-done | bytes 426016 | tf_op jit(solution)/shard_map/ppermute | solution.py:420
  27.3 3.1 %border_terms.1 = (bf16[4,64,6144]{2,1,0:T(8,128)(2,1)S(1)}, f32[3,10,4,64,128]{4,3,2,1,0:T(8,128)S(1)}, f32[3,10,4,64,128]{4,3,2,1,0:T(8,128)S(1)}, f32[16,32,128]{2,1,0:T(8,128)S(1)}, f32[16,32,128]{2,1,0:T(8,128)S(1)}) custom-call(bf16[4,64,6144]{2,1,0:T(8,128)(2,1)S(1)} %get-tuple-elem, ...), custom_call_target="tpu_custom_call", output_to_operand_aliasing={{0}: (0, {}), {1}: (1, {}), {2}: (2, {}), {3}: (5, {}), {4}... | custom-call | flops 6000000000 | bytes 6000000 | tf_op jit(solution)/shard_map/border_terms/pallas_call | solution.py:280
  30.4 1.9 %contract_near.1 = (f32[128,384]{1,0:T(8,128)S(1)}, f32[128,384]{1,0:T(8,128)S(1)}) custom-call(bf16[4,64,6144]{2,1,0:T(8,128)(2,1)S(1)} %get-tuple-element.39.w_ref, bf16[384,6144]{1,0:T(8,128)(2,1)S(1)} %right_side.1.right_ref), custom_call_target="tpu_custom_call" | custom-call | flops 1207959552 | bytes 4000000 | tf_op jit(solution)/shard_map/contract_near/pallas_call | solution.py:351
  32.3 2.0 %collective-permute-start.6 = (f32[128,384]{1,0:T(8,128)S(1)}, f32[128,384]{1,0:T(8,128)S(1)}, u32[]{:S(2)}, u32[]{:S(2)}) collective-permute-start(f32[128,384]{1,0:T(8,128)S(1)} %get-tuple-element.42), channel_id=1, source_target_pairs={{0,32},{32,0},{64,96},{96,64},{1,33},{33,1},{65,97},{97,65},{2,34}... | collective-permute-start | bytes 589832 | tf_op jit(solution)/shard_map/ppermute | solution.py:420
  34.2 1.4 %contract_far.1 = (f32[128,128]{1,0:T(8,128)S(1)}, f32[128,128]{1,0:T(8,128)S(1)}) custom-call(bf16[4,64,6144]{2,1,0:T(8,128)(2,1)S(1)} %get-tuple-element.39.w_ref, bf16[1536,128]{1,0:T(8,128)(2,1)S(1)} %collective-permute-done.7.refs_0_, bf16[1536,128]{1,0:T(8,128)(2,1)S(1)} %collective-permute-done.8.refs_1_), custom_call_target="tpu_custom_call" | custom-call | flops 402653184 | bytes 4000000 | tf_op jit(solution)/shard_map/contract_far/pallas_call | solution.py:369
  35.8 1.2 %collective-permute-done.9 = f32[128,128]{1,0:T(8,128)S(1)} collective-permute-done((f32[128,128]{1,0:T(8,128)S(1)}, f32[128,128]{1,0:T(8,128)S(1)}, u32[]{:S(2)}, u32[]{:S(2)}) %collective-permute-start.9) | collective-permute-done | bytes 65568 | tf_op jit(solution)/shard_map/ppermute | solution.py:420
  37.0 0.3 collective-permute-start.11
  37.4 2.4 %collective-permute-start.10 = (bf16[128,512]{1,0:T(8,128)(2,1)S(1)}, bf16[128,512]{1,0:T(8,128)(2,1)S(1)}, u32[]{:S(2)}, u32[]{:S(2)}) collective-permute-start(bf16[128,512]{1,0:T(8,128)(2,1)S(1)} %pad_maximum_fusion), channel_id=1, source_target_pairs={{0,8},{4,12},{8,0},{12,4},{16,24},{20,28},{24,16},{28,20},{1,9},{5... | collective-permute-start | bytes 393224 | tf_op jit(solution)/shard_map/ppermute | solution.py:420
  39.8 1.2 %collective-permute-start.12 = (bf16[128,512]{1,0:T(8,128)(2,1)S(1)}, bf16[128,512]{1,0:T(8,128)(2,1)S(1)}, u32[]{:S(2)}, u32[]{:S(2)}) collective-permute-start(bf16[128,512]{1,0:T(8,128)(2,1)S(1)} %pad_maximum_fusion), channel_id=1, source_target_pairs={{0,12},{4,0},{8,4},{12,8},{16,28},{20,16},{24,20},{28,24},{1,13},{... | collective-permute-start | bytes 393224 | tf_op jit(solution)/shard_map/ppermute | solution.py:420
  41.0 2.5 %collective-permute-done.11 = bf16[128,512]{1,0:T(8,128)(2,1)S(1)} collective-permute-done((bf16[128,512]{1,0:T(8,128)(2,1)S(1)}, bf16[128,512]{1,0:T(8,128)(2,1)S(1)}, u32[]{:S(2)}, u32[]{:S(2)}) %collective-permute-start.11) | collective-permute-done | bytes 131104 | tf_op jit(solution)/shard_map/ppermute | solution.py:420
  43.4 2.4 %collective-permute-done.10 = bf16[128,512]{1,0:T(8,128)(2,1)S(1)} collective-permute-done((bf16[128,512]{1,0:T(8,128)(2,1)S(1)}, bf16[128,512]{1,0:T(8,128)(2,1)S(1)}, u32[]{:S(2)}, u32[]{:S(2)}) %collective-permute-start.10) | collective-permute-done | bytes 131104 | tf_op jit(solution)/shard_map/ppermute | solution.py:420
  45.9 0.4 collective-permute-done.12
  46.4 3.4 %collective-permute-start.15 = (bf16[128,512]{1,0:T(8,128)(2,1)S(1)}, bf16[128,512]{1,0:T(8,128)(2,1)S(1)}, u32[]{:S(2)}, u32[]{:S(2)}) collective-permute-start(bf16[128,512]{1,0:T(8,128)(2,1)S(1)} %add_convert_fusion), channel_id=1, source_target_pairs={{0,80},{4,84},{8,88},{12,92},{16,64},{20,68},{24,72},{28,76},{32,1... | collective-permute-start | bytes 393224 | tf_op jit(solution)/shard_map/ppermute | solution.py:420
  49.8 1.3 %collective-permute-start.13 = (bf16[128,512]{1,0:T(8,128)(2,1)S(1)}, bf16[128,512]{1,0:T(8,128)(2,1)S(1)}, u32[]{:S(2)}, u32[]{:S(2)}) collective-permute-start(bf16[128,512]{1,0:T(8,128)(2,1)S(1)} %add_convert_fusion), channel_id=1, source_target_pairs={{0,16},{4,20},{8,24},{12,28},{16,0},{20,4},{24,8},{28,12},{1,17},{... | collective-permute-start | bytes 393224 | tf_op jit(solution)/shard_map/ppermute | solution.py:420
  51.1 1.1 %collective-permute-done.15 = bf16[128,512]{1,0:T(8,128)(2,1)S(1)} collective-permute-done((bf16[128,512]{1,0:T(8,128)(2,1)S(1)}, bf16[128,512]{1,0:T(8,128)(2,1)S(1)}, u32[]{:S(2)}, u32[]{:S(2)}) %collective-permute-start.15) | collective-permute-done | bytes 131104 | tf_op jit(solution)/shard_map/ppermute | solution.py:420
  52.2 1.7 %collective-permute-done.14 = bf16[128,512]{1,0:T(8,128)(2,1)S(1)} collective-permute-done((bf16[128,512]{1,0:T(8,128)(2,1)S(1)}, bf16[128,512]{1,0:T(8,128)(2,1)S(1)}, u32[]{:S(2)}, u32[]{:S(2)}) %collective-permute-start.14) | collective-permute-done | bytes 131104 | tf_op jit(solution)/shard_map/ppermute | solution.py:420
  53.9 3.0 %collective-permute-done.13 = bf16[128,512]{1,0:T(8,128)(2,1)S(1)} collective-permute-done((bf16[128,512]{1,0:T(8,128)(2,1)S(1)}, bf16[128,512]{1,0:T(8,128)(2,1)S(1)}, u32[]{:S(2)}, u32[]{:S(2)}) %collective-permute-start.13) | collective-permute-done | bytes 131104 | tf_op jit(solution)/shard_map/ppermute | solution.py:420
  56.9 1.8 %collective-permute-start.16 = (f32[128,512]{1,0:T(8,128)S(1)}, f32[128,512]{1,0:T(8,128)S(1)}, u32[]{:S(2)}, u32[]{:S(2)}) collective-permute-start(f32[128,512]{1,0:T(8,128)S(1)} %add_add_fusion.mine_ref), channel_id=1, source_target_pairs={{0,32},{32,0},{64,96},{96,64},{1,33},{33,1},{65,97},{97,65},{2,34}... | collective-permute-start | bytes 786440 | tf_op jit(solution)/shard_map/ppermute | solution.py:420
  58.7 1.2 %collective-permute-done.16.other_ref = f32[128,512]{1,0:T(8,128)S(1)} collective-permute-done((f32[128,512]{1,0:T(8,128)S(1)}, f32[128,512]{1,0:T(8,128)S(1)}, u32[]{:S(2)}, u32[]{:S(2)}) %collective-permute-start.16) | collective-permute-done | bytes 262176 | tf_op jit(solution)/shard_map/ppermute | solution.py:420
  59.9 1.8 %finish.1 = f32[4,2,64,256]{3,2,1,0:T(8,128)} custom-call(s32[3]{0:T(128)S(1)} %copy-done, f32[128,512]{1,0:T(8,128)S(1)} %add_add_fusion.mine_ref, f32[128,512]{1,0:T(8,128)S(1)} %collective-permute-done.16.other_ref), custom_call_target="tpu_custom_call" | custom-call | flops 200000 | bytes 1000000 | tf_op jit(solution)/shard_map/finish/pallas_call | solution.py:407
  (28 shorter events, 0.5 us)
Async XLA Ops:
  0.0 13.3 %copy-start.5 = (s32[3]{0:T(128)S(1)}, s32[3]{0:T(128)}, u32[]{:S(2)}) copy-start(s32[3]{0:T(128)} %momentum_ref.1) | copy-start | bytes 40
  0.0 20.9 %collective-permute-start.2 = (bf16[3072,128]{1,0:T(8,128)(2,1)}, bf16[3072,128]{1,0:T(8,128)(2,1)S(1)}, u32[]{:S(2)}, u32[]{:S(2)}) collective-permute-start(bf16[3072,128]{1,0:T(8,128)(2,1)} %bitcast.2), channel_id=1, source_target_pairs={{0,1},{1,2},{2,3},{3,0},{4,5},{5,6},{6,7},{7,4},{8,9},{9,10},{10,1... | collective-permute-start | bytes 2359304 | tf_op jit(solution)/shard_map/ppermute | solution.py:420
  2.1 18.9 %collective-permute-start.1 = (bf16[3072,128]{1,0:T(8,128)(2,1)}, bf16[3072,128]{1,0:T(8,128)(2,1)S(1)}, u32[]{:S(2)}, u32[]{:S(2)}) collective-permute-start(bf16[3072,128]{1,0:T(8,128)(2,1)} %bitcast.3), channel_id=1, source_target_pairs={{0,3},{1,0},{2,1},{3,2},{4,7},{5,4},{6,5},{7,6},{8,11},{9,8},{10,9... | collective-permute-start | bytes 2359304 | tf_op jit(solution)/shard_map/ppermute | solution.py:420
  3.6 1.2 %copy-start.1 = (bf16[64,3,8,2,128]{4,3,2,1,0:T(2,128)(2,1)S(1)}, bf16[64,3,8,2,128]{4,3,2,1,0:T(2,128)(2,1)}, u32[]{:S(2)}) copy-start(bf16[64,3,8,2,128]{4,3,2,1,0:T(2,128)(2,1)} %param.4) | copy-start | bytes 2359300
  4.8 0.9 %copy-start.3 = (bf16[3,3,3,8,2,128]{5,4,3,2,1,0:T(2,128)(2,1)S(1)}, bf16[3,3,3,8,2,128]{5,4,3,2,1,0:T(2,128)(2,1)}, u32[]{:S(2)}) copy-start(bf16[3,3,3,8,2,128]{5,4,3,2,1,0:T(2,128)(2,1)} %param.5) | copy-start | bytes 331780
  5.7 7.6 %copy-start.2 = (bf16[64,3,8,2,128]{4,3,2,1,0:T(2,128)(2,1)S(1)}, bf16[64,3,8,2,128]{4,3,2,1,0:T(2,128)(2,1)}, u32[]{:S(2)}) copy-start(bf16[64,3,8,2,128]{4,3,2,1,0:T(2,128)(2,1)} %param.4) | copy-start | bytes 2359300
  5.7 7.6 %copy-start.4 = (bf16[3,3,3,8,2,128]{5,4,3,2,1,0:T(2,128)(2,1)S(1)}, bf16[3,3,3,8,2,128]{5,4,3,2,1,0:T(2,128)(2,1)}, u32[]{:S(2)}) copy-start(bf16[3,3,3,8,2,128]{5,4,3,2,1,0:T(2,128)(2,1)} %param.5) | copy-start | bytes 331780
  6.3 11.9 %collective-permute-start.4 = (bf16[6,64,128]{2,1,0:T(8,128)(2,1)S(1)}, bf16[6,64,128]{2,1,0:T(8,128)(2,1)S(1)}, u32[]{:S(2)}, u32[]{:S(2)}) collective-permute-start(bf16[6,64,128]{2,1,0:T(8,128)(2,1)S(1)} %get-tuple-element.36), channel_id=1, source_target_pairs={{0,96},{32,0},{64,32},{96,64},{1,97},{33,1},{65,33},{97,65},{2,98}... | collective-permute-start | bytes 294920 | tf_op jit(solution)/shard_map/ppermute | solution.py:420
  7.4 18.5 %collective-permute-start = (bf16[24,64,128]{2,1,0:T(8,128)(2,1)S(1)}, bf16[24,64,128]{2,1,0:T(8,128)(2,1)S(1)}, u32[]{:S(2)}, u32[]{:S(2)}) collective-permute-start(bf16[24,64,128]{2,1,0:T(8,128)(2,1)S(1)} %get-tuple-element.32), channel_id=1, source_target_pairs={{0,28},{4,0},{8,4},{12,8},{16,12},{20,16},{24,20},{28,24},{1,29},{... | collective-permute-start | bytes 1179656 | tf_op jit(solution)/shard_map/ppermute | solution.py:420
  13.2 14.1 %collective-permute-start.3 = (bf16[26,64,128]{2,1,0:T(8,128)(2,1)S(1)}, bf16[26,64,128]{2,1,0:T(8,128)(2,1)S(1)}, u32[]{:S(2)}, u32[]{:S(2)}) collective-permute-start(bf16[26,64,128]{2,1,0:T(8,128)(2,1)S(1)} %get-tuple-element.34), channel_id=1, source_target_pairs={{0,4},{4,8},{8,12},{12,16},{16,20},{20,24},{24,28},{28,0},{1,5},{5... | collective-permute-start | bytes 1277960 | tf_op jit(solution)/shard_map/ppermute | solution.py:420
  18.1 7.8 %collective-permute-start.5 = (bf16[7,64,128]{2,1,0:T(8,128)(2,1)S(1)}, bf16[7,64,128]{2,1,0:T(8,128)(2,1)S(1)}, u32[]{:S(2)}, u32[]{:S(2)}) collective-permute-start(bf16[7,64,128]{2,1,0:T(8,128)(2,1)S(1)} %get-tuple-element.38), channel_id=1, source_target_pairs={{0,32},{32,64},{64,96},{96,0},{1,33},{33,65},{65,97},{97,1},{2,34}... | collective-permute-start | bytes 344072 | tf_op jit(solution)/shard_map/ppermute | solution.py:420
  20.9 13.3 %collective-permute-start.7 = (bf16[1536,128]{1,0:T(8,128)(2,1)S(1)}, bf16[1536,128]{1,0:T(8,128)(2,1)S(1)}, u32[]{:S(2)}, u32[]{:S(2)}) collective-permute-start(bf16[1536,128]{1,0:T(8,128)(2,1)S(1)} %slice.8), channel_id=1, source_target_pairs={{0,1},{1,2},{2,3},{3,0},{4,5},{5,6},{6,7},{7,4},{8,9},{9,10},{10,1... | collective-permute-start | bytes 1179656 | tf_op jit(solution)/shard_map/ppermute | solution.py:420
  21.0 13.2 %collective-permute-start.8 = (bf16[1536,128]{1,0:T(8,128)(2,1)S(1)}, bf16[1536,128]{1,0:T(8,128)(2,1)S(1)}, u32[]{:S(2)}, u32[]{:S(2)}) collective-permute-start(bf16[1536,128]{1,0:T(8,128)(2,1)S(1)} %slice.9), channel_id=1, source_target_pairs={{0,3},{1,0},{2,1},{3,2},{4,7},{5,4},{6,5},{7,6},{8,11},{9,8},{10,9... | collective-permute-start | bytes 1179656 | tf_op jit(solution)/shard_map/ppermute | solution.py:420
  32.3 27.6 %copy-start = (s32[3]{0:T(128)S(1)}, s32[3]{0:T(128)}, u32[]{:S(2)}) copy-start(s32[3]{0:T(128)} %dirs_ref.1) | copy-start | bytes 40
  32.3 3.5 %collective-permute-start.6 = (f32[128,384]{1,0:T(8,128)S(1)}, f32[128,384]{1,0:T(8,128)S(1)}, u32[]{:S(2)}, u32[]{:S(2)}) collective-permute-start(f32[128,384]{1,0:T(8,128)S(1)} %get-tuple-element.42), channel_id=1, source_target_pairs={{0,32},{32,0},{64,96},{96,64},{1,33},{33,1},{65,97},{97,65},{2,34}... | collective-permute-start | bytes 589832 | tf_op jit(solution)/shard_map/ppermute | solution.py:420
  35.7 1.3 %collective-permute-start.9 = (f32[128,128]{1,0:T(8,128)S(1)}, f32[128,128]{1,0:T(8,128)S(1)}, u32[]{:S(2)}, u32[]{:S(2)}) collective-permute-start(f32[128,128]{1,0:T(8,128)S(1)} %get-tuple-element.44), channel_id=1, source_target_pairs={{0,32},{32,0},{64,96},{96,64},{1,33},{33,1},{65,97},{97,65},{2,34}... | collective-permute-start | bytes 196616 | tf_op jit(solution)/shard_map/ppermute | solution.py:420
  37.0 6.4 %collective-permute-start.11 = (bf16[128,512]{1,0:T(8,128)(2,1)S(1)}, bf16[128,512]{1,0:T(8,128)(2,1)S(1)}, u32[]{:S(2)}, u32[]{:S(2)}) collective-permute-start(bf16[128,512]{1,0:T(8,128)(2,1)S(1)} %pad_maximum_fusion), channel_id=1, source_target_pairs={{0,4},{4,8},{8,12},{12,0},{16,20},{20,24},{24,28},{28,16},{1,5},{5... | collective-permute-start | bytes 393224 | tf_op jit(solution)/shard_map/ppermute | solution.py:420
  37.4 8.5 %collective-permute-start.10 = (bf16[128,512]{1,0:T(8,128)(2,1)S(1)}, bf16[128,512]{1,0:T(8,128)(2,1)S(1)}, u32[]{:S(2)}, u32[]{:S(2)}) collective-permute-start(bf16[128,512]{1,0:T(8,128)(2,1)S(1)} %pad_maximum_fusion), channel_id=1, source_target_pairs={{0,8},{4,12},{8,0},{12,4},{16,24},{20,28},{24,16},{28,20},{1,9},{5... | collective-permute-start | bytes 393224 | tf_op jit(solution)/shard_map/ppermute | solution.py:420
  39.8 6.5 %collective-permute-start.12 = (bf16[128,512]{1,0:T(8,128)(2,1)S(1)}, bf16[128,512]{1,0:T(8,128)(2,1)S(1)}, u32[]{:S(2)}, u32[]{:S(2)}) collective-permute-start(bf16[128,512]{1,0:T(8,128)(2,1)S(1)} %pad_maximum_fusion), channel_id=1, source_target_pairs={{0,12},{4,0},{8,4},{12,8},{16,28},{20,16},{24,20},{28,24},{1,13},{... | collective-permute-start | bytes 393224 | tf_op jit(solution)/shard_map/ppermute | solution.py:420
  46.4 5.8 %collective-permute-start.15 = (bf16[128,512]{1,0:T(8,128)(2,1)S(1)}, bf16[128,512]{1,0:T(8,128)(2,1)S(1)}, u32[]{:S(2)}, u32[]{:S(2)}) collective-permute-start(bf16[128,512]{1,0:T(8,128)(2,1)S(1)} %add_convert_fusion), channel_id=1, source_target_pairs={{0,80},{4,84},{8,88},{12,92},{16,64},{20,68},{24,72},{28,76},{32,1... | collective-permute-start | bytes 393224 | tf_op jit(solution)/shard_map/ppermute | solution.py:420
  49.8 4.1 %collective-permute-start.14 = (bf16[128,512]{1,0:T(8,128)(2,1)S(1)}, bf16[128,512]{1,0:T(8,128)(2,1)S(1)}, u32[]{:S(2)}, u32[]{:S(2)}) collective-permute-start(bf16[128,512]{1,0:T(8,128)(2,1)S(1)} %add_convert_fusion), channel_id=1, source_target_pairs={{0,64},{32,96},{64,0},{96,32},{1,65},{33,97},{65,1},{97,33},{2,66}... | collective-permute-start | bytes 393224 | tf_op jit(solution)/shard_map/ppermute | solution.py:420
  49.8 7.0 %collective-permute-start.13 = (bf16[128,512]{1,0:T(8,128)(2,1)S(1)}, bf16[128,512]{1,0:T(8,128)(2,1)S(1)}, u32[]{:S(2)}, u32[]{:S(2)}) collective-permute-start(bf16[128,512]{1,0:T(8,128)(2,1)S(1)} %add_convert_fusion), channel_id=1, source_target_pairs={{0,16},{4,20},{8,24},{12,28},{16,0},{20,4},{24,8},{28,12},{1,17},{... | collective-permute-start | bytes 393224 | tf_op jit(solution)/shard_map/ppermute | solution.py:420
  56.9 3.0 %collective-permute-start.16 = (f32[128,512]{1,0:T(8,128)S(1)}, f32[128,512]{1,0:T(8,128)S(1)}, u32[]{:S(2)}, u32[]{:S(2)}) collective-permute-start(f32[128,512]{1,0:T(8,128)S(1)} %add_add_fusion.mine_ref), channel_id=1, source_target_pairs={{0,32},{32,0},{64,96},{96,64},{1,33},{33,1},{65,97},{97,65},{2,34}... | collective-permute-start | bytes 786440 | tf_op jit(solution)/shard_map/ppermute | solution.py:420

commit v4 on v3

--- a/solution.py
+++ b/solution.py
@@ -224,7 +224,7 @@
 
 
 def border_kernel(
-    local_ref, e_ref, s_ref, upr, upi, r_ref, i_ref, yp_ref, ym_ref, zp_ref, zm_ref,
+    mu, before_ref, e_ref, s_ref, upr, upi, r_ref, i_ref, ahead_ref, behind_ref,
     w_ref, ext, exts, dnr, dni, lwide, real, imag,
 ):
     lane, first, sign = lane_masks()
@@ -235,61 +235,68 @@
         exts[c, z, y] = pltpu.roll(tile, HALF, 1)
 
     for c in range(COL):
-        for z in range(DZ):
-            put(c, z + 1, HY + 1, yp_ref[c * DZ + z])
-            put(c, z + 1, 0, ym_ref[c * DZ + z])
-        for y in range(HY):
-            put(c, DZ + 1, y + 1, zp_ref[c * HY + y])
-            put(c, 0, y + 1, zm_ref[c * HY + y])
-
-    lwide[0:128, :] = jnp.concatenate([ym_ref[24], ym_ref[25]], 0).astype(F32)
-    lwide[128:192, :] = zm_ref[6].astype(F32)
+        if mu == 1:
+            for z in range(DZ):
+                put(c, z + 1, HY + 1, ahead_ref[c * DZ + z])
+                put(c, z + 1, 0, behind_ref[c * DZ + z])
+        else:
+            for y in range(HY):
+                put(c, DZ + 1, y + 1, ahead_ref[c * HY + y])
+                put(c, 0, y + 1, behind_ref[c * HY + y])
+
+    if mu == 1:
+        lwide[...] = jnp.concatenate([behind_ref[24], behind_ref[25]], 0).astype(F32)
+    else:
+        lwide[0:64, :] = behind_ref[6].astype(F32)
+        lwide[64:128, :] = jnp.zeros((64, LANES), F32)
     re, im = line_coefficients(lwide[...], first)
     real[...] = re
     imag[...] = im * sign
-    for z in range(DZ):
-        pick = pl.ds(z, 9, stride=DZ)
-        dnr[z * HY, 9:18, :] = real[pick, :]
-        dni[z * HY, 9:18, :] = imag[pick, :]
-    for y in range(HY):
-        pick = pl.ds(128 + 16 * y, 9)
-        dnr[y, 18:27, :] = real[pick, :]
-        dni[y, 18:27, :] = imag[pick, :]
+    if mu == 1:
+        for z in range(DZ):
+            pick = pl.ds(z, 9, stride=DZ)
+            dnr[z * HY, 9:18, :] = real[pick, :]
+            dni[z * HY, 9:18, :] = imag[pick, :]
+    else:
+        for y in range(HY):
+            pick = pl.ds(16 * y, 9)
+            dnr[y, 18:27, :] = real[pick, :]
+            dni[y, 18:27, :] = imag[pick, :]
 
     def site(zy, carry):
         z = lax.div(zy, HY) + 1
         y = lax.rem(zy, HY) + 1
-        for mu in (1, 2):
-
-            def neighbour(c, step):
-                at = (c, z, y + step) if mu == 1 else (c, z + step, y)
-                return ext[at], exts[at]
-
-            def store(r, value):
-                column = pl.multiple_of((r * NZY + zy) * LANES, LANES)
-                w_ref[mu + 1, :, pl.ds(column, LANES)] = value
-
-            derivative(mu, neighbour, (upr, upi, dnr, dni), zy, store)
+
+        def neighbour(c, step):
+            at = (c, z, y + step) if mu == 1 else (c, z + step, y)
+            return ext[at], exts[at]
+
+        def store(r, value):
+            column = pl.multiple_of((r * NZY + zy) * LANES, LANES)
+            w_ref[mu + 1, :, pl.ds(column, LANES)] = value
+
+        derivative(mu, neighbour, (upr, upi, dnr, dni), zy, store)
         return carry
 
     lax.fori_loop(0, NZY, site, 0)
 
 
-def border_terms(w, ext, exts, upr, upi, dnr, dni, yp, ym, zp, zm):
-    line = pltpu.VMEM((192, LANES), F32)
-    return pl.pallas_call(
-        border_kernel,
+def border_terms(mu, w, ext, exts, upr, upi, dnr, dni, ahead, behind):
+    line = pltpu.VMEM((128, LANES), F32)
+    w, ext, exts, dnr, dni = pl.pallas_call(
+        functools.partial(border_kernel, mu),
         out_shape=(shape((4, NV, KDIM), BF16),)
         + (shape(EXTENDED, F32),) * 2
         + (shape(TABLE, F32),) * 2,
-        in_specs=[VMEM] * 11,
+        in_specs=[VMEM] * 9,
         out_specs=(VMEM,) * 5,
         input_output_aliases={0: 0, 1: 1, 2: 2, 5: 3, 6: 4},
         scratch_shapes=[line, line, line],
         compiler_params=params(4),
-        cost_estimate=pl.CostEstimate(flops=6000000000, bytes_accessed=6000000, transcendentals=0),
-        name="border_terms",
-    )(w, ext, exts, upr, upi, dnr, dni, yp, ym, zp, zm)[0]
+        cost_estimate=pl.CostEstimate(flops=3000000000, bytes_accessed=3000000, transcendentals=0),
+        name="border_y" if mu == 1 else "border_z",
+    )(w, ext, exts, upr, upi, dnr, dni, ahead, behind)
+    return w, ext, exts, upr, upi, dnr, dni
 
 
 def fill_right(counts, blocks, wide, right):
@@ -384,35 +391,46 @@
     )(w, *blocks)
 
 
-def finish_kernel(scale, dirs_ref, mine_ref, other_ref, out_ref):
+def finish_kernel(scale, other, dirs_ref, rows_ref, *refs):
+    out_ref, lines, sem = refs[-3:]
     shift = lax.axis_index("vec").astype(jnp.int32) * HALF
-    core = lax.axis_index("gz").astype(jnp.int32) & 1
+    half = (lax.axis_index("gz").astype(jnp.int32) & 1) ^ other
     slots = [
         sum(jnp.where(dirs_ref[o] == mu, o, 0) for o in range(3)).astype(jnp.int32)
         for mu in range(3)
     ]
-    for ch, rows_ref in enumerate((mine_ref, other_ref)):
-        rows = rows_ref[...]
-        for part in range(2):
-            near = rows[:, part * 192:(part + 1) * 192]
-            far = rows[:, 384 + part * 64:384 + (part + 1) * 64]
-            line = jnp.concatenate([near[:, 0:128], far, near[:, 128:192]], 1) * scale
-            line = pltpu.roll(line, shift, 1)
-            half = core if ch == 0 else 1 - core
-            out_ref[jnp.where(half == 0, slots[0], slots[1]), part] = line[0:NV]
-            out_ref[jnp.where(half == 0, 3, slots[2]), part] = line[NV:2 * NV]
-
-
-def finish(directions, mine, other, scale):
-    return pl.pallas_call(
-        functools.partial(finish_kernel, scale),
+    places = [jnp.where(half == 0, slots[0], slots[1]), jnp.where(half == 0, 3, slots[2])]
+    rows = rows_ref[...]
+    copies = []
+    for part in range(2):
+        near = rows[:, part * 192:(part + 1) * 192]
+        far = rows[:, 384 + part * 64:384 + (part + 1) * 64]
+        line = jnp.concatenate([near[:, 0:128], far, near[:, 128:192]], 1) * scale
+        line = pltpu.roll(line, shift, 1)
+        for which in range(2):
+            lines[which, part] = line[which * NV:(which + 1) * NV]
+            copy = pltpu.make_async_copy(
+                lines.at[which, part], out_ref.at[places[which], part], sem.at[which, part]
+            )
+            copy.start()
+            copies.append(copy)
+    for copy in copies:
+        copy.wait()
+
+
+def finish(directions, rows, scale, so_far=None):
+    other = so_far is not None
+    return pl.pallas_call(
+        functools.partial(finish_kernel, scale, int(other)),
         out_shape=shape((4, 2, NV, 256), F32),
-        in_specs=[SMEM] + [VMEM] * 2,
-        out_specs=VMEM,
-        compiler_params=params(16),
+        in_specs=[SMEM, VMEM] + [HBM] * other,
+        out_specs=HBM,
+        input_output_aliases={2: 0} if other else {},
+        scratch_shapes=[pltpu.VMEM((2, 2, NV, 256), F32), pltpu.SemaphoreType.DMA((2, 2))],
+        compiler_params=params(4),
         cost_estimate=pl.CostEstimate(flops=200000, bytes_accessed=1000000, transcendentals=0),
-        name="finish",
-    )(directions, mine, other)
+        name="finish_other" if other else "finish_mine",
+    )(directions, rows, *([so_far] if other else []))
 
 
 def permuted(value, axis, target):
@@ -420,9 +438,9 @@
     return lax.ppermute(value, axis, [(source, target(source)) for source in range(size)])
 
 
-def four_sum(own, axis_opposite, axis_side, axis_other):
-    wide = [t.astype(F32) for t in (own, axis_opposite, axis_side, axis_other)]
-    return (wide[0] + wide[1]) + (wide[2] + wide[3])
+def four_sum(own, opposite, side, other):
+    pair = side.astype(F32) + other.astype(F32)
+    return pair + (own.astype(F32) + opposite.astype(F32))
 
 
 def body(vectors, links, momentum, directions):
@@ -444,8 +462,9 @@
     far_high = permuted(next_[mid:], "vec", lambda s: (s - 1) % 4)
 
     right = right_side([rows, next_, prev])
-    yp, right = lax.optimization_barrier((yp, right))
-    w = border_terms(*partial, yp, ym, zp, zm)
+    zm, right = lax.optimization_barrier((zm, right))
+    partial = border_terms(2, *partial, zp, zm)
+    w = border_terms(1, *partial, yp, ym)[0]
 
     mate = lambda v: permuted(v, "gz", lambda s: s ^ 1)
     along_x = lambda v, step: permuted(v, "gy", lambda s: (s // 4) * 4 + (s + step) % 4)
@@ -456,13 +475,15 @@
     near = chip_sum(*contract_near(w, right))
     far = chip_sum(*contract_far(w, [far_low, far_high]))
     chip = jnp.concatenate([near, far], 1)
-    row = four_sum(chip, along_x(chip, 2), along_x(chip, 1), along_x(chip, 3)).astype(BF16)
-    across = permuted(row, "gy", lambda s: s ^ 4)
+    ahead, behind = along_x(chip, 1), along_x(chip, 3)
+    row = four_sum(chip, along_x(chip, 2), ahead, behind).astype(BF16)
     side = permuted(row, "gz", lambda s: s ^ 2)
     both = permuted(row, ("gz", "gy"), lambda s: s ^ 20)
+    across = permuted(row, "gy", lambda s: s ^ 4)
     plane = four_sum(row, across, side, both)
     scale = 1.0 / math.sqrt(EXT_X * EXT_Y * EXT_Z)
-    return finish(directions, plane, mate(plane), scale)
+    mine = finish(directions, plane, scale)
+    return finish(directions, mate(plane), scale, mine)
 
 
 def solution(mesh):

time: 61.8 us -> 60.5 us (0.979)
  waiting for transfers between devices: 16.6 us -> 12.9 us
  Pallas kernels: 15.7 us -> 17.3 us
  starting transfers between devices: 27 us -> 27.7 us
    ppermute x17, waiting for transfers between devices: 16.6 us -> 12.9 us  [permuted(): lax.ppermute(value, axis, [(source, target(source)) for source in range(s...]
    pallas_call x2 -> x4, Pallas kernels: 4.81 us -> 6.23 us  [the longest x2 3.37 us: border_terms(): pl.pallas_call(functools.partial(border_kernel, mu), out_shape=(shape((4,...]
    ppermute x17, starting transfers between devices: 27 us -> 27.7 us  [permuted(): lax.ppermute(value, axis, [(source, target(source)) for source in range(s...]
    unnamed x12 -> x10, local copies, waits for them, and re-layouts: 2.08 us -> 2.08 us
  transfers between devices with their start and end apart: 17 -> 17, of which waited for: 10 -> 7; matrix products, arithmetic and copies ran while one was open for 0% -> 0% of each run, Pallas kernels for 23% -> 26%
where the time goes in v4:
time: 60.5 us; the launch traced here: 60.3 us
  starting transfers between devices  27.7 us (46%)
  Pallas kernels  17.3 us (29%)
  waiting for transfers between devices  12.9 us (21%)
  local copies, waits for them, and re-layouts  2.13 us (4%)
    ppermute x17, starting transfers between devices, permuted(): lax.ppermute(value, axis, [(source, target(source)) for source in range(s...  27.7 us
    ppermute x17, waiting for transfers between devices, permuted(): lax.ppermute(value, axis, [(source, target(source)) for source in range(s...  12.9 us
    pallas_call x1, Pallas kernels, local_terms(): pl.pallas_call(local_kernel, out_shape=(shape((4, NV, KDIM), BF16),) + (s...  4.9 us
    pallas_call x2, Pallas kernels, border_terms(): pl.pallas_call(functools.partial(border_kernel, mu), out_shape=(shape((4,...  3.37 us
    pallas_call x2, Pallas kernels, finish(): pl.pallas_call(functools.partial(finish_kernel, scale, int(other)), out_s...  2.86 us
    pallas_call x1, Pallas kernels, right_side(): pl.pallas_call(functools.partial(right_kernel, counts), out_shape=shape((...  2.27 us
    unnamed x10, local copies, waits for them, and re-layouts  2.08 us
    pallas_call x1, Pallas kernels, contract_near(): pl.pallas_call(near_kernel, out_shape=(out, out), in_specs=[VMEM] * 2, ou...  1.87 us
  transfers between devices with their start and end apart: 17, of which 7 were waited for; matrix products, arithmetic and copies ran while one was open for 0% of the time, Pallas kernels for 26%

profile of v4, /device:TPU:1, one launch (start us, length us, event | category | flops | bytes accessed | tf_op | source)
XLA Modules:
  0.0 60.3 jit_solution(776559332942670997)
XLA Ops:
  0.0 2.1 %collective-permute-start.3 = (bf16[3072,128]{1,0:T(8,128)(2,1)}, bf16[3072,128]{1,0:T(8,128)(2,1)S(1)}, u32[]{:S(2)}, u32[]{:S(2)}) collective-permute-start(bf16[3072,128]{1,0:T(8,128)(2,1)} %bitcast.2), channel_id=1, source_target_pairs={{0,1},{1,2},{2,3},{3,0},{4,5},{5,6},{6,7},{7,4},{8,9},{9,10},{10,1... | collective-permute-start | bytes 2359304 | tf_op jit(solution)/shard_map/ppermute | solution.py:438
  2.1 1.5 %collective-permute-start.2 = (bf16[3072,128]{1,0:T(8,128)(2,1)}, bf16[3072,128]{1,0:T(8,128)(2,1)S(1)}, u32[]{:S(2)}, u32[]{:S(2)}) collective-permute-start(bf16[3072,128]{1,0:T(8,128)(2,1)} %bitcast.3), channel_id=1, source_target_pairs={{0,3},{1,0},{2,1},{3,2},{4,7},{5,4},{6,5},{7,6},{8,11},{9,8},{10,9... | collective-permute-start | bytes 2359304 | tf_op jit(solution)/shard_map/ppermute | solution.py:438
  3.6 1.2 %copy-done.1 = bf16[64,3,8,2,128]{4,3,2,1,0:T(2,128)(2,1)S(1)} copy-done((bf16[64,3,8,2,128]{4,3,2,1,0:T(2,128)(2,1)S(1)}, bf16[64,3,8,2,128]{4,3,2,1,0:T(2,128)(2,1)}, u32[]{:S(2)}) %copy-start.1) | copy-done | bytes 786456
  4.8 0.9 %copy-done.3 = bf16[3,3,3,8,2,128]{5,4,3,2,1,0:T(2,128)(2,1)S(1)} copy-done((bf16[3,3,3,8,2,128]{5,4,3,2,1,0:T(2,128)(2,1)S(1)}, bf16[3,3,3,8,2,128]{5,4,3,2,1,0:T(2,128)(2,1)}, u32[]{:S(2)}) %copy-start.3) | copy-done | bytes 110616
  5.7 0.6 prepare.1
  6.3 1.1 %collective-permute-start = (bf16[6,64,128]{2,1,0:T(8,128)(2,1)S(1)}, bf16[6,64,128]{2,1,0:T(8,128)(2,1)S(1)}, u32[]{:S(2)}, u32[]{:S(2)}) collective-permute-start(bf16[6,64,128]{2,1,0:T(8,128)(2,1)S(1)} %get-tuple-element.38), channel_id=1, source_target_pairs={{0,96},{32,0},{64,32},{96,64},{1,97},{33,1},{65,33},{97,65},{2,98}... | collective-permute-start | bytes 294920 | tf_op jit(solution)/shard_map/ppermute | solution.py:438
  7.4 5.9 %collective-permute-start.4 = (bf16[24,64,128]{2,1,0:T(8,128)(2,1)S(1)}, bf16[24,64,128]{2,1,0:T(8,128)(2,1)S(1)}, u32[]{:S(2)}, u32[]{:S(2)}) collective-permute-start(bf16[24,64,128]{2,1,0:T(8,128)(2,1)S(1)} %get-tuple-element.47), channel_id=1, source_target_pairs={{0,28},{4,0},{8,4},{12,8},{16,12},{20,16},{24,20},{28,24},{1,29},{... | collective-permute-start | bytes 1179656 | tf_op jit(solution)/shard_map/ppermute | solution.py:438
  13.3 4.9 %local_terms.1 = (bf16[4,64,6144]{2,1,0:T(8,128)(2,1)S(1)}, f32[3,10,4,64,128]{4,3,2,1,0:T(8,128)S(1)}, f32[3,10,4,64,128]{4,3,2,1,0:T(8,128)S(1)}, f32[16,32,12...) custom-call(s32[3]{0:T(128)S(1)} %copy-done.4, ...), custom_call_target="tpu_custom_call" | custom-call | flops 6000000000 | bytes 6000000 | tf_op jit(solution)/shard_map/local_terms/pallas_call | solution.py:205
  18.2 1.1 %collective-permute-start.1 = (bf16[7,64,128]{2,1,0:T(8,128)(2,1)S(1)}, bf16[7,64,128]{2,1,0:T(8,128)(2,1)S(1)}, u32[]{:S(2)}, u32[]{:S(2)}) collective-permute-start(bf16[7,64,128]{2,1,0:T(8,128)(2,1)S(1)} %get-tuple-element.40), channel_id=1, source_target_pairs={{0,32},{32,64},{64,96},{96,0},{1,33},{33,65},{65,97},{97,1},{2,34}... | collective-permute-start | bytes 344072 | tf_op jit(solution)/shard_map/ppermute | solution.py:438
  19.2 1.7 %collective-permute-done.3.refs_2_ = bf16[3072,128]{1,0:T(8,128)(2,1)S(1)} collective-permute-done((bf16[3072,128]{1,0:T(8,128)(2,1)}, bf16[3072,128]{1,0:T(8,128)(2,1)S(1)}, u32[]{:S(2)}, u32[]{:S(2)}) %collective-permute-start.3) | collective-permute-done | bytes 786464 | tf_op jit(solution)/shard_map/ppermute | solution.py:438
  21.0 2.7 %collective-permute-start.8 = (bf16[1536,128]{1,0:T(8,128)(2,1)S(1)}, bf16[1536,128]{1,0:T(8,128)(2,1)S(1)}, u32[]{:S(2)}, u32[]{:S(2)}) collective-permute-start(bf16[1536,128]{1,0:T(8,128)(2,1)S(1)} %slice.9), channel_id=1, source_target_pairs={{0,3},{1,0},{2,1},{3,2},{4,7},{5,4},{6,5},{7,6},{8,11},{9,8},{10,9... | collective-permute-start | bytes 1179656 | tf_op jit(solution)/shard_map/ppermute | solution.py:438
  23.8 2.3 %right_side.1.right_ref = bf16[384,6144]{1,0:T(8,128)(2,1)S(1)} custom-call(bf16[3072,128]{1,0:T(8,128)(2,1)S(1)} %bitcast.6, bf16[3072,128]{1,0:T(8,128)(2,1)S(1)} %collective-permute-done.2.refs_1_, bf16[3072,128]{1,0:T(8,128)(2,1)S(1)} %collective-permute-done.3.refs_2_), custom_call_target="tpu_custom_call" | custom-call | flops 2000000000 | bytes 4000000 | tf_op jit(solution)/shard_map/right_side/pallas_call | solution.py:332
  26.1 1.6 %border_z.1 = (bf16[4,64,6144]{2,1,0:T(8,128)(2,1)S(1)}, f32[3,10,4,64,128]{4,3,2,1,0:T(8,128)S(1)}, f32[3,10,4,64,128]{4,3,2,1,0:T(8,128)S(1)}, f32[16,32,128]{2,1,0:T(8,128)S(1)}, f32[16,32,128]{2,1,0:T(8,128)S(1)}) custom-call(bf16[4,64,6144]{2,1,0:T(8,128)(2,1)S(1)} %get-tuple-elem, ...), custom_call_target="tpu_custom_call", output_to_operand_aliasing={{0}: (0, {}), {1}: (1, {}), {2}: (2, {}), {3}: (5, {}), {4}... | custom-call | flops 3000000000 | bytes 3000000 | tf_op jit(solution)/shard_map/border_z/pallas_call | solution.py:286
  27.7 1.8 %border_y.1 = (bf16[4,64,6144]{2,1,0:T(8,128)(2,1)S(1)}, f32[3,10,4,64,128]{4,3,2,1,0:T(8,128)S(1)}, f32[3,10,4,64,128]{4,3,2,1,0:T(8,128)S(1)}, f32[16,32,128]{2,1,0:T(8,128)S(1)}, f32[16,32,128]{2,1,0:T(8,128)S(1)}) custom-call(bf16[4,64,6144]{2,1,0:T(8,128)(2,1)S(1)} %get-tuple-elem, ...), custom_call_target="tpu_custom_call", output_to_operand_aliasing={{0}: (0, {}), {1}: (1, {}), {2}: (2, {}), {3}: (5, {}), {4}... | custom-call | flops 3000000000 | bytes 3000000 | tf_op jit(solution)/shard_map/border_y/pallas_call | solution.py:286
  29.5 1.9 %contract_near.1 = (f32[128,384]{1,0:T(8,128)S(1)}, f32[128,384]{1,0:T(8,128)S(1)}) custom-call(bf16[4,64,6144]{2,1,0:T(8,128)(2,1)S(1)} %get-tuple-element.49.w_ref, bf16[384,6144]{1,0:T(8,128)(2,1)S(1)} %right_side.1.right_ref), custom_call_target="tpu_custom_call" | custom-call | flops 1207959552 | bytes 4000000 | tf_op jit(solution)/shard_map/contract_near/pallas_call | solution.py:358
  31.3 2.4 %collective-permute-start.6 = (f32[128,384]{1,0:T(8,128)S(1)}, f32[128,384]{1,0:T(8,128)S(1)}, u32[]{:S(2)}, u32[]{:S(2)}) collective-permute-start(f32[128,384]{1,0:T(8,128)S(1)} %get-tuple-element.52), channel_id=1, source_target_pairs={{0,32},{32,0},{64,96},{96,64},{1,33},{33,1},{65,97},{97,65},{2,34}... | collective-permute-start | bytes 589832 | tf_op jit(solution)/shard_map/ppermute | solution.py:438
  33.7 1.5 %contract_far.1 = (f32[128,128]{1,0:T(8,128)S(1)}, f32[128,128]{1,0:T(8,128)S(1)}) custom-call(bf16[4,64,6144]{2,1,0:T(8,128)(2,1)S(1)} %get-tuple-element.49.w_ref, bf16[1536,128]{1,0:T(8,128)(2,1)S(1)} %collective-permute-done.7.refs_0_, bf16[1536,128]{1,0:T(8,128)(2,1)S(1)} %collective-permute-done.8.refs_1_), custom_call_target="tpu_custom_call" | custom-call | flops 402653184 | bytes 4000000 | tf_op jit(solution)/shard_map/contract_far/pallas_call | solution.py:376
  35.3 1.2 %collective-permute-done.9 = f32[128,128]{1,0:T(8,128)S(1)} collective-permute-done((f32[128,128]{1,0:T(8,128)S(1)}, f32[128,128]{1,0:T(8,128)S(1)}, u32[]{:S(2)}, u32[]{:S(2)}) %collective-permute-start.9) | collective-permute-done | bytes 65568 | tf_op jit(solution)/shard_map/ppermute | solution.py:438
  36.6 2.4 %collective-permute-start.12 = (bf16[128,512]{1,0:T(8,128)(2,1)S(1)}, bf16[128,512]{1,0:T(8,128)(2,1)S(1)}, u32[]{:S(2)}, u32[]{:S(2)}) collective-permute-start(bf16[128,512]{1,0:T(8,128)(2,1)S(1)} %pad_maximum_fusion), channel_id=1, source_target_pairs={{0,8},{4,12},{8,0},{12,4},{16,24},{20,28},{24,16},{28,20},{1,9},{5... | collective-permute-start | bytes 393224 | tf_op jit(solution)/shard_map/ppermute | solution.py:438
  39.0 0.9 %collective-permute-start.11 = (bf16[128,512]{1,0:T(8,128)(2,1)S(1)}, bf16[128,512]{1,0:T(8,128)(2,1)S(1)}, u32[]{:S(2)}, u32[]{:S(2)}) collective-permute-start(bf16[128,512]{1,0:T(8,128)(2,1)S(1)} %pad_maximum_fusion), channel_id=1, source_target_pairs={{0,12},{4,0},{8,4},{12,8},{16,28},{20,16},{24,20},{28,24},{1,13},{... | collective-permute-start | bytes 393224 | tf_op jit(solution)/shard_map/ppermute | solution.py:438
  39.9 0.6 %collective-permute-start.10 = (bf16[128,512]{1,0:T(8,128)(2,1)S(1)}, bf16[128,512]{1,0:T(8,128)(2,1)S(1)}, u32[]{:S(2)}, u32[]{:S(2)}) collective-permute-start(bf16[128,512]{1,0:T(8,128)(2,1)S(1)} %pad_maximum_fusion), channel_id=1, source_target_pairs={{0,4},{4,8},{8,12},{12,0},{16,20},{20,24},{24,28},{28,16},{1,5},{5... | collective-permute-start | bytes 393224 | tf_op jit(solution)/shard_map/ppermute | solution.py:438
  40.5 2.6 %collective-permute-done.12 = bf16[128,512]{1,0:T(8,128)(2,1)S(1)} collective-permute-done((bf16[128,512]{1,0:T(8,128)(2,1)S(1)}, bf16[128,512]{1,0:T(8,128)(2,1)S(1)}, u32[]{:S(2)}, u32[]{:S(2)}) %collective-permute-start.12) | collective-permute-done | bytes 131104 | tf_op jit(solution)/shard_map/ppermute | solution.py:438
  43.1 2.4 %collective-permute-done.11 = bf16[128,512]{1,0:T(8,128)(2,1)S(1)} collective-permute-done((bf16[128,512]{1,0:T(8,128)(2,1)S(1)}, bf16[128,512]{1,0:T(8,128)(2,1)S(1)}, u32[]{:S(2)}, u32[]{:S(2)}) %collective-permute-start.11) | collective-permute-done | bytes 131104 | tf_op jit(solution)/shard_map/ppermute | solution.py:438
  45.5 0.2 collective-permute-done.10
  45.8 3.5 %collective-permute-start.15 = (bf16[128,512]{1,0:T(8,128)(2,1)S(1)}, bf16[128,512]{1,0:T(8,128)(2,1)S(1)}, u32[]{:S(2)}, u32[]{:S(2)}) collective-permute-start(bf16[128,512]{1,0:T(8,128)(2,1)S(1)} %add_convert_fusion), channel_id=1, source_target_pairs={{0,16},{4,20},{8,24},{12,28},{16,0},{20,4},{24,8},{28,12},{1,17},{... | collective-permute-start | bytes 393224 | tf_op jit(solution)/shard_map/ppermute | solution.py:438
  49.3 0.4 collective-permute-start.14
  49.7 0.3 collective-permute-start.13
  50.0 1.6 %collective-permute-done.15 = bf16[128,512]{1,0:T(8,128)(2,1)S(1)} collective-permute-done((bf16[128,512]{1,0:T(8,128)(2,1)S(1)}, bf16[128,512]{1,0:T(8,128)(2,1)S(1)}, u32[]{:S(2)}, u32[]{:S(2)}) %collective-permute-start.15) | collective-permute-done | bytes 131104 | tf_op jit(solution)/shard_map/ppermute | solution.py:438
  51.6 3.2 %collective-permute-done.14 = bf16[128,512]{1,0:T(8,128)(2,1)S(1)} collective-permute-done((bf16[128,512]{1,0:T(8,128)(2,1)S(1)}, bf16[128,512]{1,0:T(8,128)(2,1)S(1)}, u32[]{:S(2)}, u32[]{:S(2)}) %collective-permute-start.14) | collective-permute-done | bytes 131104 | tf_op jit(solution)/shard_map/ppermute | solution.py:438
  54.8 2.6 %collective-permute-start.16 = (f32[128,512]{1,0:T(8,128)S(1)}, f32[128,512]{1,0:T(8,128)S(1)}, u32[]{:S(2)}, u32[]{:S(2)}) collective-permute-start(f32[128,512]{1,0:T(8,128)S(1)} %add_add_fusion.rows_ref), channel_id=1, source_target_pairs={{0,32},{32,0},{64,96},{96,64},{1,33},{33,1},{65,97},{97,65},{2,34}... | collective-permute-start | bytes 786440 | tf_op jit(solution)/shard_map/ppermute | solution.py:438
  57.4 1.4 %finish_mine.1.refs_0_ = f32[4,2,64,256]{3,2,1,0:T(8,128)} custom-call(s32[3]{0:T(128)S(1)} %copy-done, f32[128,512]{1,0:T(8,128)S(1)} %add_add_fusion.rows_ref), custom_call_target="tpu_custom_call" | custom-call | flops 200000 | bytes 1000000 | tf_op jit(solution)/shard_map/finish_mine/pallas_call | solution.py:423
  58.9 1.4 %finish_other.1 = f32[4,2,64,256]{3,2,1,0:T(8,128)} custom-call(s32[3]{0:T(128)S(1)} %copy-done, f32[128,512]{1,0:T(8,128)S(1)} %collective-permute-done.16.rows_ref, f32[4,2,64,256]{3,2,1,0:T(8,128)} %finish_mine.1.refs_0_), custom_call_target="tpu_custom_call", output_to_operand_aliasing={{}: (2, {})} | custom-call | flops 200000 | bytes 1000000 | tf_op jit(solution)/shard_map/finish_other/pallas_call | solution.py:423
  (28 shorter events, 0.5 us)
Async XLA Ops:
  0.0 13.3 %copy-start.4 = (s32[3]{0:T(128)S(1)}, s32[3]{0:T(128)}, u32[]{:S(2)}) copy-start(s32[3]{0:T(128)} %momentum_ref.1) | copy-start | bytes 40
  0.0 20.9 %collective-permute-start.3 = (bf16[3072,128]{1,0:T(8,128)(2,1)}, bf16[3072,128]{1,0:T(8,128)(2,1)S(1)}, u32[]{:S(2)}, u32[]{:S(2)}) collective-permute-start(bf16[3072,128]{1,0:T(8,128)(2,1)} %bitcast.2), channel_id=1, source_target_pairs={{0,1},{1,2},{2,3},{3,0},{4,5},{5,6},{6,7},{7,4},{8,9},{9,10},{10,1... | collective-permute-start | bytes 2359304 | tf_op jit(solution)/shard_map/ppermute | solution.py:438
  2.1 18.9 %collective-permute-start.2 = (bf16[3072,128]{1,0:T(8,128)(2,1)}, bf16[3072,128]{1,0:T(8,128)(2,1)S(1)}, u32[]{:S(2)}, u32[]{:S(2)}) collective-permute-start(bf16[3072,128]{1,0:T(8,128)(2,1)} %bitcast.3), channel_id=1, source_target_pairs={{0,3},{1,0},{2,1},{3,2},{4,7},{5,4},{6,5},{7,6},{8,11},{9,8},{10,9... | collective-permute-start | bytes 2359304 | tf_op jit(solution)/shard_map/ppermute | solution.py:438
  3.6 1.2 %copy-start.1 = (bf16[64,3,8,2,128]{4,3,2,1,0:T(2,128)(2,1)S(1)}, bf16[64,3,8,2,128]{4,3,2,1,0:T(2,128)(2,1)}, u32[]{:S(2)}) copy-start(bf16[64,3,8,2,128]{4,3,2,1,0:T(2,128)(2,1)} %param.4) | copy-start | bytes 2359300
  4.8 0.9 %copy-start.3 = (bf16[3,3,3,8,2,128]{5,4,3,2,1,0:T(2,128)(2,1)S(1)}, bf16[3,3,3,8,2,128]{5,4,3,2,1,0:T(2,128)(2,1)}, u32[]{:S(2)}) copy-start(bf16[3,3,3,8,2,128]{5,4,3,2,1,0:T(2,128)(2,1)} %param.5) | copy-start | bytes 331780
  5.7 7.6 %copy-start.2 = (bf16[64,3,8,2,128]{4,3,2,1,0:T(2,128)(2,1)S(1)}, bf16[64,3,8,2,128]{4,3,2,1,0:T(2,128)(2,1)}, u32[]{:S(2)}) copy-start(bf16[64,3,8,2,128]{4,3,2,1,0:T(2,128)(2,1)} %param.4) | copy-start | bytes 2359300
  6.3 11.9 %collective-permute-start = (bf16[6,64,128]{2,1,0:T(8,128)(2,1)S(1)}, bf16[6,64,128]{2,1,0:T(8,128)(2,1)S(1)}, u32[]{:S(2)}, u32[]{:S(2)}) collective-permute-start(bf16[6,64,128]{2,1,0:T(8,128)(2,1)S(1)} %get-tuple-element.38), channel_id=1, source_target_pairs={{0,96},{32,0},{64,32},{96,64},{1,97},{33,1},{65,33},{97,65},{2,98}... | collective-permute-start | bytes 294920 | tf_op jit(solution)/shard_map/ppermute | solution.py:438
  7.4 20.3 %collective-permute-start.4 = (bf16[24,64,128]{2,1,0:T(8,128)(2,1)S(1)}, bf16[24,64,128]{2,1,0:T(8,128)(2,1)S(1)}, u32[]{:S(2)}, u32[]{:S(2)}) collective-permute-start(bf16[24,64,128]{2,1,0:T(8,128)(2,1)S(1)} %get-tuple-element.47), channel_id=1, source_target_pairs={{0,28},{4,0},{8,4},{12,8},{16,12},{20,16},{24,20},{28,24},{1,29},{... | collective-permute-start | bytes 1179656 | tf_op jit(solution)/shard_map/ppermute | solution.py:438
  13.2 14.4 %collective-permute-start.5 = (bf16[26,64,128]{2,1,0:T(8,128)(2,1)S(1)}, bf16[26,64,128]{2,1,0:T(8,128)(2,1)S(1)}, u32[]{:S(2)}, u32[]{:S(2)}) collective-permute-start(bf16[26,64,128]{2,1,0:T(8,128)(2,1)S(1)} %get-tuple-element.48), channel_id=1, source_target_pairs={{0,4},{4,8},{8,12},{12,16},{16,20},{20,24},{24,28},{28,0},{1,5},{5... | collective-permute-start | bytes 1277960 | tf_op jit(solution)/shard_map/ppermute | solution.py:438
  18.2 7.9 %collective-permute-start.1 = (bf16[7,64,128]{2,1,0:T(8,128)(2,1)S(1)}, bf16[7,64,128]{2,1,0:T(8,128)(2,1)S(1)}, u32[]{:S(2)}, u32[]{:S(2)}) collective-permute-start(bf16[7,64,128]{2,1,0:T(8,128)(2,1)S(1)} %get-tuple-element.40), channel_id=1, source_target_pairs={{0,32},{32,64},{64,96},{96,0},{1,33},{33,65},{65,97},{97,1},{2,34}... | collective-permute-start | bytes 344072 | tf_op jit(solution)/shard_map/ppermute | solution.py:438
  20.9 12.8 %collective-permute-start.7 = (bf16[1536,128]{1,0:T(8,128)(2,1)S(1)}, bf16[1536,128]{1,0:T(8,128)(2,1)S(1)}, u32[]{:S(2)}, u32[]{:S(2)}) collective-permute-start(bf16[1536,128]{1,0:T(8,128)(2,1)S(1)} %slice.8), channel_id=1, source_target_pairs={{0,1},{1,2},{2,3},{3,0},{4,5},{5,6},{6,7},{7,4},{8,9},{9,10},{10,1... | collective-permute-start | bytes 1179656 | tf_op jit(solution)/shard_map/ppermute | solution.py:438
  21.0 12.7 %collective-permute-start.8 = (bf16[1536,128]{1,0:T(8,128)(2,1)S(1)}, bf16[1536,128]{1,0:T(8,128)(2,1)S(1)}, u32[]{:S(2)}, u32[]{:S(2)}) collective-permute-start(bf16[1536,128]{1,0:T(8,128)(2,1)S(1)} %slice.9), channel_id=1, source_target_pairs={{0,3},{1,0},{2,1},{3,2},{4,7},{5,4},{6,5},{7,6},{8,11},{9,8},{10,9... | collective-permute-start | bytes 1179656 | tf_op jit(solution)/shard_map/ppermute | solution.py:438
  31.3 26.1 %copy-start = (s32[3]{0:T(128)S(1)}, s32[3]{0:T(128)}, u32[]{:S(2)}) copy-start(s32[3]{0:T(128)} %dirs_ref.3) | copy-start | bytes 40
  31.3 4.0 %collective-permute-start.6 = (f32[128,384]{1,0:T(8,128)S(1)}, f32[128,384]{1,0:T(8,128)S(1)}, u32[]{:S(2)}, u32[]{:S(2)}) collective-permute-start(f32[128,384]{1,0:T(8,128)S(1)} %get-tuple-element.52), channel_id=1, source_target_pairs={{0,32},{32,0},{64,96},{96,64},{1,33},{33,1},{65,97},{97,65},{2,34}... | collective-permute-start | bytes 589832 | tf_op jit(solution)/shard_map/ppermute | solution.py:438
  35.2 1.3 %collective-permute-start.9 = (f32[128,128]{1,0:T(8,128)S(1)}, f32[128,128]{1,0:T(8,128)S(1)}, u32[]{:S(2)}, u32[]{:S(2)}) collective-permute-start(f32[128,128]{1,0:T(8,128)S(1)} %get-tuple-element.54), channel_id=1, source_target_pairs={{0,32},{32,0},{64,96},{96,64},{1,33},{33,1},{65,97},{97,65},{2,34}... | collective-permute-start | bytes 196616 | tf_op jit(solution)/shard_map/ppermute | solution.py:438
  36.6 6.5 %collective-permute-start.12 = (bf16[128,512]{1,0:T(8,128)(2,1)S(1)}, bf16[128,512]{1,0:T(8,128)(2,1)S(1)}, u32[]{:S(2)}, u32[]{:S(2)}) collective-permute-start(bf16[128,512]{1,0:T(8,128)(2,1)S(1)} %pad_maximum_fusion), channel_id=1, source_target_pairs={{0,8},{4,12},{8,0},{12,4},{16,24},{20,28},{24,16},{28,20},{1,9},{5... | collective-permute-start | bytes 393224 | tf_op jit(solution)/shard_map/ppermute | solution.py:438
  39.0 6.5 %collective-permute-start.11 = (bf16[128,512]{1,0:T(8,128)(2,1)S(1)}, bf16[128,512]{1,0:T(8,128)(2,1)S(1)}, u32[]{:S(2)}, u32[]{:S(2)}) collective-permute-start(bf16[128,512]{1,0:T(8,128)(2,1)S(1)} %pad_maximum_fusion), channel_id=1, source_target_pairs={{0,12},{4,0},{8,4},{12,8},{16,28},{20,16},{24,20},{28,24},{1,13},{... | collective-permute-start | bytes 393224 | tf_op jit(solution)/shard_map/ppermute | solution.py:438
  39.9 5.8 %collective-permute-start.10 = (bf16[128,512]{1,0:T(8,128)(2,1)S(1)}, bf16[128,512]{1,0:T(8,128)(2,1)S(1)}, u32[]{:S(2)}, u32[]{:S(2)}) collective-permute-start(bf16[128,512]{1,0:T(8,128)(2,1)S(1)} %pad_maximum_fusion), channel_id=1, source_target_pairs={{0,4},{4,8},{8,12},{12,0},{16,20},{20,24},{24,28},{28,16},{1,5},{5... | collective-permute-start | bytes 393224 | tf_op jit(solution)/shard_map/ppermute | solution.py:438
  45.8 5.8 %collective-permute-start.15 = (bf16[128,512]{1,0:T(8,128)(2,1)S(1)}, bf16[128,512]{1,0:T(8,128)(2,1)S(1)}, u32[]{:S(2)}, u32[]{:S(2)}) collective-permute-start(bf16[128,512]{1,0:T(8,128)(2,1)S(1)} %add_convert_fusion), channel_id=1, source_target_pairs={{0,16},{4,20},{8,24},{12,28},{16,0},{20,4},{24,8},{28,12},{1,17},{... | collective-permute-start | bytes 393224 | tf_op jit(solution)/shard_map/ppermute | solution.py:438
  49.3 5.5 %collective-permute-start.14 = (bf16[128,512]{1,0:T(8,128)(2,1)S(1)}, bf16[128,512]{1,0:T(8,128)(2,1)S(1)}, u32[]{:S(2)}, u32[]{:S(2)}) collective-permute-start(bf16[128,512]{1,0:T(8,128)(2,1)S(1)} %add_convert_fusion), channel_id=1, source_target_pairs={{0,80},{4,84},{8,88},{12,92},{16,64},{20,68},{24,72},{28,76},{32,1... | collective-permute-start | bytes 393224 | tf_op jit(solution)/shard_map/ppermute | solution.py:438
  49.7 5.1 %collective-permute-start.13 = (bf16[128,512]{1,0:T(8,128)(2,1)S(1)}, bf16[128,512]{1,0:T(8,128)(2,1)S(1)}, u32[]{:S(2)}, u32[]{:S(2)}) collective-permute-start(bf16[128,512]{1,0:T(8,128)(2,1)S(1)} %add_convert_fusion), channel_id=1, source_target_pairs={{0,64},{32,96},{64,0},{96,32},{1,65},{33,97},{65,1},{97,33},{2,66}... | collective-permute-start | bytes 393224 | tf_op jit(solution)/shard_map/ppermute | solution.py:438
  54.8 4.0 %collective-permute-start.16 = (f32[128,512]{1,0:T(8,128)S(1)}, f32[128,512]{1,0:T(8,128)S(1)}, u32[]{:S(2)}, u32[]{:S(2)}) collective-permute-start(f32[128,512]{1,0:T(8,128)S(1)} %add_add_fusion.rows_ref), channel_id=1, source_target_pairs={{0,32},{32,0},{64,96},{96,64},{1,33},{33,1},{65,97},{97,65},{2,34}... | collective-permute-start | bytes 786440 | tf_op jit(solution)/shard_map/ppermute | solution.py:438

commit v5 on v4

--- a/solution.py
+++ b/solution.py
@@ -438,6 +438,19 @@
     return lax.ppermute(value, axis, [(source, target(source)) for source in range(size)])
 
 
+def crossed(value, flip, turn):
+    pairs = []
+    for gz in range(4):
+        for gy in range(8):
+            x, z = gy % 4, (gy // 4) * 2 + gz // 2
+            if gz % 2 == turn:
+                x ^= flip
+            else:
+                z ^= flip
+            pairs.append((gz * 8 + gy, ((z % 2) * 2 + gz % 2) * 8 + (z // 2) * 4 + x))
+    return lax.ppermute(value, ("gz", "gy"), pairs)
+
+
 def four_sum(own, opposite, side, other):
     pair = side.astype(F32) + other.astype(F32)
     return pair + (own.astype(F32) + opposite.astype(F32))
@@ -467,7 +480,6 @@
     w = border_terms(1, *partial, yp, ym)[0]
 
     mate = lambda v: permuted(v, "gz", lambda s: s ^ 1)
-    along_x = lambda v, step: permuted(v, "gy", lambda s: (s // 4) * 4 + (s + step) % 4)
 
     def chip_sum(keep, send):
         return (keep + mate(send)).astype(BF16)
@@ -475,12 +487,8 @@
     near = chip_sum(*contract_near(w, right))
     far = chip_sum(*contract_far(w, [far_low, far_high]))
     chip = jnp.concatenate([near, far], 1)
-    ahead, behind = along_x(chip, 1), along_x(chip, 3)
-    row = four_sum(chip, along_x(chip, 2), ahead, behind).astype(BF16)
-    side = permuted(row, "gz", lambda s: s ^ 2)
-    both = permuted(row, ("gz", "gy"), lambda s: s ^ 20)
-    across = permuted(row, "gy", lambda s: s ^ 4)
-    plane = four_sum(row, across, side, both)
+    row = four_sum(chip, *[crossed(chip, flip, 0) for flip in (2, 1, 3)]).astype(BF16)
+    plane = four_sum(row, *[crossed(row, flip, 1) for flip in (2, 1, 3)])
     scale = 1.0 / math.sqrt(EXT_X * EXT_Y * EXT_Z)
     mine = finish(directions, plane, scale)
     return finish(directions, mate(plane), scale, mine)

time: 60.5 us -> 59.2 us (0.979)
  waiting for transfers between devices: 12.9 us -> 11.7 us
    ppermute x17 -> x11, waiting for transfers between devices: 12.9 us -> 2.88 us  [permuted(): lax.ppermute(value, axis, [(source, target(source)) for source in range(s...]
    ppermute x0 -> x6, waiting for transfers between devices: none -> 8.85 us  [crossed(): return lax.ppermute(value, ('gz', 'gy'), pairs)]
    ppermute x17 -> x11, starting transfers between devices: 27.7 us -> 20.1 us  [permuted(): lax.ppermute(value, axis, [(source, target(source)) for source in range(s...]
    ppermute x0 -> x6, starting transfers between devices: none -> 7.34 us  [crossed(): return lax.ppermute(value, ('gz', 'gy'), pairs)]
  transfers between devices with their start and end apart: 17 -> 17, of which waited for: 7 -> 6; matrix products, arithmetic and copies ran while one was open for 0% -> 0% of each run, Pallas kernels for 26% -> 27%
where the time goes in v5:
time: 59.2 us; the launch traced here: 59 us
  starting transfers between devices  27.5 us (46%)
  Pallas kernels  17.3 us (29%)
  waiting for transfers between devices  11.7 us (20%)
  local copies, waits for them, and re-layouts  2.13 us (4%)
    ppermute x11, starting transfers between devices, permuted(): lax.ppermute(value, axis, [(source, target(source)) for source in range(s...  20.1 us
    ppermute x6, waiting for transfers between devices, crossed(): return lax.ppermute(value, ('gz', 'gy'), pairs)  8.85 us
    ppermute x6, starting transfers between devices, crossed(): return lax.ppermute(value, ('gz', 'gy'), pairs)  7.34 us
    pallas_call x1, Pallas kernels, local_terms(): pl.pallas_call(local_kernel, out_shape=(shape((4, NV, KDIM), BF16),) + (s...  4.9 us
    pallas_call x2, Pallas kernels, border_terms(): pl.pallas_call(functools.partial(border_kernel, mu), out_shape=(shape((4,...  3.37 us
    ppermute x11, waiting for transfers between devices, permuted(): lax.ppermute(value, axis, [(source, target(source)) for source in range(s...  2.88 us
    pallas_call x2, Pallas kernels, finish(): pl.pallas_call(functools.partial(finish_kernel, scale, int(other)), out_s...  2.86 us
    pallas_call x1, Pallas kernels, right_side(): pl.pallas_call(functools.partial(right_kernel, counts), out_shape=shape((...  2.27 us
  transfers between devices with their start and end apart: 17, of which 6 were waited for; matrix products, arithmetic and copies ran while one was open for 0% of the time, Pallas kernels for 27%

profile of v5, /device:TPU:1, one launch (start us, length us, event | category | flops | bytes accessed | tf_op | source)
XLA Modules:
  0.0 59.0 jit_solution(15730911794452677834)
XLA Ops:
  0.0 2.1 %collective-permute-start.3 = (bf16[3072,128]{1,0:T(8,128)(2,1)}, bf16[3072,128]{1,0:T(8,128)(2,1)S(1)}, u32[]{:S(2)}, u32[]{:S(2)}) collective-permute-start(bf16[3072,128]{1,0:T(8,128)(2,1)} %bitcast.2), channel_id=1, source_target_pairs={{0,1},{1,2},{2,3},{3,0},{4,5},{5,6},{6,7},{7,4},{8,9},{9,10},{10,1... | collective-permute-start | bytes 2359304 | tf_op jit(solution)/shard_map/ppermute | solution.py:438
  2.1 1.5 %collective-permute-start.2 = (bf16[3072,128]{1,0:T(8,128)(2,1)}, bf16[3072,128]{1,0:T(8,128)(2,1)S(1)}, u32[]{:S(2)}, u32[]{:S(2)}) collective-permute-start(bf16[3072,128]{1,0:T(8,128)(2,1)} %bitcast.3), channel_id=1, source_target_pairs={{0,3},{1,0},{2,1},{3,2},{4,7},{5,4},{6,5},{7,6},{8,11},{9,8},{10,9... | collective-permute-start | bytes 2359304 | tf_op jit(solution)/shard_map/ppermute | solution.py:438
  3.6 1.2 %copy-done.1 = bf16[64,3,8,2,128]{4,3,2,1,0:T(2,128)(2,1)S(1)} copy-done((bf16[64,3,8,2,128]{4,3,2,1,0:T(2,128)(2,1)S(1)}, bf16[64,3,8,2,128]{4,3,2,1,0:T(2,128)(2,1)}, u32[]{:S(2)}) %copy-start.1) | copy-done | bytes 786456
  4.8 0.9 %copy-done.3 = bf16[3,3,3,8,2,128]{5,4,3,2,1,0:T(2,128)(2,1)S(1)} copy-done((bf16[3,3,3,8,2,128]{5,4,3,2,1,0:T(2,128)(2,1)S(1)}, bf16[3,3,3,8,2,128]{5,4,3,2,1,0:T(2,128)(2,1)}, u32[]{:S(2)}) %copy-start.3) | copy-done | bytes 110616
  5.7 0.6 prepare.1
  6.3 1.1 %collective-permute-start = (bf16[6,64,128]{2,1,0:T(8,128)(2,1)S(1)}, bf16[6,64,128]{2,1,0:T(8,128)(2,1)S(1)}, u32[]{:S(2)}, u32[]{:S(2)}) collective-permute-start(bf16[6,64,128]{2,1,0:T(8,128)(2,1)S(1)} %get-tuple-element.38), channel_id=1, source_target_pairs={{0,96},{32,0},{64,32},{96,64},{1,97},{33,1},{65,33},{97,65},{2,98}... | collective-permute-start | bytes 294920 | tf_op jit(solution)/shard_map/ppermute | solution.py:438
  7.4 5.9 %collective-permute-start.4 = (bf16[24,64,128]{2,1,0:T(8,128)(2,1)S(1)}, bf16[24,64,128]{2,1,0:T(8,128)(2,1)S(1)}, u32[]{:S(2)}, u32[]{:S(2)}) collective-permute-start(bf16[24,64,128]{2,1,0:T(8,128)(2,1)S(1)} %get-tuple-element.47), channel_id=1, source_target_pairs={{0,28},{4,0},{8,4},{12,8},{16,12},{20,16},{24,20},{28,24},{1,29},{... | collective-permute-start | bytes 1179656 | tf_op jit(solution)/shard_map/ppermute | solution.py:438
  13.3 4.9 %local_terms.1 = (bf16[4,64,6144]{2,1,0:T(8,128)(2,1)S(1)}, f32[3,10,4,64,128]{4,3,2,1,0:T(8,128)S(1)}, f32[3,10,4,64,128]{4,3,2,1,0:T(8,128)S(1)}, f32[16,32,12...) custom-call(s32[3]{0:T(128)S(1)} %copy-done.4, ...), custom_call_target="tpu_custom_call" | custom-call | flops 6000000000 | bytes 6000000 | tf_op jit(solution)/shard_map/local_terms/pallas_call | solution.py:205
  18.2 1.1 %collective-permute-start.1 = (bf16[7,64,128]{2,1,0:T(8,128)(2,1)S(1)}, bf16[7,64,128]{2,1,0:T(8,128)(2,1)S(1)}, u32[]{:S(2)}, u32[]{:S(2)}) collective-permute-start(bf16[7,64,128]{2,1,0:T(8,128)(2,1)S(1)} %get-tuple-element.40), channel_id=1, source_target_pairs={{0,32},{32,64},{64,96},{96,0},{1,33},{33,65},{65,97},{97,1},{2,34}... | collective-permute-start | bytes 344072 | tf_op jit(solution)/shard_map/ppermute | solution.py:438
  19.2 1.7 %collective-permute-done.3.refs_2_ = bf16[3072,128]{1,0:T(8,128)(2,1)S(1)} collective-permute-done((bf16[3072,128]{1,0:T(8,128)(2,1)}, bf16[3072,128]{1,0:T(8,128)(2,1)S(1)}, u32[]{:S(2)}, u32[]{:S(2)}) %collective-permute-start.3) | collective-permute-done | bytes 786464 | tf_op jit(solution)/shard_map/ppermute | solution.py:438
  20.9 0.1 collective-permute-start.7
  21.0 2.7 %collective-permute-start.8 = (bf16[1536,128]{1,0:T(8,128)(2,1)S(1)}, bf16[1536,128]{1,0:T(8,128)(2,1)S(1)}, u32[]{:S(2)}, u32[]{:S(2)}) collective-permute-start(bf16[1536,128]{1,0:T(8,128)(2,1)S(1)} %slice.9), channel_id=1, source_target_pairs={{0,3},{1,0},{2,1},{3,2},{4,7},{5,4},{6,5},{7,6},{8,11},{9,8},{10,9... | collective-permute-start | bytes 1179656 | tf_op jit(solution)/shard_map/ppermute | solution.py:438
  23.8 2.3 %right_side.1.right_ref = bf16[384,6144]{1,0:T(8,128)(2,1)S(1)} custom-call(bf16[3072,128]{1,0:T(8,128)(2,1)S(1)} %bitcast.6, bf16[3072,128]{1,0:T(8,128)(2,1)S(1)} %collective-permute-done.2.refs_1_, bf16[3072,128]{1,0:T(8,128)(2,1)S(1)} %collective-permute-done.3.refs_2_), custom_call_target="tpu_custom_call" | custom-call | flops 2000000000 | bytes 4000000 | tf_op jit(solution)/shard_map/right_side/pallas_call | solution.py:332
  26.1 1.6 %border_z.1 = (bf16[4,64,6144]{2,1,0:T(8,128)(2,1)S(1)}, f32[3,10,4,64,128]{4,3,2,1,0:T(8,128)S(1)}, f32[3,10,4,64,128]{4,3,2,1,0:T(8,128)S(1)}, f32[16,32,128]{2,1,0:T(8,128)S(1)}, f32[16,32,128]{2,1,0:T(8,128)S(1)}) custom-call(bf16[4,64,6144]{2,1,0:T(8,128)(2,1)S(1)} %get-tuple-elem, ...), custom_call_target="tpu_custom_call", output_to_operand_aliasing={{0}: (0, {}), {1}: (1, {}), {2}: (2, {}), {3}: (5, {}), {4}... | custom-call | flops 3000000000 | bytes 3000000 | tf_op jit(solution)/shard_map/border_z/pallas_call | solution.py:286
  27.7 1.8 %border_y.1 = (bf16[4,64,6144]{2,1,0:T(8,128)(2,1)S(1)}, f32[3,10,4,64,128]{4,3,2,1,0:T(8,128)S(1)}, f32[3,10,4,64,128]{4,3,2,1,0:T(8,128)S(1)}, f32[16,32,128]{2,1,0:T(8,128)S(1)}, f32[16,32,128]{2,1,0:T(8,128)S(1)}) custom-call(bf16[4,64,6144]{2,1,0:T(8,128)(2,1)S(1)} %get-tuple-elem, ...), custom_call_target="tpu_custom_call", output_to_operand_aliasing={{0}: (0, {}), {1}: (1, {}), {2}: (2, {}), {3}: (5, {}), {4}... | custom-call | flops 3000000000 | bytes 3000000 | tf_op jit(solution)/shard_map/border_y/pallas_call | solution.py:286
  29.5 1.9 %contract_near.1 = (f32[128,384]{1,0:T(8,128)S(1)}, f32[128,384]{1,0:T(8,128)S(1)}) custom-call(bf16[4,64,6144]{2,1,0:T(8,128)(2,1)S(1)} %get-tuple-element.49.w_ref, bf16[384,6144]{1,0:T(8,128)(2,1)S(1)} %right_side.1.right_ref), custom_call_target="tpu_custom_call" | custom-call | flops 1207959552 | bytes 4000000 | tf_op jit(solution)/shard_map/contract_near/pallas_call | solution.py:358
  31.3 2.4 %collective-permute-start.6 = (f32[128,384]{1,0:T(8,128)S(1)}, f32[128,384]{1,0:T(8,128)S(1)}, u32[]{:S(2)}, u32[]{:S(2)}) collective-permute-start(f32[128,384]{1,0:T(8,128)S(1)} %get-tuple-element.52), channel_id=1, source_target_pairs={{0,32},{32,0},{64,96},{96,64},{1,33},{33,1},{65,97},{97,65},{2,34}... | collective-permute-start | bytes 589832 | tf_op jit(solution)/shard_map/ppermute | solution.py:438
  33.7 1.5 %contract_far.1 = (f32[128,128]{1,0:T(8,128)S(1)}, f32[128,128]{1,0:T(8,128)S(1)}) custom-call(bf16[4,64,6144]{2,1,0:T(8,128)(2,1)S(1)} %get-tuple-element.49.w_ref, bf16[1536,128]{1,0:T(8,128)(2,1)S(1)} %collective-permute-done.7.refs_0_, bf16[1536,128]{1,0:T(8,128)(2,1)S(1)} %collective-permute-done.8.refs_1_), custom_call_target="tpu_custom_call" | custom-call | flops 402653184 | bytes 4000000 | tf_op jit(solution)/shard_map/contract_far/pallas_call | solution.py:376
  35.2 0.1 collective-permute-start.9
  35.3 1.2 %collective-permute-done.9 = f32[128,128]{1,0:T(8,128)S(1)} collective-permute-done((f32[128,128]{1,0:T(8,128)S(1)}, f32[128,128]{1,0:T(8,128)S(1)}, u32[]{:S(2)}, u32[]{:S(2)}) %collective-permute-start.9) | collective-permute-done | bytes 65568 | tf_op jit(solution)/shard_map/ppermute | solution.py:438
  36.6 3.4 %collective-permute-start.12 = (bf16[128,512]{1,0:T(8,128)(2,1)S(1)}, bf16[128,512]{1,0:T(8,128)(2,1)S(1)}, u32[]{:S(2)}, u32[]{:S(2)}) collective-permute-start(bf16[128,512]{1,0:T(8,128)(2,1)S(1)} %pad_maximum_fusion), channel_id=1, source_target_pairs={{0,8},{4,12},{8,0},{12,4},{16,24},{20,28},{24,16},{28,20},{32,48},... | collective-permute-start | bytes 393224 | tf_op jit(solution)/shard_map/ppermute | solution.py:451
  40.0 0.4 collective-permute-start.11
  40.3 0.3 collective-permute-start.10
  40.6 2.0 %collective-permute-done.12 = bf16[128,512]{1,0:T(8,128)(2,1)S(1)} collective-permute-done((bf16[128,512]{1,0:T(8,128)(2,1)S(1)}, bf16[128,512]{1,0:T(8,128)(2,1)S(1)}, u32[]{:S(2)}, u32[]{:S(2)}) %collective-permute-start.12) | collective-permute-done | bytes 131104 | tf_op jit(solution)/shard_map/ppermute | solution.py:451
  42.6 2.7 %collective-permute-done.11 = bf16[128,512]{1,0:T(8,128)(2,1)S(1)} collective-permute-done((bf16[128,512]{1,0:T(8,128)(2,1)S(1)}, bf16[128,512]{1,0:T(8,128)(2,1)S(1)}, u32[]{:S(2)}, u32[]{:S(2)}) %collective-permute-start.11) | collective-permute-done | bytes 131104 | tf_op jit(solution)/shard_map/ppermute | solution.py:451
  45.4 2.4 %collective-permute-start.15 = (bf16[128,512]{1,0:T(8,128)(2,1)S(1)}, bf16[128,512]{1,0:T(8,128)(2,1)S(1)}, u32[]{:S(2)}, u32[]{:S(2)}) collective-permute-start(bf16[128,512]{1,0:T(8,128)(2,1)S(1)} %add_convert_fusion), channel_id=1, source_target_pairs={{0,16},{4,20},{8,24},{12,28},{16,0},{20,4},{24,8},{28,12},{32,40},... | collective-permute-start | bytes 393224 | tf_op jit(solution)/shard_map/ppermute | solution.py:451
  47.8 0.9 %collective-permute-start.14 = (bf16[128,512]{1,0:T(8,128)(2,1)S(1)}, bf16[128,512]{1,0:T(8,128)(2,1)S(1)}, u32[]{:S(2)}, u32[]{:S(2)}) collective-permute-start(bf16[128,512]{1,0:T(8,128)(2,1)S(1)} %add_convert_fusion), channel_id=1, source_target_pairs={{0,80},{4,84},{8,88},{12,92},{16,64},{20,68},{24,72},{28,76},{32,4... | collective-permute-start | bytes 393224 | tf_op jit(solution)/shard_map/ppermute | solution.py:451
  48.7 2.4 %collective-permute-done.15 = bf16[128,512]{1,0:T(8,128)(2,1)S(1)} collective-permute-done((bf16[128,512]{1,0:T(8,128)(2,1)S(1)}, bf16[128,512]{1,0:T(8,128)(2,1)S(1)}, u32[]{:S(2)}, u32[]{:S(2)}) %collective-permute-start.15) | collective-permute-done | bytes 131104 | tf_op jit(solution)/shard_map/ppermute | solution.py:451
  51.1 1.8 %collective-permute-done.14 = bf16[128,512]{1,0:T(8,128)(2,1)S(1)} collective-permute-done((bf16[128,512]{1,0:T(8,128)(2,1)S(1)}, bf16[128,512]{1,0:T(8,128)(2,1)S(1)}, u32[]{:S(2)}, u32[]{:S(2)}) %collective-permute-start.14) | collective-permute-done | bytes 131104 | tf_op jit(solution)/shard_map/ppermute | solution.py:451
  52.9 3.2 %collective-permute-start.16 = (f32[128,512]{1,0:T(8,128)S(1)}, f32[128,512]{1,0:T(8,128)S(1)}, u32[]{:S(2)}, u32[]{:S(2)}) collective-permute-start(f32[128,512]{1,0:T(8,128)S(1)} %add_add_fusion.rows_ref), channel_id=1, source_target_pairs={{0,32},{32,0},{64,96},{96,64},{1,33},{33,1},{65,97},{97,65},{2,34}... | collective-permute-start | bytes 786440 | tf_op jit(solution)/shard_map/ppermute | solution.py:438
  56.1 1.4 %finish_mine.1.refs_0_ = f32[4,2,64,256]{3,2,1,0:T(8,128)} custom-call(s32[3]{0:T(128)S(1)} %copy-done, f32[128,512]{1,0:T(8,128)S(1)} %add_add_fusion.rows_ref), custom_call_target="tpu_custom_call" | custom-call | flops 200000 | bytes 1000000 | tf_op jit(solution)/shard_map/finish_mine/pallas_call | solution.py:423
  57.6 1.4 %finish_other.1 = f32[4,2,64,256]{3,2,1,0:T(8,128)} custom-call(s32[3]{0:T(128)S(1)} %copy-done, f32[128,512]{1,0:T(8,128)S(1)} %collective-permute-done.16.rows_ref, f32[4,2,64,256]{3,2,1,0:T(8,128)} %finish_mine.1.refs_0_), custom_call_target="tpu_custom_call", output_to_operand_aliasing={{}: (2, {})} | custom-call | flops 200000 | bytes 1000000 | tf_op jit(solution)/shard_map/finish_other/pallas_call | solution.py:423
  (28 shorter events, 0.3 us)
Async XLA Ops:
  0.0 13.3 %copy-start.4 = (s32[3]{0:T(128)S(1)}, s32[3]{0:T(128)}, u32[]{:S(2)}) copy-start(s32[3]{0:T(128)} %momentum_ref.1) | copy-start | bytes 40
  0.0 20.9 %collective-permute-start.3 = (bf16[3072,128]{1,0:T(8,128)(2,1)}, bf16[3072,128]{1,0:T(8,128)(2,1)S(1)}, u32[]{:S(2)}, u32[]{:S(2)}) collective-permute-start(bf16[3072,128]{1,0:T(8,128)(2,1)} %bitcast.2), channel_id=1, source_target_pairs={{0,1},{1,2},{2,3},{3,0},{4,5},{5,6},{6,7},{7,4},{8,9},{9,10},{10,1... | collective-permute-start | bytes 2359304 | tf_op jit(solution)/shard_map/ppermute | solution.py:438
  2.1 18.9 %collective-permute-start.2 = (bf16[3072,128]{1,0:T(8,128)(2,1)}, bf16[3072,128]{1,0:T(8,128)(2,1)S(1)}, u32[]{:S(2)}, u32[]{:S(2)}) collective-permute-start(bf16[3072,128]{1,0:T(8,128)(2,1)} %bitcast.3), channel_id=1, source_target_pairs={{0,3},{1,0},{2,1},{3,2},{4,7},{5,4},{6,5},{7,6},{8,11},{9,8},{10,9... | collective-permute-start | bytes 2359304 | tf_op jit(solution)/shard_map/ppermute | solution.py:438
  3.6 1.2 %copy-start.1 = (bf16[64,3,8,2,128]{4,3,2,1,0:T(2,128)(2,1)S(1)}, bf16[64,3,8,2,128]{4,3,2,1,0:T(2,128)(2,1)}, u32[]{:S(2)}) copy-start(bf16[64,3,8,2,128]{4,3,2,1,0:T(2,128)(2,1)} %param.4) | copy-start | bytes 2359300
  4.8 0.9 %copy-start.3 = (bf16[3,3,3,8,2,128]{5,4,3,2,1,0:T(2,128)(2,1)S(1)}, bf16[3,3,3,8,2,128]{5,4,3,2,1,0:T(2,128)(2,1)}, u32[]{:S(2)}) copy-start(bf16[3,3,3,8,2,128]{5,4,3,2,1,0:T(2,128)(2,1)} %param.5) | copy-start | bytes 331780
  5.7 7.6 %copy-start.2 = (bf16[64,3,8,2,128]{4,3,2,1,0:T(2,128)(2,1)S(1)}, bf16[64,3,8,2,128]{4,3,2,1,0:T(2,128)(2,1)}, u32[]{:S(2)}) copy-start(bf16[64,3,8,2,128]{4,3,2,1,0:T(2,128)(2,1)} %param.4) | copy-start | bytes 2359300
  6.3 11.9 %collective-permute-start = (bf16[6,64,128]{2,1,0:T(8,128)(2,1)S(1)}, bf16[6,64,128]{2,1,0:T(8,128)(2,1)S(1)}, u32[]{:S(2)}, u32[]{:S(2)}) collective-permute-start(bf16[6,64,128]{2,1,0:T(8,128)(2,1)S(1)} %get-tuple-element.38), channel_id=1, source_target_pairs={{0,96},{32,0},{64,32},{96,64},{1,97},{33,1},{65,33},{97,65},{2,98}... | collective-permute-start | bytes 294920 | tf_op jit(solution)/shard_map/ppermute | solution.py:438
  7.4 20.3 %collective-permute-start.4 = (bf16[24,64,128]{2,1,0:T(8,128)(2,1)S(1)}, bf16[24,64,128]{2,1,0:T(8,128)(2,1)S(1)}, u32[]{:S(2)}, u32[]{:S(2)}) collective-permute-start(bf16[24,64,128]{2,1,0:T(8,128)(2,1)S(1)} %get-tuple-element.47), channel_id=1, source_target_pairs={{0,28},{4,0},{8,4},{12,8},{16,12},{20,16},{24,20},{28,24},{1,29},{... | collective-permute-start | bytes 1179656 | tf_op jit(solution)/shard_map/ppermute | solution.py:438
  13.2 14.4 %collective-permute-start.5 = (bf16[26,64,128]{2,1,0:T(8,128)(2,1)S(1)}, bf16[26,64,128]{2,1,0:T(8,128)(2,1)S(1)}, u32[]{:S(2)}, u32[]{:S(2)}) collective-permute-start(bf16[26,64,128]{2,1,0:T(8,128)(2,1)S(1)} %get-tuple-element.48), channel_id=1, source_target_pairs={{0,4},{4,8},{8,12},{12,16},{16,20},{20,24},{24,28},{28,0},{1,5},{5... | collective-permute-start | bytes 1277960 | tf_op jit(solution)/shard_map/ppermute | solution.py:438
  18.2 7.9 %collective-permute-start.1 = (bf16[7,64,128]{2,1,0:T(8,128)(2,1)S(1)}, bf16[7,64,128]{2,1,0:T(8,128)(2,1)S(1)}, u32[]{:S(2)}, u32[]{:S(2)}) collective-permute-start(bf16[7,64,128]{2,1,0:T(8,128)(2,1)S(1)} %get-tuple-element.40), channel_id=1, source_target_pairs={{0,32},{32,64},{64,96},{96,0},{1,33},{33,65},{65,97},{97,1},{2,34}... | collective-permute-start | bytes 344072 | tf_op jit(solution)/shard_map/ppermute | solution.py:438
  20.9 12.8 %collective-permute-start.7 = (bf16[1536,128]{1,0:T(8,128)(2,1)S(1)}, bf16[1536,128]{1,0:T(8,128)(2,1)S(1)}, u32[]{:S(2)}, u32[]{:S(2)}) collective-permute-start(bf16[1536,128]{1,0:T(8,128)(2,1)S(1)} %slice.8), channel_id=1, source_target_pairs={{0,1},{1,2},{2,3},{3,0},{4,5},{5,6},{6,7},{7,4},{8,9},{9,10},{10,1... | collective-permute-start | bytes 1179656 | tf_op jit(solution)/shard_map/ppermute | solution.py:438
  21.0 12.7 %collective-permute-start.8 = (bf16[1536,128]{1,0:T(8,128)(2,1)S(1)}, bf16[1536,128]{1,0:T(8,128)(2,1)S(1)}, u32[]{:S(2)}, u32[]{:S(2)}) collective-permute-start(bf16[1536,128]{1,0:T(8,128)(2,1)S(1)} %slice.9), channel_id=1, source_target_pairs={{0,3},{1,0},{2,1},{3,2},{4,7},{5,4},{6,5},{7,6},{8,11},{9,8},{10,9... | collective-permute-start | bytes 1179656 | tf_op jit(solution)/shard_map/ppermute | solution.py:438
  31.3 24.8 %copy-start = (s32[3]{0:T(128)S(1)}, s32[3]{0:T(128)}, u32[]{:S(2)}) copy-start(s32[3]{0:T(128)} %dirs_ref.3) | copy-start | bytes 40
  31.3 4.0 %collective-permute-start.6 = (f32[128,384]{1,0:T(8,128)S(1)}, f32[128,384]{1,0:T(8,128)S(1)}, u32[]{:S(2)}, u32[]{:S(2)}) collective-permute-start(f32[128,384]{1,0:T(8,128)S(1)} %get-tuple-element.52), channel_id=1, source_target_pairs={{0,32},{32,0},{64,96},{96,64},{1,33},{33,1},{65,97},{97,65},{2,34}... | collective-permute-start | bytes 589832 | tf_op jit(solution)/shard_map/ppermute | solution.py:438
  35.2 1.3 %collective-permute-start.9 = (f32[128,128]{1,0:T(8,128)S(1)}, f32[128,128]{1,0:T(8,128)S(1)}, u32[]{:S(2)}, u32[]{:S(2)}) collective-permute-start(f32[128,128]{1,0:T(8,128)S(1)} %get-tuple-element.54), channel_id=1, source_target_pairs={{0,32},{32,0},{64,96},{96,64},{1,33},{33,1},{65,97},{97,65},{2,34}... | collective-permute-start | bytes 196616 | tf_op jit(solution)/shard_map/ppermute | solution.py:438
  36.6 6.0 %collective-permute-start.12 = (bf16[128,512]{1,0:T(8,128)(2,1)S(1)}, bf16[128,512]{1,0:T(8,128)(2,1)S(1)}, u32[]{:S(2)}, u32[]{:S(2)}) collective-permute-start(bf16[128,512]{1,0:T(8,128)(2,1)S(1)} %pad_maximum_fusion), channel_id=1, source_target_pairs={{0,8},{4,12},{8,0},{12,4},{16,24},{20,28},{24,16},{28,20},{32,48},... | collective-permute-start | bytes 393224 | tf_op jit(solution)/shard_map/ppermute | solution.py:451
  40.0 5.3 %collective-permute-start.11 = (bf16[128,512]{1,0:T(8,128)(2,1)S(1)}, bf16[128,512]{1,0:T(8,128)(2,1)S(1)}, u32[]{:S(2)}, u32[]{:S(2)}) collective-permute-start(bf16[128,512]{1,0:T(8,128)(2,1)S(1)} %pad_maximum_fusion), channel_id=1, source_target_pairs={{0,12},{4,8},{8,4},{12,0},{16,28},{20,24},{24,20},{28,16},{32,112}... | collective-permute-start | bytes 393224 | tf_op jit(solution)/shard_map/ppermute | solution.py:451
  40.3 5.0 %collective-permute-start.10 = (bf16[128,512]{1,0:T(8,128)(2,1)S(1)}, bf16[128,512]{1,0:T(8,128)(2,1)S(1)}, u32[]{:S(2)}, u32[]{:S(2)}) collective-permute-start(bf16[128,512]{1,0:T(8,128)(2,1)S(1)} %pad_maximum_fusion), channel_id=1, source_target_pairs={{0,4},{4,0},{8,12},{12,8},{16,20},{20,16},{24,28},{28,24},{32,96},... | collective-permute-start | bytes 393224 | tf_op jit(solution)/shard_map/ppermute | solution.py:451
  45.4 5.7 %collective-permute-start.15 = (bf16[128,512]{1,0:T(8,128)(2,1)S(1)}, bf16[128,512]{1,0:T(8,128)(2,1)S(1)}, u32[]{:S(2)}, u32[]{:S(2)}) collective-permute-start(bf16[128,512]{1,0:T(8,128)(2,1)S(1)} %add_convert_fusion), channel_id=1, source_target_pairs={{0,16},{4,20},{8,24},{12,28},{16,0},{20,4},{24,8},{28,12},{32,40},... | collective-permute-start | bytes 393224 | tf_op jit(solution)/shard_map/ppermute | solution.py:451
  47.8 5.0 %collective-permute-start.14 = (bf16[128,512]{1,0:T(8,128)(2,1)S(1)}, bf16[128,512]{1,0:T(8,128)(2,1)S(1)}, u32[]{:S(2)}, u32[]{:S(2)}) collective-permute-start(bf16[128,512]{1,0:T(8,128)(2,1)S(1)} %add_convert_fusion), channel_id=1, source_target_pairs={{0,80},{4,84},{8,88},{12,92},{16,64},{20,68},{24,72},{28,76},{32,4... | collective-permute-start | bytes 393224 | tf_op jit(solution)/shard_map/ppermute | solution.py:451
  48.7 4.2 %collective-permute-start.13 = (bf16[128,512]{1,0:T(8,128)(2,1)S(1)}, bf16[128,512]{1,0:T(8,128)(2,1)S(1)}, u32[]{:S(2)}, u32[]{:S(2)}) collective-permute-start(bf16[128,512]{1,0:T(8,128)(2,1)S(1)} %add_convert_fusion), channel_id=1, source_target_pairs={{0,64},{4,68},{8,72},{12,76},{16,80},{20,84},{24,88},{28,92},{32,3... | collective-permute-start | bytes 393224 | tf_op jit(solution)/shard_map/ppermute | solution.py:451
  52.9 4.6 %collective-permute-start.16 = (f32[128,512]{1,0:T(8,128)S(1)}, f32[128,512]{1,0:T(8,128)S(1)}, u32[]{:S(2)}, u32[]{:S(2)}) collective-permute-start(f32[128,512]{1,0:T(8,128)S(1)} %add_add_fusion.rows_ref), channel_id=1, source_target_pairs={{0,32},{32,0},{64,96},{96,64},{1,33},{33,1},{65,97},{97,65},{2,34}... | collective-permute-start | bytes 786440 | tf_op jit(solution)/shard_map/ppermute | solution.py:438

commit v6 on v5

--- a/solution.py
+++ b/solution.py
@@ -134,8 +134,8 @@
     frac_y = ((momentum_ref[1] * y) & (EXT_Y - 1)).astype(F32) / EXT_Y
     frac_z = ((momentum_ref[2] * z) & (EXT_Z - 1)).astype(F32) / EXT_Z
     angle = 2.0 * math.pi * (frac_z + frac_y + frac_x)
-    cos_ref[...] = jnp.cos(angle)
-    sin_ref[...] = -sign * jnp.sin(angle)
+    cos_ref[0:NZY, :] = jnp.cos(angle)
+    sin_ref[0:NZY, :] = -sign * jnp.sin(angle)
 
     wide[...] = v_ref[...].astype(F32)
     for c in range(COL):
@@ -145,7 +145,8 @@
                 ext[c, z + 1, y + 1] = tile
                 exts[c, z + 1, y + 1] = pltpu.roll(tile, HALF, 1)
 
-    lwide[...] = l_ref[...].astype(F32)
+    lwide[0:432, :] = l_ref[...].astype(F32)
+    lwide[432:LINES, :] = jnp.zeros((LINES - 432, LANES), F32)
     re, im = line_coefficients(lwide[...], first)
     real[...] = re
     imag[...] = im
@@ -197,11 +198,12 @@
 
 
 EXTENDED = (COL, DZ + 2, HY + 2, NV, LANES)
-TABLE = (NZY, 32, LANES)
+TABLE = (NZY, 40, LANES)
+LINES = 576
 
 
 def local_terms(momentum, rows, link_rows):
-    line = pltpu.VMEM((27 * NZY, LANES), F32)
+    line = pltpu.VMEM((LINES, LANES), F32)
     return pl.pallas_call(
         local_kernel,
         out_shape=(shape((4, NV, KDIM), BF16),)
@@ -214,8 +216,8 @@
             line,
             line,
             line,
-            pltpu.VMEM((NZY, LANES), F32),
-            pltpu.VMEM((NZY, LANES), F32),
+            pltpu.VMEM((NZY + 8, LANES), F32),
+            pltpu.VMEM((NZY + 8, LANES), F32),
         ],
         compiler_params=params(8),
         cost_estimate=pl.CostEstimate(flops=6000000000, bytes_accessed=6000000, transcendentals=0),

time: 59.2 us -> 59.2 us (level)
  no operation moved by 1% of the time
where the time goes in v6:
time: 59.2 us; the launch traced here: 59 us
  starting transfers between devices  27.5 us (46%)
  Pallas kernels  17.3 us (29%)
  waiting for transfers between devices  11.7 us (20%)
  local copies, waits for them, and re-layouts  2.13 us (4%)
    ppermute x11, starting transfers between devices, permuted(): lax.ppermute(value, axis, [(source, target(source)) for source in range(s...  20.2 us
    ppermute x6, waiting for transfers between devices, crossed(): return lax.ppermute(value, ('gz', 'gy'), pairs)  8.84 us
    ppermute x6, starting transfers between devices, crossed(): return lax.ppermute(value, ('gz', 'gy'), pairs)  7.35 us
    pallas_call x1, Pallas kernels, local_terms(): pl.pallas_call(local_kernel, out_shape=(shape((4, NV, KDIM), BF16),) + (s...  4.92 us
    pallas_call x2, Pallas kernels, border_terms(): pl.pallas_call(functools.partial(border_kernel, mu), out_shape=(shape((4,...  3.33 us
    pallas_call x2, Pallas kernels, finish(): pl.pallas_call(functools.partial(finish_kernel, scale, int(other)), out_s...  2.86 us
    ppermute x11, waiting for transfers between devices, permuted(): lax.ppermute(value, axis, [(source, target(source)) for source in range(s...  2.86 us
    pallas_call x1, Pallas kernels, right_side(): pl.pallas_call(functools.partial(right_kernel, counts), out_shape=shape((...  2.27 us
  transfers between devices with their start and end apart: 17, of which 6 were waited for; matrix products, arithmetic and copies ran while one was open for 0% of the time, Pallas kernels for 27%

profile of v6, /device:TPU:1, one launch (start us, length us, event | category | flops | bytes accessed | tf_op | source)
XLA Modules:
  0.0 59.0 jit_solution(6213066045170788108)
XLA Ops:
  0.0 2.1 %collective-permute-start.3 = (bf16[3072,128]{1,0:T(8,128)(2,1)}, bf16[3072,128]{1,0:T(8,128)(2,1)S(1)}, u32[]{:S(2)}, u32[]{:S(2)}) collective-permute-start(bf16[3072,128]{1,0:T(8,128)(2,1)} %bitcast.2), channel_id=1, source_target_pairs={{0,1},{1,2},{2,3},{3,0},{4,5},{5,6},{6,7},{7,4},{8,9},{9,10},{10,1... | collective-permute-start | bytes 2359304 | tf_op jit(solution)/shard_map/ppermute | solution.py:440
  2.1 1.5 %collective-permute-start.2 = (bf16[3072,128]{1,0:T(8,128)(2,1)}, bf16[3072,128]{1,0:T(8,128)(2,1)S(1)}, u32[]{:S(2)}, u32[]{:S(2)}) collective-permute-start(bf16[3072,128]{1,0:T(8,128)(2,1)} %bitcast.3), channel_id=1, source_target_pairs={{0,3},{1,0},{2,1},{3,2},{4,7},{5,4},{6,5},{7,6},{8,11},{9,8},{10,9... | collective-permute-start | bytes 2359304 | tf_op jit(solution)/shard_map/ppermute | solution.py:440
  3.6 1.2 %copy-done.1 = bf16[64,3,8,2,128]{4,3,2,1,0:T(2,128)(2,1)S(1)} copy-done((bf16[64,3,8,2,128]{4,3,2,1,0:T(2,128)(2,1)S(1)}, bf16[64,3,8,2,128]{4,3,2,1,0:T(2,128)(2,1)}, u32[]{:S(2)}) %copy-start.1) | copy-done | bytes 786456
  4.8 0.9 %copy-done.3 = bf16[3,3,3,8,2,128]{5,4,3,2,1,0:T(2,128)(2,1)S(1)} copy-done((bf16[3,3,3,8,2,128]{5,4,3,2,1,0:T(2,128)(2,1)S(1)}, bf16[3,3,3,8,2,128]{5,4,3,2,1,0:T(2,128)(2,1)}, u32[]{:S(2)}) %copy-start.3) | copy-done | bytes 110616
  5.7 0.6 prepare.1
  6.3 1.1 %collective-permute-start = (bf16[6,64,128]{2,1,0:T(8,128)(2,1)S(1)}, bf16[6,64,128]{2,1,0:T(8,128)(2,1)S(1)}, u32[]{:S(2)}, u32[]{:S(2)}) collective-permute-start(bf16[6,64,128]{2,1,0:T(8,128)(2,1)S(1)} %get-tuple-element.38), channel_id=1, source_target_pairs={{0,96},{32,0},{64,32},{96,64},{1,97},{33,1},{65,33},{97,65},{2,98}... | collective-permute-start | bytes 294920 | tf_op jit(solution)/shard_map/ppermute | solution.py:440
  7.4 5.9 %collective-permute-start.4 = (bf16[24,64,128]{2,1,0:T(8,128)(2,1)S(1)}, bf16[24,64,128]{2,1,0:T(8,128)(2,1)S(1)}, u32[]{:S(2)}, u32[]{:S(2)}) collective-permute-start(bf16[24,64,128]{2,1,0:T(8,128)(2,1)S(1)} %get-tuple-element.47), channel_id=1, source_target_pairs={{0,28},{4,0},{8,4},{12,8},{16,12},{20,16},{24,20},{28,24},{1,29},{... | collective-permute-start | bytes 1179656 | tf_op jit(solution)/shard_map/ppermute | solution.py:440
  13.3 4.9 %local_terms.1 = (bf16[4,64,6144]{2,1,0:T(8,128)(2,1)S(1)}, f32[3,10,4,64,128]{4,3,2,1,0:T(8,128)S(1)}, f32[3,10,4,64,128]{4,3,2,1,0:T(8,128)S(1)}, f32[16,40,12...) custom-call(s32[3]{0:T(128)S(1)} %copy-done.4, ...), custom_call_target="tpu_custom_call" | custom-call | flops 6000000000 | bytes 6000000 | tf_op jit(solution)/shard_map/local_terms/pallas_call | solution.py:207
  18.2 1.1 %collective-permute-start.1 = (bf16[7,64,128]{2,1,0:T(8,128)(2,1)S(1)}, bf16[7,64,128]{2,1,0:T(8,128)(2,1)S(1)}, u32[]{:S(2)}, u32[]{:S(2)}) collective-permute-start(bf16[7,64,128]{2,1,0:T(8,128)(2,1)S(1)} %get-tuple-element.40), channel_id=1, source_target_pairs={{0,32},{32,64},{64,96},{96,0},{1,33},{33,65},{65,97},{97,1},{2,34}... | collective-permute-start | bytes 344072 | tf_op jit(solution)/shard_map/ppermute | solution.py:440
  19.2 1.6 %collective-permute-done.3.refs_2_ = bf16[3072,128]{1,0:T(8,128)(2,1)S(1)} collective-permute-done((bf16[3072,128]{1,0:T(8,128)(2,1)}, bf16[3072,128]{1,0:T(8,128)(2,1)S(1)}, u32[]{:S(2)}, u32[]{:S(2)}) %collective-permute-start.3) | collective-permute-done | bytes 786464 | tf_op jit(solution)/shard_map/ppermute | solution.py:440
  20.9 0.1 collective-permute-start.7
  21.0 2.7 %collective-permute-start.8 = (bf16[1536,128]{1,0:T(8,128)(2,1)S(1)}, bf16[1536,128]{1,0:T(8,128)(2,1)S(1)}, u32[]{:S(2)}, u32[]{:S(2)}) collective-permute-start(bf16[1536,128]{1,0:T(8,128)(2,1)S(1)} %slice.9), channel_id=1, source_target_pairs={{0,3},{1,0},{2,1},{3,2},{4,7},{5,4},{6,5},{7,6},{8,11},{9,8},{10,9... | collective-permute-start | bytes 1179656 | tf_op jit(solution)/shard_map/ppermute | solution.py:440
  23.8 2.3 %right_side.1.right_ref = bf16[384,6144]{1,0:T(8,128)(2,1)S(1)} custom-call(bf16[3072,128]{1,0:T(8,128)(2,1)S(1)} %bitcast.6, bf16[3072,128]{1,0:T(8,128)(2,1)S(1)} %collective-permute-done.2.refs_1_, bf16[3072,128]{1,0:T(8,128)(2,1)S(1)} %collective-permute-done.3.refs_2_), custom_call_target="tpu_custom_call" | custom-call | flops 2000000000 | bytes 4000000 | tf_op jit(solution)/shard_map/right_side/pallas_call | solution.py:334
  26.1 1.6 %border_z.1 = (bf16[4,64,6144]{2,1,0:T(8,128)(2,1)S(1)}, f32[3,10,4,64,128]{4,3,2,1,0:T(8,128)S(1)}, f32[3,10,4,64,128]{4,3,2,1,0:T(8,128)S(1)}, f32[16,40,128]{2,1,0:T(8,128)S(1)}, f32[16,40,128]{2,1,0:T(8,128)S(1)}) custom-call(bf16[4,64,6144]{2,1,0:T(8,128)(2,1)S(1)} %get-tuple-elem, ...), custom_call_target="tpu_custom_call", output_to_operand_aliasing={{0}: (0, {}), {1}: (1, {}), {2}: (2, {}), {3}: (5, {}), {4}... | custom-call | flops 3000000000 | bytes 3000000 | tf_op jit(solution)/shard_map/border_z/pallas_call | solution.py:288
  27.7 1.8 %border_y.1 = (bf16[4,64,6144]{2,1,0:T(8,128)(2,1)S(1)}, f32[3,10,4,64,128]{4,3,2,1,0:T(8,128)S(1)}, f32[3,10,4,64,128]{4,3,2,1,0:T(8,128)S(1)}, f32[16,40,128]{2,1,0:T(8,128)S(1)}, f32[16,40,128]{2,1,0:T(8,128)S(1)}) custom-call(bf16[4,64,6144]{2,1,0:T(8,128)(2,1)S(1)} %get-tuple-elem, ...), custom_call_target="tpu_custom_call", output_to_operand_aliasing={{0}: (0, {}), {1}: (1, {}), {2}: (2, {}), {3}: (5, {}), {4}... | custom-call | flops 3000000000 | bytes 3000000 | tf_op jit(solution)/shard_map/border_y/pallas_call | solution.py:288
  29.4 1.9 %contract_near.1 = (f32[128,384]{1,0:T(8,128)S(1)}, f32[128,384]{1,0:T(8,128)S(1)}) custom-call(bf16[4,64,6144]{2,1,0:T(8,128)(2,1)S(1)} %get-tuple-element.49.w_ref, bf16[384,6144]{1,0:T(8,128)(2,1)S(1)} %right_side.1.right_ref), custom_call_target="tpu_custom_call" | custom-call | flops 1207959552 | bytes 4000000 | tf_op jit(solution)/shard_map/contract_near/pallas_call | solution.py:360
  31.3 2.4 %collective-permute-start.6 = (f32[128,384]{1,0:T(8,128)S(1)}, f32[128,384]{1,0:T(8,128)S(1)}, u32[]{:S(2)}, u32[]{:S(2)}) collective-permute-start(f32[128,384]{1,0:T(8,128)S(1)} %get-tuple-element.52), channel_id=1, source_target_pairs={{0,32},{32,0},{64,96},{96,64},{1,33},{33,1},{65,97},{97,65},{2,34}... | collective-permute-start | bytes 589832 | tf_op jit(solution)/shard_map/ppermute | solution.py:440
  33.7 1.5 %contract_far.1 = (f32[128,128]{1,0:T(8,128)S(1)}, f32[128,128]{1,0:T(8,128)S(1)}) custom-call(bf16[4,64,6144]{2,1,0:T(8,128)(2,1)S(1)} %get-tuple-element.49.w_ref, bf16[1536,128]{1,0:T(8,128)(2,1)S(1)} %collective-permute-done.7.refs_0_, bf16[1536,128]{1,0:T(8,128)(2,1)S(1)} %collective-permute-done.8.refs_1_), custom_call_target="tpu_custom_call" | custom-call | flops 402653184 | bytes 4000000 | tf_op jit(solution)/shard_map/contract_far/pallas_call | solution.py:378
  35.2 0.1 collective-permute-start.9
  35.3 1.2 %collective-permute-done.9 = f32[128,128]{1,0:T(8,128)S(1)} collective-permute-done((f32[128,128]{1,0:T(8,128)S(1)}, f32[128,128]{1,0:T(8,128)S(1)}, u32[]{:S(2)}, u32[]{:S(2)}) %collective-permute-start.9) | collective-permute-done | bytes 65568 | tf_op jit(solution)/shard_map/ppermute | solution.py:440
  36.5 3.4 %collective-permute-start.12 = (bf16[128,512]{1,0:T(8,128)(2,1)S(1)}, bf16[128,512]{1,0:T(8,128)(2,1)S(1)}, u32[]{:S(2)}, u32[]{:S(2)}) collective-permute-start(bf16[128,512]{1,0:T(8,128)(2,1)S(1)} %pad_maximum_fusion), channel_id=1, source_target_pairs={{0,8},{4,12},{8,0},{12,4},{16,24},{20,28},{24,16},{28,20},{32,48},... | collective-permute-start | bytes 393224 | tf_op jit(solution)/shard_map/ppermute | solution.py:453
  39.9 0.4 collective-permute-start.11
  40.3 0.3 collective-permute-start.10
  40.6 2.0 %collective-permute-done.12 = bf16[128,512]{1,0:T(8,128)(2,1)S(1)} collective-permute-done((bf16[128,512]{1,0:T(8,128)(2,1)S(1)}, bf16[128,512]{1,0:T(8,128)(2,1)S(1)}, u32[]{:S(2)}, u32[]{:S(2)}) %collective-permute-start.12) | collective-permute-done | bytes 131104 | tf_op jit(solution)/shard_map/ppermute | solution.py:453
  42.6 2.7 %collective-permute-done.11 = bf16[128,512]{1,0:T(8,128)(2,1)S(1)} collective-permute-done((bf16[128,512]{1,0:T(8,128)(2,1)S(1)}, bf16[128,512]{1,0:T(8,128)(2,1)S(1)}, u32[]{:S(2)}, u32[]{:S(2)}) %collective-permute-start.11) | collective-permute-done | bytes 131104 | tf_op jit(solution)/shard_map/ppermute | solution.py:453
  45.3 2.4 %collective-permute-start.15 = (bf16[128,512]{1,0:T(8,128)(2,1)S(1)}, bf16[128,512]{1,0:T(8,128)(2,1)S(1)}, u32[]{:S(2)}, u32[]{:S(2)}) collective-permute-start(bf16[128,512]{1,0:T(8,128)(2,1)S(1)} %add_convert_fusion), channel_id=1, source_target_pairs={{0,16},{4,20},{8,24},{12,28},{16,0},{20,4},{24,8},{28,12},{32,40},... | collective-permute-start | bytes 393224 | tf_op jit(solution)/shard_map/ppermute | solution.py:453
  47.8 0.9 %collective-permute-start.14 = (bf16[128,512]{1,0:T(8,128)(2,1)S(1)}, bf16[128,512]{1,0:T(8,128)(2,1)S(1)}, u32[]{:S(2)}, u32[]{:S(2)}) collective-permute-start(bf16[128,512]{1,0:T(8,128)(2,1)S(1)} %add_convert_fusion), channel_id=1, source_target_pairs={{0,80},{4,84},{8,88},{12,92},{16,64},{20,68},{24,72},{28,76},{32,4... | collective-permute-start | bytes 393224 | tf_op jit(solution)/shard_map/ppermute | solution.py:453
  48.6 2.4 %collective-permute-done.15 = bf16[128,512]{1,0:T(8,128)(2,1)S(1)} collective-permute-done((bf16[128,512]{1,0:T(8,128)(2,1)S(1)}, bf16[128,512]{1,0:T(8,128)(2,1)S(1)}, u32[]{:S(2)}, u32[]{:S(2)}) %collective-permute-start.15) | collective-permute-done | bytes 131104 | tf_op jit(solution)/shard_map/ppermute | solution.py:453
  51.0 1.8 %collective-permute-done.14 = bf16[128,512]{1,0:T(8,128)(2,1)S(1)} collective-permute-done((bf16[128,512]{1,0:T(8,128)(2,1)S(1)}, bf16[128,512]{1,0:T(8,128)(2,1)S(1)}, u32[]{:S(2)}, u32[]{:S(2)}) %collective-permute-start.14) | collective-permute-done | bytes 131104 | tf_op jit(solution)/shard_map/ppermute | solution.py:453
  52.9 3.2 %collective-permute-start.16 = (f32[128,512]{1,0:T(8,128)S(1)}, f32[128,512]{1,0:T(8,128)S(1)}, u32[]{:S(2)}, u32[]{:S(2)}) collective-permute-start(f32[128,512]{1,0:T(8,128)S(1)} %add_add_fusion.rows_ref), channel_id=1, source_target_pairs={{0,32},{32,0},{64,96},{96,64},{1,33},{33,1},{65,97},{97,65},{2,34}... | collective-permute-start | bytes 786440 | tf_op jit(solution)/shard_map/ppermute | solution.py:440
  56.1 1.4 %finish_mine.1.refs_0_ = f32[4,2,64,256]{3,2,1,0:T(8,128)} custom-call(s32[3]{0:T(128)S(1)} %copy-done, f32[128,512]{1,0:T(8,128)S(1)} %add_add_fusion.rows_ref), custom_call_target="tpu_custom_call" | custom-call | flops 200000 | bytes 1000000 | tf_op jit(solution)/shard_map/finish_mine/pallas_call | solution.py:425
  57.6 1.4 %finish_other.1 = f32[4,2,64,256]{3,2,1,0:T(8,128)} custom-call(s32[3]{0:T(128)S(1)} %copy-done, f32[128,512]{1,0:T(8,128)S(1)} %collective-permute-done.16.rows_ref, f32[4,2,64,256]{3,2,1,0:T(8,128)} %finish_mine.1.refs_0_), custom_call_target="tpu_custom_call", output_to_operand_aliasing={{}: (2, {})} | custom-call | flops 200000 | bytes 1000000 | tf_op jit(solution)/shard_map/finish_other/pallas_call | solution.py:425
  (28 shorter events, 0.3 us)
Async XLA Ops:
  0.0 13.3 %copy-start.4 = (s32[3]{0:T(128)S(1)}, s32[3]{0:T(128)}, u32[]{:S(2)}) copy-start(s32[3]{0:T(128)} %momentum_ref.1) | copy-start | bytes 40
  0.0 20.9 %collective-permute-start.3 = (bf16[3072,128]{1,0:T(8,128)(2,1)}, bf16[3072,128]{1,0:T(8,128)(2,1)S(1)}, u32[]{:S(2)}, u32[]{:S(2)}) collective-permute-start(bf16[3072,128]{1,0:T(8,128)(2,1)} %bitcast.2), channel_id=1, source_target_pairs={{0,1},{1,2},{2,3},{3,0},{4,5},{5,6},{6,7},{7,4},{8,9},{9,10},{10,1... | collective-permute-start | bytes 2359304 | tf_op jit(solution)/shard_map/ppermute | solution.py:440
  2.1 18.9 %collective-permute-start.2 = (bf16[3072,128]{1,0:T(8,128)(2,1)}, bf16[3072,128]{1,0:T(8,128)(2,1)S(1)}, u32[]{:S(2)}, u32[]{:S(2)}) collective-permute-start(bf16[3072,128]{1,0:T(8,128)(2,1)} %bitcast.3), channel_id=1, source_target_pairs={{0,3},{1,0},{2,1},{3,2},{4,7},{5,4},{6,5},{7,6},{8,11},{9,8},{10,9... | collective-permute-start | bytes 2359304 | tf_op jit(solution)/shard_map/ppermute | solution.py:440
  3.6 1.2 %copy-start.1 = (bf16[64,3,8,2,128]{4,3,2,1,0:T(2,128)(2,1)S(1)}, bf16[64,3,8,2,128]{4,3,2,1,0:T(2,128)(2,1)}, u32[]{:S(2)}) copy-start(bf16[64,3,8,2,128]{4,3,2,1,0:T(2,128)(2,1)} %param.4) | copy-start | bytes 2359300
  4.8 0.9 %copy-start.3 = (bf16[3,3,3,8,2,128]{5,4,3,2,1,0:T(2,128)(2,1)S(1)}, bf16[3,3,3,8,2,128]{5,4,3,2,1,0:T(2,128)(2,1)}, u32[]{:S(2)}) copy-start(bf16[3,3,3,8,2,128]{5,4,3,2,1,0:T(2,128)(2,1)} %param.5) | copy-start | bytes 331780
  5.7 7.6 %copy-start.2 = (bf16[64,3,8,2,128]{4,3,2,1,0:T(2,128)(2,1)S(1)}, bf16[64,3,8,2,128]{4,3,2,1,0:T(2,128)(2,1)}, u32[]{:S(2)}) copy-start(bf16[64,3,8,2,128]{4,3,2,1,0:T(2,128)(2,1)} %param.4) | copy-start | bytes 2359300
  6.3 11.9 %collective-permute-start = (bf16[6,64,128]{2,1,0:T(8,128)(2,1)S(1)}, bf16[6,64,128]{2,1,0:T(8,128)(2,1)S(1)}, u32[]{:S(2)}, u32[]{:S(2)}) collective-permute-start(bf16[6,64,128]{2,1,0:T(8,128)(2,1)S(1)} %get-tuple-element.38), channel_id=1, source_target_pairs={{0,96},{32,0},{64,32},{96,64},{1,97},{33,1},{65,33},{97,65},{2,98}... | collective-permute-start | bytes 294920 | tf_op jit(solution)/shard_map/ppermute | solution.py:440
  7.4 20.3 %collective-permute-start.4 = (bf16[24,64,128]{2,1,0:T(8,128)(2,1)S(1)}, bf16[24,64,128]{2,1,0:T(8,128)(2,1)S(1)}, u32[]{:S(2)}, u32[]{:S(2)}) collective-permute-start(bf16[24,64,128]{2,1,0:T(8,128)(2,1)S(1)} %get-tuple-element.47), channel_id=1, source_target_pairs={{0,28},{4,0},{8,4},{12,8},{16,12},{20,16},{24,20},{28,24},{1,29},{... | collective-permute-start | bytes 1179656 | tf_op jit(solution)/shard_map/ppermute | solution.py:440
  13.2 14.4 %collective-permute-start.5 = (bf16[26,64,128]{2,1,0:T(8,128)(2,1)S(1)}, bf16[26,64,128]{2,1,0:T(8,128)(2,1)S(1)}, u32[]{:S(2)}, u32[]{:S(2)}) collective-permute-start(bf16[26,64,128]{2,1,0:T(8,128)(2,1)S(1)} %get-tuple-element.48), channel_id=1, source_target_pairs={{0,4},{4,8},{8,12},{12,16},{16,20},{20,24},{24,28},{28,0},{1,5},{5... | collective-permute-start | bytes 1277960 | tf_op jit(solution)/shard_map/ppermute | solution.py:440
  18.2 7.9 %collective-permute-start.1 = (bf16[7,64,128]{2,1,0:T(8,128)(2,1)S(1)}, bf16[7,64,128]{2,1,0:T(8,128)(2,1)S(1)}, u32[]{:S(2)}, u32[]{:S(2)}) collective-permute-start(bf16[7,64,128]{2,1,0:T(8,128)(2,1)S(1)} %get-tuple-element.40), channel_id=1, source_target_pairs={{0,32},{32,64},{64,96},{96,0},{1,33},{33,65},{65,97},{97,1},{2,34}... | collective-permute-start | bytes 344072 | tf_op jit(solution)/shard_map/ppermute | solution.py:440
  20.9 12.8 %collective-permute-start.7 = (bf16[1536,128]{1,0:T(8,128)(2,1)S(1)}, bf16[1536,128]{1,0:T(8,128)(2,1)S(1)}, u32[]{:S(2)}, u32[]{:S(2)}) collective-permute-start(bf16[1536,128]{1,0:T(8,128)(2,1)S(1)} %slice.8), channel_id=1, source_target_pairs={{0,1},{1,2},{2,3},{3,0},{4,5},{5,6},{6,7},{7,4},{8,9},{9,10},{10,1... | collective-permute-start | bytes 1179656 | tf_op jit(solution)/shard_map/ppermute | solution.py:440
  21.0 12.7 %collective-permute-start.8 = (bf16[1536,128]{1,0:T(8,128)(2,1)S(1)}, bf16[1536,128]{1,0:T(8,128)(2,1)S(1)}, u32[]{:S(2)}, u32[]{:S(2)}) collective-permute-start(bf16[1536,128]{1,0:T(8,128)(2,1)S(1)} %slice.9), channel_id=1, source_target_pairs={{0,3},{1,0},{2,1},{3,2},{4,7},{5,4},{6,5},{7,6},{8,11},{9,8},{10,9... | collective-permute-start | bytes 1179656 | tf_op jit(solution)/shard_map/ppermute | solution.py:440
  31.3 24.8 %copy-start = (s32[3]{0:T(128)S(1)}, s32[3]{0:T(128)}, u32[]{:S(2)}) copy-start(s32[3]{0:T(128)} %dirs_ref.3) | copy-start | bytes 40
  31.3 4.0 %collective-permute-start.6 = (f32[128,384]{1,0:T(8,128)S(1)}, f32[128,384]{1,0:T(8,128)S(1)}, u32[]{:S(2)}, u32[]{:S(2)}) collective-permute-start(f32[128,384]{1,0:T(8,128)S(1)} %get-tuple-element.52), channel_id=1, source_target_pairs={{0,32},{32,0},{64,96},{96,64},{1,33},{33,1},{65,97},{97,65},{2,34}... | collective-permute-start | bytes 589832 | tf_op jit(solution)/shard_map/ppermute | solution.py:440
  35.2 1.3 %collective-permute-start.9 = (f32[128,128]{1,0:T(8,128)S(1)}, f32[128,128]{1,0:T(8,128)S(1)}, u32[]{:S(2)}, u32[]{:S(2)}) collective-permute-start(f32[128,128]{1,0:T(8,128)S(1)} %get-tuple-element.54), channel_id=1, source_target_pairs={{0,32},{32,0},{64,96},{96,64},{1,33},{33,1},{65,97},{97,65},{2,34}... | collective-permute-start | bytes 196616 | tf_op jit(solution)/shard_map/ppermute | solution.py:440
  36.5 6.0 %collective-permute-start.12 = (bf16[128,512]{1,0:T(8,128)(2,1)S(1)}, bf16[128,512]{1,0:T(8,128)(2,1)S(1)}, u32[]{:S(2)}, u32[]{:S(2)}) collective-permute-start(bf16[128,512]{1,0:T(8,128)(2,1)S(1)} %pad_maximum_fusion), channel_id=1, source_target_pairs={{0,8},{4,12},{8,0},{12,4},{16,24},{20,28},{24,16},{28,20},{32,48},... | collective-permute-start | bytes 393224 | tf_op jit(solution)/shard_map/ppermute | solution.py:453
  39.9 5.3 %collective-permute-start.11 = (bf16[128,512]{1,0:T(8,128)(2,1)S(1)}, bf16[128,512]{1,0:T(8,128)(2,1)S(1)}, u32[]{:S(2)}, u32[]{:S(2)}) collective-permute-start(bf16[128,512]{1,0:T(8,128)(2,1)S(1)} %pad_maximum_fusion), channel_id=1, source_target_pairs={{0,12},{4,8},{8,4},{12,0},{16,28},{20,24},{24,20},{28,16},{32,112}... | collective-permute-start | bytes 393224 | tf_op jit(solution)/shard_map/ppermute | solution.py:453
  40.3 5.0 %collective-permute-start.10 = (bf16[128,512]{1,0:T(8,128)(2,1)S(1)}, bf16[128,512]{1,0:T(8,128)(2,1)S(1)}, u32[]{:S(2)}, u32[]{:S(2)}) collective-permute-start(bf16[128,512]{1,0:T(8,128)(2,1)S(1)} %pad_maximum_fusion), channel_id=1, source_target_pairs={{0,4},{4,0},{8,12},{12,8},{16,20},{20,16},{24,28},{28,24},{32,96},... | collective-permute-start | bytes 393224 | tf_op jit(solution)/shard_map/ppermute | solution.py:453
  45.3 5.7 %collective-permute-start.15 = (bf16[128,512]{1,0:T(8,128)(2,1)S(1)}, bf16[128,512]{1,0:T(8,128)(2,1)S(1)}, u32[]{:S(2)}, u32[]{:S(2)}) collective-permute-start(bf16[128,512]{1,0:T(8,128)(2,1)S(1)} %add_convert_fusion), channel_id=1, source_target_pairs={{0,16},{4,20},{8,24},{12,28},{16,0},{20,4},{24,8},{28,12},{32,40},... | collective-permute-start | bytes 393224 | tf_op jit(solution)/shard_map/ppermute | solution.py:453
  47.8 5.0 %collective-permute-start.14 = (bf16[128,512]{1,0:T(8,128)(2,1)S(1)}, bf16[128,512]{1,0:T(8,128)(2,1)S(1)}, u32[]{:S(2)}, u32[]{:S(2)}) collective-permute-start(bf16[128,512]{1,0:T(8,128)(2,1)S(1)} %add_convert_fusion), channel_id=1, source_target_pairs={{0,80},{4,84},{8,88},{12,92},{16,64},{20,68},{24,72},{28,76},{32,4... | collective-permute-start | bytes 393224 | tf_op jit(solution)/shard_map/ppermute | solution.py:453
  48.6 4.2 %collective-permute-start.13 = (bf16[128,512]{1,0:T(8,128)(2,1)S(1)}, bf16[128,512]{1,0:T(8,128)(2,1)S(1)}, u32[]{:S(2)}, u32[]{:S(2)}) collective-permute-start(bf16[128,512]{1,0:T(8,128)(2,1)S(1)} %add_convert_fusion), channel_id=1, source_target_pairs={{0,64},{4,68},{8,72},{12,76},{16,80},{20,84},{24,88},{28,92},{32,3... | collective-permute-start | bytes 393224 | tf_op jit(solution)/shard_map/ppermute | solution.py:453
  52.9 4.7 %collective-permute-start.16 = (f32[128,512]{1,0:T(8,128)S(1)}, f32[128,512]{1,0:T(8,128)S(1)}, u32[]{:S(2)}, u32[]{:S(2)}) collective-permute-start(f32[128,512]{1,0:T(8,128)S(1)} %add_add_fusion.rows_ref), channel_id=1, source_target_pairs={{0,32},{32,0},{64,96},{96,64},{1,33},{33,1},{65,97},{97,65},{2,34}... | collective-permute-start | bytes 786440 | tf_op jit(solution)/shard_map/ppermute | solution.py:440

commit v7 on v6

--- a/solution.py
+++ b/solution.py
@@ -194,7 +194,7 @@
             w_ref[1, :, pl.ds(column, LANES)] = phased.astype(BF16)
         return carry
 
-    lax.fori_loop(0, NZY, site, 0)
+    lax.fori_loop(0, NZY, site, 0, unroll=2)
 
 
 EXTENDED = (COL, DZ + 2, HY + 2, NV, LANES)
@@ -280,7 +280,7 @@
         derivative(mu, neighbour, (upr, upi, dnr, dni), zy, store)
         return carry
 
-    lax.fori_loop(0, NZY, site, 0)
+    lax.fori_loop(0, NZY, site, 0, unroll=2)
 
 
 def border_terms(mu, w, ext, exts, upr, upi, dnr, dni, ahead, behind):
@@ -489,8 +489,8 @@
     near = chip_sum(*contract_near(w, right))
     far = chip_sum(*contract_far(w, [far_low, far_high]))
     chip = jnp.concatenate([near, far], 1)
-    row = four_sum(chip, *[crossed(chip, flip, 0) for flip in (2, 1, 3)]).astype(BF16)
-    plane = four_sum(row, *[crossed(row, flip, 1) for flip in (2, 1, 3)])
+    row = four_sum(chip, *[crossed(chip, flip, 1) for flip in (2, 1, 3)]).astype(BF16)
+    plane = four_sum(row, *[crossed(row, flip, 0) for flip in (2, 1, 3)])
     scale = 1.0 / math.sqrt(EXT_X * EXT_Y * EXT_Z)
     mine = finish(directions, plane, scale)
     return finish(directions, mate(plane), scale, mine)

time: 59.2 us -> 59.2 us (level)
  Pallas kernels: 17.3 us -> 16.5 us
    pallas_call x1, Pallas kernels: 4.92 us -> 4.2 us  [local_terms(): pl.pallas_call(local_kernel, out_shape=(shape((4, NV, KDIM), BF16),) + (s...]
    ppermute x11, waiting for transfers between devices: 2.86 us -> 3.51 us  [permuted(): lax.ppermute(value, axis, [(source, target(source)) for source in range(s...]
  transfers between devices with their start and end apart: 17 -> 17, of which waited for: 6 -> 6; matrix products, arithmetic and copies ran while one was open for 0% -> 0% of each run, Pallas kernels for 27% -> 26%
where the time goes in v7:
time: 59.2 us; the launch traced here: 59 us
  starting transfers between devices  28 us (47%)
  Pallas kernels  16.5 us (28%)
  waiting for transfers between devices  12 us (20%)
  local copies, waits for them, and re-layouts  2.13 us (4%)
    ppermute x11, starting transfers between devices, permuted(): lax.ppermute(value, axis, [(source, target(source)) for source in range(s...  20.2 us
    ppermute x6, waiting for transfers between devices, crossed(): return lax.ppermute(value, ('gz', 'gy'), pairs)  8.49 us
    ppermute x6, starting transfers between devices, crossed(): return lax.ppermute(value, ('gz', 'gy'), pairs)  7.81 us
    pallas_call x1, Pallas kernels, local_terms(): pl.pallas_call(local_kernel, out_shape=(shape((4, NV, KDIM), BF16),) + (s...  4.2 us
    ppermute x11, waiting for transfers between devices, permuted(): lax.ppermute(value, axis, [(source, target(source)) for source in range(s...  3.51 us
    pallas_call x2, Pallas kernels, border_terms(): pl.pallas_call(functools.partial(border_kernel, mu), out_shape=(shape((4,...  3.26 us
    pallas_call x2, Pallas kernels, finish(): pl.pallas_call(functools.partial(finish_kernel, scale, int(other)), out_s...  2.86 us
    pallas_call x1, Pallas kernels, right_side(): pl.pallas_call(functools.partial(right_kernel, counts), out_shape=shape((...  2.27 us
  transfers between devices with their start and end apart: 17, of which 6 were waited for; matrix products, arithmetic and copies ran while one was open for 0% of the time, Pallas kernels for 26%

profile of v7, /device:TPU:1, one launch (start us, length us, event | category | flops | bytes accessed | tf_op | source)
XLA Modules:
  0.0 59.0 jit_solution(12472668384851102830)
XLA Ops:
  0.0 2.1 %collective-permute-start.3 = (bf16[3072,128]{1,0:T(8,128)(2,1)}, bf16[3072,128]{1,0:T(8,128)(2,1)S(1)}, u32[]{:S(2)}, u32[]{:S(2)}) collective-permute-start(bf16[3072,128]{1,0:T(8,128)(2,1)} %bitcast.2), channel_id=1, source_target_pairs={{0,1},{1,2},{2,3},{3,0},{4,5},{5,6},{6,7},{7,4},{8,9},{9,10},{10,1... | collective-permute-start | bytes 2359304 | tf_op jit(solution)/shard_map/ppermute | solution.py:440
  2.1 1.5 %collective-permute-start.2 = (bf16[3072,128]{1,0:T(8,128)(2,1)}, bf16[3072,128]{1,0:T(8,128)(2,1)S(1)}, u32[]{:S(2)}, u32[]{:S(2)}) collective-permute-start(bf16[3072,128]{1,0:T(8,128)(2,1)} %bitcast.3), channel_id=1, source_target_pairs={{0,3},{1,0},{2,1},{3,2},{4,7},{5,4},{6,5},{7,6},{8,11},{9,8},{10,9... | collective-permute-start | bytes 2359304 | tf_op jit(solution)/shard_map/ppermute | solution.py:440
  3.6 1.2 %copy-done.1 = bf16[64,3,8,2,128]{4,3,2,1,0:T(2,128)(2,1)S(1)} copy-done((bf16[64,3,8,2,128]{4,3,2,1,0:T(2,128)(2,1)S(1)}, bf16[64,3,8,2,128]{4,3,2,1,0:T(2,128)(2,1)}, u32[]{:S(2)}) %copy-start.1) | copy-done | bytes 786456
  4.8 0.9 %copy-done.3 = bf16[3,3,3,8,2,128]{5,4,3,2,1,0:T(2,128)(2,1)S(1)} copy-done((bf16[3,3,3,8,2,128]{5,4,3,2,1,0:T(2,128)(2,1)S(1)}, bf16[3,3,3,8,2,128]{5,4,3,2,1,0:T(2,128)(2,1)}, u32[]{:S(2)}) %copy-start.3) | copy-done | bytes 110616
  5.7 0.6 prepare.1
  6.3 1.1 %collective-permute-start = (bf16[6,64,128]{2,1,0:T(8,128)(2,1)S(1)}, bf16[6,64,128]{2,1,0:T(8,128)(2,1)S(1)}, u32[]{:S(2)}, u32[]{:S(2)}) collective-permute-start(bf16[6,64,128]{2,1,0:T(8,128)(2,1)S(1)} %get-tuple-element.38), channel_id=1, source_target_pairs={{0,96},{32,0},{64,32},{96,64},{1,97},{33,1},{65,33},{97,65},{2,98}... | collective-permute-start | bytes 294920 | tf_op jit(solution)/shard_map/ppermute | solution.py:440
  7.4 5.9 %collective-permute-start.4 = (bf16[24,64,128]{2,1,0:T(8,128)(2,1)S(1)}, bf16[24,64,128]{2,1,0:T(8,128)(2,1)S(1)}, u32[]{:S(2)}, u32[]{:S(2)}) collective-permute-start(bf16[24,64,128]{2,1,0:T(8,128)(2,1)S(1)} %get-tuple-element.47), channel_id=1, source_target_pairs={{0,28},{4,0},{8,4},{12,8},{16,12},{20,16},{24,20},{28,24},{1,29},{... | collective-permute-start | bytes 1179656 | tf_op jit(solution)/shard_map/ppermute | solution.py:440
  13.3 4.2 %local_terms.1 = (bf16[4,64,6144]{2,1,0:T(8,128)(2,1)S(1)}, f32[3,10,4,64,128]{4,3,2,1,0:T(8,128)S(1)}, f32[3,10,4,64,128]{4,3,2,1,0:T(8,128)S(1)}, f32[16,40,12...) custom-call(s32[3]{0:T(128)S(1)} %copy-done.4, ...), custom_call_target="tpu_custom_call" | custom-call | flops 6000000000 | bytes 6000000 | tf_op jit(solution)/shard_map/local_terms/pallas_call | solution.py:207
  17.5 1.1 %collective-permute-start.1 = (bf16[7,64,128]{2,1,0:T(8,128)(2,1)S(1)}, bf16[7,64,128]{2,1,0:T(8,128)(2,1)S(1)}, u32[]{:S(2)}, u32[]{:S(2)}) collective-permute-start(bf16[7,64,128]{2,1,0:T(8,128)(2,1)S(1)} %get-tuple-element.40), channel_id=1, source_target_pairs={{0,32},{32,64},{64,96},{96,0},{1,33},{33,65},{65,97},{97,1},{2,34}... | collective-permute-start | bytes 344072 | tf_op jit(solution)/shard_map/ppermute | solution.py:440
  18.5 2.4 %collective-permute-done.3.refs_2_ = bf16[3072,128]{1,0:T(8,128)(2,1)S(1)} collective-permute-done((bf16[3072,128]{1,0:T(8,128)(2,1)}, bf16[3072,128]{1,0:T(8,128)(2,1)S(1)}, u32[]{:S(2)}, u32[]{:S(2)}) %collective-permute-start.3) | collective-permute-done | bytes 786464 | tf_op jit(solution)/shard_map/ppermute | solution.py:440
  20.9 0.1 collective-permute-start.7
  21.0 2.7 %collective-permute-start.8 = (bf16[1536,128]{1,0:T(8,128)(2,1)S(1)}, bf16[1536,128]{1,0:T(8,128)(2,1)S(1)}, u32[]{:S(2)}, u32[]{:S(2)}) collective-permute-start(bf16[1536,128]{1,0:T(8,128)(2,1)S(1)} %slice.9), channel_id=1, source_target_pairs={{0,3},{1,0},{2,1},{3,2},{4,7},{5,4},{6,5},{7,6},{8,11},{9,8},{10,9... | collective-permute-start | bytes 1179656 | tf_op jit(solution)/shard_map/ppermute | solution.py:440
  23.8 2.3 %right_side.1.right_ref = bf16[384,6144]{1,0:T(8,128)(2,1)S(1)} custom-call(bf16[3072,128]{1,0:T(8,128)(2,1)S(1)} %bitcast.6, bf16[3072,128]{1,0:T(8,128)(2,1)S(1)} %collective-permute-done.2.refs_1_, bf16[3072,128]{1,0:T(8,128)(2,1)S(1)} %collective-permute-done.3.refs_2_), custom_call_target="tpu_custom_call" | custom-call | flops 2000000000 | bytes 4000000 | tf_op jit(solution)/shard_map/right_side/pallas_call | solution.py:334
  26.1 1.5 %border_z.1 = (bf16[4,64,6144]{2,1,0:T(8,128)(2,1)S(1)}, f32[3,10,4,64,128]{4,3,2,1,0:T(8,128)S(1)}, f32[3,10,4,64,128]{4,3,2,1,0:T(8,128)S(1)}, f32[16,40,128]{2,1,0:T(8,128)S(1)}, f32[16,40,128]{2,1,0:T(8,128)S(1)}) custom-call(bf16[4,64,6144]{2,1,0:T(8,128)(2,1)S(1)} %get-tuple-elem, ...), custom_call_target="tpu_custom_call", output_to_operand_aliasing={{0}: (0, {}), {1}: (1, {}), {2}: (2, {}), {3}: (5, {}), {4}... | custom-call | flops 3000000000 | bytes 3000000 | tf_op jit(solution)/shard_map/border_z/pallas_call | solution.py:288
  27.6 1.7 %border_y.1 = (bf16[4,64,6144]{2,1,0:T(8,128)(2,1)S(1)}, f32[3,10,4,64,128]{4,3,2,1,0:T(8,128)S(1)}, f32[3,10,4,64,128]{4,3,2,1,0:T(8,128)S(1)}, f32[16,40,128]{2,1,0:T(8,128)S(1)}, f32[16,40,128]{2,1,0:T(8,128)S(1)}) custom-call(bf16[4,64,6144]{2,1,0:T(8,128)(2,1)S(1)} %get-tuple-elem, ...), custom_call_target="tpu_custom_call", output_to_operand_aliasing={{0}: (0, {}), {1}: (1, {}), {2}: (2, {}), {3}: (5, {}), {4}... | custom-call | flops 3000000000 | bytes 3000000 | tf_op jit(solution)/shard_map/border_y/pallas_call | solution.py:288
  29.3 1.9 %contract_near.1 = (f32[128,384]{1,0:T(8,128)S(1)}, f32[128,384]{1,0:T(8,128)S(1)}) custom-call(bf16[4,64,6144]{2,1,0:T(8,128)(2,1)S(1)} %get-tuple-element.49.w_ref, bf16[384,6144]{1,0:T(8,128)(2,1)S(1)} %right_side.1.right_ref), custom_call_target="tpu_custom_call" | custom-call | flops 1207959552 | bytes 4000000 | tf_op jit(solution)/shard_map/contract_near/pallas_call | solution.py:360
  31.2 2.4 %collective-permute-start.6 = (f32[128,384]{1,0:T(8,128)S(1)}, f32[128,384]{1,0:T(8,128)S(1)}, u32[]{:S(2)}, u32[]{:S(2)}) collective-permute-start(f32[128,384]{1,0:T(8,128)S(1)} %get-tuple-element.52), channel_id=1, source_target_pairs={{0,32},{32,0},{64,96},{96,64},{1,33},{33,1},{65,97},{97,65},{2,34}... | collective-permute-start | bytes 589832 | tf_op jit(solution)/shard_map/ppermute | solution.py:440
  33.6 1.5 %contract_far.1 = (f32[128,128]{1,0:T(8,128)S(1)}, f32[128,128]{1,0:T(8,128)S(1)}) custom-call(bf16[4,64,6144]{2,1,0:T(8,128)(2,1)S(1)} %get-tuple-element.49.w_ref, bf16[1536,128]{1,0:T(8,128)(2,1)S(1)} %collective-permute-done.7.refs_0_, bf16[1536,128]{1,0:T(8,128)(2,1)S(1)} %collective-permute-done.8.refs_1_), custom_call_target="tpu_custom_call" | custom-call | flops 402653184 | bytes 4000000 | tf_op jit(solution)/shard_map/contract_far/pallas_call | solution.py:378
  35.1 0.2 collective-permute-start.9
  35.3 1.1 %collective-permute-done.9 = f32[128,128]{1,0:T(8,128)S(1)} collective-permute-done((f32[128,128]{1,0:T(8,128)S(1)}, f32[128,128]{1,0:T(8,128)S(1)}, u32[]{:S(2)}, u32[]{:S(2)}) %collective-permute-start.9) | collective-permute-done | bytes 65568 | tf_op jit(solution)/shard_map/ppermute | solution.py:440
  36.5 2.5 %collective-permute-start.12 = (bf16[128,512]{1,0:T(8,128)(2,1)S(1)}, bf16[128,512]{1,0:T(8,128)(2,1)S(1)}, u32[]{:S(2)}, u32[]{:S(2)}) collective-permute-start(bf16[128,512]{1,0:T(8,128)(2,1)S(1)} %pad_maximum_fusion), channel_id=1, source_target_pairs={{0,16},{4,20},{8,24},{12,28},{16,0},{20,4},{24,8},{28,12},{32,40},... | collective-permute-start | bytes 393224 | tf_op jit(solution)/shard_map/ppermute | solution.py:453
  38.9 0.9 %collective-permute-start.11 = (bf16[128,512]{1,0:T(8,128)(2,1)S(1)}, bf16[128,512]{1,0:T(8,128)(2,1)S(1)}, u32[]{:S(2)}, u32[]{:S(2)}) collective-permute-start(bf16[128,512]{1,0:T(8,128)(2,1)S(1)} %pad_maximum_fusion), channel_id=1, source_target_pairs={{0,80},{4,84},{8,88},{12,92},{16,64},{20,68},{24,72},{28,76},{32,4... | collective-permute-start | bytes 393224 | tf_op jit(solution)/shard_map/ppermute | solution.py:453
  39.8 2.4 %collective-permute-done.12 = bf16[128,512]{1,0:T(8,128)(2,1)S(1)} collective-permute-done((bf16[128,512]{1,0:T(8,128)(2,1)S(1)}, bf16[128,512]{1,0:T(8,128)(2,1)S(1)}, u32[]{:S(2)}, u32[]{:S(2)}) %collective-permute-start.12) | collective-permute-done | bytes 131104 | tf_op jit(solution)/shard_map/ppermute | solution.py:453
  42.2 1.8 %collective-permute-done.11 = bf16[128,512]{1,0:T(8,128)(2,1)S(1)} collective-permute-done((bf16[128,512]{1,0:T(8,128)(2,1)S(1)}, bf16[128,512]{1,0:T(8,128)(2,1)S(1)}, u32[]{:S(2)}, u32[]{:S(2)}) %collective-permute-start.11) | collective-permute-done | bytes 131104 | tf_op jit(solution)/shard_map/ppermute | solution.py:453
  44.0 3.7 %collective-permute-start.15 = (bf16[128,512]{1,0:T(8,128)(2,1)S(1)}, bf16[128,512]{1,0:T(8,128)(2,1)S(1)}, u32[]{:S(2)}, u32[]{:S(2)}) collective-permute-start(bf16[128,512]{1,0:T(8,128)(2,1)S(1)} %add_convert_fusion), channel_id=1, source_target_pairs={{0,8},{4,12},{8,0},{12,4},{16,24},{20,28},{24,16},{28,20},{32,48},... | collective-permute-start | bytes 393224 | tf_op jit(solution)/shard_map/ppermute | solution.py:453
  47.7 0.4 collective-permute-start.14
  48.1 0.4 collective-permute-start.13
  48.5 1.6 %collective-permute-done.15 = bf16[128,512]{1,0:T(8,128)(2,1)S(1)} collective-permute-done((bf16[128,512]{1,0:T(8,128)(2,1)S(1)}, bf16[128,512]{1,0:T(8,128)(2,1)S(1)}, u32[]{:S(2)}, u32[]{:S(2)}) %collective-permute-start.15) | collective-permute-done | bytes 131104 | tf_op jit(solution)/shard_map/ppermute | solution.py:453
  50.1 2.8 %collective-permute-done.14 = bf16[128,512]{1,0:T(8,128)(2,1)S(1)} collective-permute-done((bf16[128,512]{1,0:T(8,128)(2,1)S(1)}, bf16[128,512]{1,0:T(8,128)(2,1)S(1)}, u32[]{:S(2)}, u32[]{:S(2)}) %collective-permute-start.14) | collective-permute-done | bytes 131104 | tf_op jit(solution)/shard_map/ppermute | solution.py:453
  52.9 3.2 %collective-permute-start.16 = (f32[128,512]{1,0:T(8,128)S(1)}, f32[128,512]{1,0:T(8,128)S(1)}, u32[]{:S(2)}, u32[]{:S(2)}) collective-permute-start(f32[128,512]{1,0:T(8,128)S(1)} %add_add_fusion.rows_ref), channel_id=1, source_target_pairs={{0,32},{32,0},{64,96},{96,64},{1,33},{33,1},{65,97},{97,65},{2,34}... | collective-permute-start | bytes 786440 | tf_op jit(solution)/shard_map/ppermute | solution.py:440
  56.1 1.4 %finish_mine.1.refs_0_ = f32[4,2,64,256]{3,2,1,0:T(8,128)} custom-call(s32[3]{0:T(128)S(1)} %copy-done, f32[128,512]{1,0:T(8,128)S(1)} %add_add_fusion.rows_ref), custom_call_target="tpu_custom_call" | custom-call | flops 200000 | bytes 1000000 | tf_op jit(solution)/shard_map/finish_mine/pallas_call | solution.py:425
  57.6 1.4 %finish_other.1 = f32[4,2,64,256]{3,2,1,0:T(8,128)} custom-call(s32[3]{0:T(128)S(1)} %copy-done, f32[128,512]{1,0:T(8,128)S(1)} %collective-permute-done.16.rows_ref, f32[4,2,64,256]{3,2,1,0:T(8,128)} %finish_mine.1.refs_0_), custom_call_target="tpu_custom_call", output_to_operand_aliasing={{}: (2, {})} | custom-call | flops 200000 | bytes 1000000 | tf_op jit(solution)/shard_map/finish_other/pallas_call | solution.py:425
  (28 shorter events, 0.3 us)
Async XLA Ops:
  0.0 13.3 %copy-start.4 = (s32[3]{0:T(128)S(1)}, s32[3]{0:T(128)}, u32[]{:S(2)}) copy-start(s32[3]{0:T(128)} %momentum_ref.1) | copy-start | bytes 40
  0.0 20.9 %collective-permute-start.3 = (bf16[3072,128]{1,0:T(8,128)(2,1)}, bf16[3072,128]{1,0:T(8,128)(2,1)S(1)}, u32[]{:S(2)}, u32[]{:S(2)}) collective-permute-start(bf16[3072,128]{1,0:T(8,128)(2,1)} %bitcast.2), channel_id=1, source_target_pairs={{0,1},{1,2},{2,3},{3,0},{4,5},{5,6},{6,7},{7,4},{8,9},{9,10},{10,1... | collective-permute-start | bytes 2359304 | tf_op jit(solution)/shard_map/ppermute | solution.py:440
  2.1 18.9 %collective-permute-start.2 = (bf16[3072,128]{1,0:T(8,128)(2,1)}, bf16[3072,128]{1,0:T(8,128)(2,1)S(1)}, u32[]{:S(2)}, u32[]{:S(2)}) collective-permute-start(bf16[3072,128]{1,0:T(8,128)(2,1)} %bitcast.3), channel_id=1, source_target_pairs={{0,3},{1,0},{2,1},{3,2},{4,7},{5,4},{6,5},{7,6},{8,11},{9,8},{10,9... | collective-permute-start | bytes 2359304 | tf_op jit(solution)/shard_map/ppermute | solution.py:440
  3.6 1.2 %copy-start.1 = (bf16[64,3,8,2,128]{4,3,2,1,0:T(2,128)(2,1)S(1)}, bf16[64,3,8,2,128]{4,3,2,1,0:T(2,128)(2,1)}, u32[]{:S(2)}) copy-start(bf16[64,3,8,2,128]{4,3,2,1,0:T(2,128)(2,1)} %param.4) | copy-start | bytes 2359300
  4.8 0.9 %copy-start.3 = (bf16[3,3,3,8,2,128]{5,4,3,2,1,0:T(2,128)(2,1)S(1)}, bf16[3,3,3,8,2,128]{5,4,3,2,1,0:T(2,128)(2,1)}, u32[]{:S(2)}) copy-start(bf16[3,3,3,8,2,128]{5,4,3,2,1,0:T(2,128)(2,1)} %param.5) | copy-start | bytes 331780
  5.7 7.6 %copy-start.2 = (bf16[64,3,8,2,128]{4,3,2,1,0:T(2,128)(2,1)S(1)}, bf16[64,3,8,2,128]{4,3,2,1,0:T(2,128)(2,1)}, u32[]{:S(2)}) copy-start(bf16[64,3,8,2,128]{4,3,2,1,0:T(2,128)(2,1)} %param.4) | copy-start | bytes 2359300
  6.3 11.2 %collective-permute-start = (bf16[6,64,128]{2,1,0:T(8,128)(2,1)S(1)}, bf16[6,64,128]{2,1,0:T(8,128)(2,1)S(1)}, u32[]{:S(2)}, u32[]{:S(2)}) collective-permute-start(bf16[6,64,128]{2,1,0:T(8,128)(2,1)S(1)} %get-tuple-element.38), channel_id=1, source_target_pairs={{0,96},{32,0},{64,32},{96,64},{1,97},{33,1},{65,33},{97,65},{2,98}... | collective-permute-start | bytes 294920 | tf_op jit(solution)/shard_map/ppermute | solution.py:440
  7.4 20.2 %collective-permute-start.4 = (bf16[24,64,128]{2,1,0:T(8,128)(2,1)S(1)}, bf16[24,64,128]{2,1,0:T(8,128)(2,1)S(1)}, u32[]{:S(2)}, u32[]{:S(2)}) collective-permute-start(bf16[24,64,128]{2,1,0:T(8,128)(2,1)S(1)} %get-tuple-element.47), channel_id=1, source_target_pairs={{0,28},{4,0},{8,4},{12,8},{16,12},{20,16},{24,20},{28,24},{1,29},{... | collective-permute-start | bytes 1179656 | tf_op jit(solution)/shard_map/ppermute | solution.py:440
  13.2 14.4 %collective-permute-start.5 = (bf16[26,64,128]{2,1,0:T(8,128)(2,1)S(1)}, bf16[26,64,128]{2,1,0:T(8,128)(2,1)S(1)}, u32[]{:S(2)}, u32[]{:S(2)}) collective-permute-start(bf16[26,64,128]{2,1,0:T(8,128)(2,1)S(1)} %get-tuple-element.48), channel_id=1, source_target_pairs={{0,4},{4,8},{8,12},{12,16},{16,20},{20,24},{24,28},{28,0},{1,5},{5... | collective-permute-start | bytes 1277960 | tf_op jit(solution)/shard_map/ppermute | solution.py:440
  17.5 8.6 %collective-permute-start.1 = (bf16[7,64,128]{2,1,0:T(8,128)(2,1)S(1)}, bf16[7,64,128]{2,1,0:T(8,128)(2,1)S(1)}, u32[]{:S(2)}, u32[]{:S(2)}) collective-permute-start(bf16[7,64,128]{2,1,0:T(8,128)(2,1)S(1)} %get-tuple-element.40), channel_id=1, source_target_pairs={{0,32},{32,64},{64,96},{96,0},{1,33},{33,65},{65,97},{97,1},{2,34}... | collective-permute-start | bytes 344072 | tf_op jit(solution)/shard_map/ppermute | solution.py:440
  20.9 12.7 %collective-permute-start.7 = (bf16[1536,128]{1,0:T(8,128)(2,1)S(1)}, bf16[1536,128]{1,0:T(8,128)(2,1)S(1)}, u32[]{:S(2)}, u32[]{:S(2)}) collective-permute-start(bf16[1536,128]{1,0:T(8,128)(2,1)S(1)} %slice.8), channel_id=1, source_target_pairs={{0,1},{1,2},{2,3},{3,0},{4,5},{5,6},{6,7},{7,4},{8,9},{9,10},{10,1... | collective-permute-start | bytes 1179656 | tf_op jit(solution)/shard_map/ppermute | solution.py:440
  21.0 12.6 %collective-permute-start.8 = (bf16[1536,128]{1,0:T(8,128)(2,1)S(1)}, bf16[1536,128]{1,0:T(8,128)(2,1)S(1)}, u32[]{:S(2)}, u32[]{:S(2)}) collective-permute-start(bf16[1536,128]{1,0:T(8,128)(2,1)S(1)} %slice.9), channel_id=1, source_target_pairs={{0,3},{1,0},{2,1},{3,2},{4,7},{5,4},{6,5},{7,6},{8,11},{9,8},{10,9... | collective-permute-start | bytes 1179656 | tf_op jit(solution)/shard_map/ppermute | solution.py:440
  31.2 24.9 %copy-start = (s32[3]{0:T(128)S(1)}, s32[3]{0:T(128)}, u32[]{:S(2)}) copy-start(s32[3]{0:T(128)} %dirs_ref.3) | copy-start | bytes 40
  31.2 4.0 %collective-permute-start.6 = (f32[128,384]{1,0:T(8,128)S(1)}, f32[128,384]{1,0:T(8,128)S(1)}, u32[]{:S(2)}, u32[]{:S(2)}) collective-permute-start(f32[128,384]{1,0:T(8,128)S(1)} %get-tuple-element.52), channel_id=1, source_target_pairs={{0,32},{32,0},{64,96},{96,64},{1,33},{33,1},{65,97},{97,65},{2,34}... | collective-permute-start | bytes 589832 | tf_op jit(solution)/shard_map/ppermute | solution.py:440
  35.1 1.3 %collective-permute-start.9 = (f32[128,128]{1,0:T(8,128)S(1)}, f32[128,128]{1,0:T(8,128)S(1)}, u32[]{:S(2)}, u32[]{:S(2)}) collective-permute-start(f32[128,128]{1,0:T(8,128)S(1)} %get-tuple-element.54), channel_id=1, source_target_pairs={{0,32},{32,0},{64,96},{96,64},{1,33},{33,1},{65,97},{97,65},{2,34}... | collective-permute-start | bytes 196616 | tf_op jit(solution)/shard_map/ppermute | solution.py:440
  36.5 5.7 %collective-permute-start.12 = (bf16[128,512]{1,0:T(8,128)(2,1)S(1)}, bf16[128,512]{1,0:T(8,128)(2,1)S(1)}, u32[]{:S(2)}, u32[]{:S(2)}) collective-permute-start(bf16[128,512]{1,0:T(8,128)(2,1)S(1)} %pad_maximum_fusion), channel_id=1, source_target_pairs={{0,16},{4,20},{8,24},{12,28},{16,0},{20,4},{24,8},{28,12},{32,40},... | collective-permute-start | bytes 393224 | tf_op jit(solution)/shard_map/ppermute | solution.py:453
  38.9 5.0 %collective-permute-start.11 = (bf16[128,512]{1,0:T(8,128)(2,1)S(1)}, bf16[128,512]{1,0:T(8,128)(2,1)S(1)}, u32[]{:S(2)}, u32[]{:S(2)}) collective-permute-start(bf16[128,512]{1,0:T(8,128)(2,1)S(1)} %pad_maximum_fusion), channel_id=1, source_target_pairs={{0,80},{4,84},{8,88},{12,92},{16,64},{20,68},{24,72},{28,76},{32,4... | collective-permute-start | bytes 393224 | tf_op jit(solution)/shard_map/ppermute | solution.py:453
  39.8 4.2 %collective-permute-start.10 = (bf16[128,512]{1,0:T(8,128)(2,1)S(1)}, bf16[128,512]{1,0:T(8,128)(2,1)S(1)}, u32[]{:S(2)}, u32[]{:S(2)}) collective-permute-start(bf16[128,512]{1,0:T(8,128)(2,1)S(1)} %pad_maximum_fusion), channel_id=1, source_target_pairs={{0,64},{4,68},{8,72},{12,76},{16,80},{20,84},{24,88},{28,92},{32,3... | collective-permute-start | bytes 393224 | tf_op jit(solution)/shard_map/ppermute | solution.py:453
  44.0 6.0 %collective-permute-start.15 = (bf16[128,512]{1,0:T(8,128)(2,1)S(1)}, bf16[128,512]{1,0:T(8,128)(2,1)S(1)}, u32[]{:S(2)}, u32[]{:S(2)}) collective-permute-start(bf16[128,512]{1,0:T(8,128)(2,1)S(1)} %add_convert_fusion), channel_id=1, source_target_pairs={{0,8},{4,12},{8,0},{12,4},{16,24},{20,28},{24,16},{28,20},{32,48},... | collective-permute-start | bytes 393224 | tf_op jit(solution)/shard_map/ppermute | solution.py:453
  47.7 5.1 %collective-permute-start.14 = (bf16[128,512]{1,0:T(8,128)(2,1)S(1)}, bf16[128,512]{1,0:T(8,128)(2,1)S(1)}, u32[]{:S(2)}, u32[]{:S(2)}) collective-permute-start(bf16[128,512]{1,0:T(8,128)(2,1)S(1)} %add_convert_fusion), channel_id=1, source_target_pairs={{0,12},{4,8},{8,4},{12,0},{16,28},{20,24},{24,20},{28,16},{32,112}... | collective-permute-start | bytes 393224 | tf_op jit(solution)/shard_map/ppermute | solution.py:453
  48.1 4.7 %collective-permute-start.13 = (bf16[128,512]{1,0:T(8,128)(2,1)S(1)}, bf16[128,512]{1,0:T(8,128)(2,1)S(1)}, u32[]{:S(2)}, u32[]{:S(2)}) collective-permute-start(bf16[128,512]{1,0:T(8,128)(2,1)S(1)} %add_convert_fusion), channel_id=1, source_target_pairs={{0,4},{4,0},{8,12},{12,8},{16,20},{20,16},{24,28},{28,24},{32,96},... | collective-permute-start | bytes 393224 | tf_op jit(solution)/shard_map/ppermute | solution.py:453
  52.9 4.6 %collective-permute-start.16 = (f32[128,512]{1,0:T(8,128)S(1)}, f32[128,512]{1,0:T(8,128)S(1)}, u32[]{:S(2)}, u32[]{:S(2)}) collective-permute-start(f32[128,512]{1,0:T(8,128)S(1)} %add_add_fusion.rows_ref), channel_id=1, source_target_pairs={{0,32},{32,0},{64,96},{96,64},{1,33},{33,1},{65,97},{97,65},{2,34}... | collective-permute-start | bytes 786440 | tf_op jit(solution)/shard_map/ppermute | solution.py:440

commit v8 on v7

--- a/solution.py
+++ b/solution.py
@@ -194,7 +194,7 @@
             w_ref[1, :, pl.ds(column, LANES)] = phased.astype(BF16)
         return carry
 
-    lax.fori_loop(0, NZY, site, 0, unroll=2)
+    lax.fori_loop(0, NZY, site, 0)
 
 
 EXTENDED = (COL, DZ + 2, HY + 2, NV, LANES)
@@ -280,7 +280,7 @@
         derivative(mu, neighbour, (upr, upi, dnr, dni), zy, store)
         return carry
 
-    lax.fori_loop(0, NZY, site, 0, unroll=2)
+    lax.fori_loop(0, NZY, site, 0)
 
 
 def border_terms(mu, w, ext, exts, upr, upi, dnr, dni, ahead, behind):

time: 59.2 us -> 59.2 us (level)
  Pallas kernels: 16.5 us -> 17.3 us
  waiting for transfers between devices: 12 us -> 11.3 us
    pallas_call x1, Pallas kernels: 4.2 us -> 4.92 us  [local_terms(): pl.pallas_call(local_kernel, out_shape=(shape((4, NV, KDIM), BF16),) + (s...]
    ppermute x11, waiting for transfers between devices: 3.51 us -> 2.86 us  [permuted(): lax.ppermute(value, axis, [(source, target(source)) for source in range(s...]
  transfers between devices with their start and end apart: 17 -> 17, of which waited for: 6 -> 6; matrix products, arithmetic and copies ran while one was open for 0% -> 0% of each run, Pallas kernels for 26% -> 27%
where the time goes in v8:
time: 59.2 us; the launch traced here: 59 us
  starting transfers between devices  27.9 us (47%)
  Pallas kernels  17.3 us (29%)
  waiting for transfers between devices  11.3 us (19%)
  local copies, waits for them, and re-layouts  2.13 us (4%)
    ppermute x11, starting transfers between devices, permuted(): lax.ppermute(value, axis, [(source, target(source)) for source in range(s...  20.1 us
    ppermute x6, waiting for transfers between devices, crossed(): return lax.ppermute(value, ('gz', 'gy'), pairs)  8.48 us
    ppermute x6, starting transfers between devices, crossed(): return lax.ppermute(value, ('gz', 'gy'), pairs)  7.74 us
    pallas_call x1, Pallas kernels, local_terms(): pl.pallas_call(local_kernel, out_shape=(shape((4, NV, KDIM), BF16),) + (s...  4.92 us
    pallas_call x2, Pallas kernels, border_terms(): pl.pallas_call(functools.partial(border_kernel, mu), out_shape=(shape((4,...  3.33 us
    pallas_call x2, Pallas kernels, finish(): pl.pallas_call(functools.partial(finish_kernel, scale, int(other)), out_s...  2.86 us
    ppermute x11, waiting for transfers between devices, permuted(): lax.ppermute(value, axis, [(source, target(source)) for source in range(s...  2.86 us
    pallas_call x1, Pallas kernels, right_side(): pl.pallas_call(functools.partial(right_kernel, counts), out_shape=shape((...  2.27 us
  transfers between devices with their start and end apart: 17, of which 6 were waited for; matrix products, arithmetic and copies ran while one was open for 0% of the time, Pallas kernels for 27%

profile of v8, /device:TPU:1, one launch (start us, length us, event | category | flops | bytes accessed | tf_op | source)
XLA Modules:
  0.0 59.0 jit_solution(3608481285216956477)
XLA Ops:
  0.0 2.1 %collective-permute-start.3 = (bf16[3072,128]{1,0:T(8,128)(2,1)}, bf16[3072,128]{1,0:T(8,128)(2,1)S(1)}, u32[]{:S(2)}, u32[]{:S(2)}) collective-permute-start(bf16[3072,128]{1,0:T(8,128)(2,1)} %bitcast.2), channel_id=1, source_target_pairs={{0,1},{1,2},{2,3},{3,0},{4,5},{5,6},{6,7},{7,4},{8,9},{9,10},{10,1... | collective-permute-start | bytes 2359304 | tf_op jit(solution)/shard_map/ppermute | solution.py:440
  2.1 1.5 %collective-permute-start.2 = (bf16[3072,128]{1,0:T(8,128)(2,1)}, bf16[3072,128]{1,0:T(8,128)(2,1)S(1)}, u32[]{:S(2)}, u32[]{:S(2)}) collective-permute-start(bf16[3072,128]{1,0:T(8,128)(2,1)} %bitcast.3), channel_id=1, source_target_pairs={{0,3},{1,0},{2,1},{3,2},{4,7},{5,4},{6,5},{7,6},{8,11},{9,8},{10,9... | collective-permute-start | bytes 2359304 | tf_op jit(solution)/shard_map/ppermute | solution.py:440
  3.6 1.2 %copy-done.1 = bf16[64,3,8,2,128]{4,3,2,1,0:T(2,128)(2,1)S(1)} copy-done((bf16[64,3,8,2,128]{4,3,2,1,0:T(2,128)(2,1)S(1)}, bf16[64,3,8,2,128]{4,3,2,1,0:T(2,128)(2,1)}, u32[]{:S(2)}) %copy-start.1) | copy-done | bytes 786456
  4.8 0.9 %copy-done.3 = bf16[3,3,3,8,2,128]{5,4,3,2,1,0:T(2,128)(2,1)S(1)} copy-done((bf16[3,3,3,8,2,128]{5,4,3,2,1,0:T(2,128)(2,1)S(1)}, bf16[3,3,3,8,2,128]{5,4,3,2,1,0:T(2,128)(2,1)}, u32[]{:S(2)}) %copy-start.3) | copy-done | bytes 110616
  5.7 0.6 prepare.1
  6.3 1.1 %collective-permute-start = (bf16[6,64,128]{2,1,0:T(8,128)(2,1)S(1)}, bf16[6,64,128]{2,1,0:T(8,128)(2,1)S(1)}, u32[]{:S(2)}, u32[]{:S(2)}) collective-permute-start(bf16[6,64,128]{2,1,0:T(8,128)(2,1)S(1)} %get-tuple-element.38), channel_id=1, source_target_pairs={{0,96},{32,0},{64,32},{96,64},{1,97},{33,1},{65,33},{97,65},{2,98}... | collective-permute-start | bytes 294920 | tf_op jit(solution)/shard_map/ppermute | solution.py:440
  7.4 5.9 %collective-permute-start.4 = (bf16[24,64,128]{2,1,0:T(8,128)(2,1)S(1)}, bf16[24,64,128]{2,1,0:T(8,128)(2,1)S(1)}, u32[]{:S(2)}, u32[]{:S(2)}) collective-permute-start(bf16[24,64,128]{2,1,0:T(8,128)(2,1)S(1)} %get-tuple-element.47), channel_id=1, source_target_pairs={{0,28},{4,0},{8,4},{12,8},{16,12},{20,16},{24,20},{28,24},{1,29},{... | collective-permute-start | bytes 1179656 | tf_op jit(solution)/shard_map/ppermute | solution.py:440
  13.3 4.9 %local_terms.1 = (bf16[4,64,6144]{2,1,0:T(8,128)(2,1)S(1)}, f32[3,10,4,64,128]{4,3,2,1,0:T(8,128)S(1)}, f32[3,10,4,64,128]{4,3,2,1,0:T(8,128)S(1)}, f32[16,40,12...) custom-call(s32[3]{0:T(128)S(1)} %copy-done.4, ...), custom_call_target="tpu_custom_call" | custom-call | flops 6000000000 | bytes 6000000 | tf_op jit(solution)/shard_map/local_terms/pallas_call | solution.py:207
  18.2 1.1 %collective-permute-start.1 = (bf16[7,64,128]{2,1,0:T(8,128)(2,1)S(1)}, bf16[7,64,128]{2,1,0:T(8,128)(2,1)S(1)}, u32[]{:S(2)}, u32[]{:S(2)}) collective-permute-start(bf16[7,64,128]{2,1,0:T(8,128)(2,1)S(1)} %get-tuple-element.40), channel_id=1, source_target_pairs={{0,32},{32,64},{64,96},{96,0},{1,33},{33,65},{65,97},{97,1},{2,34}... | collective-permute-start | bytes 344072 | tf_op jit(solution)/shard_map/ppermute | solution.py:440
  19.2 1.6 %collective-permute-done.3.refs_2_ = bf16[3072,128]{1,0:T(8,128)(2,1)S(1)} collective-permute-done((bf16[3072,128]{1,0:T(8,128)(2,1)}, bf16[3072,128]{1,0:T(8,128)(2,1)S(1)}, u32[]{:S(2)}, u32[]{:S(2)}) %collective-permute-start.3) | collective-permute-done | bytes 786464 | tf_op jit(solution)/shard_map/ppermute | solution.py:440
  20.9 0.1 collective-permute-start.7
  21.0 2.7 %collective-permute-start.8 = (bf16[1536,128]{1,0:T(8,128)(2,1)S(1)}, bf16[1536,128]{1,0:T(8,128)(2,1)S(1)}, u32[]{:S(2)}, u32[]{:S(2)}) collective-permute-start(bf16[1536,128]{1,0:T(8,128)(2,1)S(1)} %slice.9), channel_id=1, source_target_pairs={{0,3},{1,0},{2,1},{3,2},{4,7},{5,4},{6,5},{7,6},{8,11},{9,8},{10,9... | collective-permute-start | bytes 1179656 | tf_op jit(solution)/shard_map/ppermute | solution.py:440
  23.8 2.3 %right_side.1.right_ref = bf16[384,6144]{1,0:T(8,128)(2,1)S(1)} custom-call(bf16[3072,128]{1,0:T(8,128)(2,1)S(1)} %bitcast.6, bf16[3072,128]{1,0:T(8,128)(2,1)S(1)} %collective-permute-done.2.refs_1_, bf16[3072,128]{1,0:T(8,128)(2,1)S(1)} %collective-permute-done.3.refs_2_), custom_call_target="tpu_custom_call" | custom-call | flops 2000000000 | bytes 4000000 | tf_op jit(solution)/shard_map/right_side/pallas_call | solution.py:334
  26.1 1.6 %border_z.1 = (bf16[4,64,6144]{2,1,0:T(8,128)(2,1)S(1)}, f32[3,10,4,64,128]{4,3,2,1,0:T(8,128)S(1)}, f32[3,10,4,64,128]{4,3,2,1,0:T(8,128)S(1)}, f32[16,40,128]{2,1,0:T(8,128)S(1)}, f32[16,40,128]{2,1,0:T(8,128)S(1)}) custom-call(bf16[4,64,6144]{2,1,0:T(8,128)(2,1)S(1)} %get-tuple-elem, ...), custom_call_target="tpu_custom_call", output_to_operand_aliasing={{0}: (0, {}), {1}: (1, {}), {2}: (2, {}), {3}: (5, {}), {4}... | custom-call | flops 3000000000 | bytes 3000000 | tf_op jit(solution)/shard_map/border_z/pallas_call | solution.py:288
  27.7 1.8 %border_y.1 = (bf16[4,64,6144]{2,1,0:T(8,128)(2,1)S(1)}, f32[3,10,4,64,128]{4,3,2,1,0:T(8,128)S(1)}, f32[3,10,4,64,128]{4,3,2,1,0:T(8,128)S(1)}, f32[16,40,128]{2,1,0:T(8,128)S(1)}, f32[16,40,128]{2,1,0:T(8,128)S(1)}) custom-call(bf16[4,64,6144]{2,1,0:T(8,128)(2,1)S(1)} %get-tuple-elem, ...), custom_call_target="tpu_custom_call", output_to_operand_aliasing={{0}: (0, {}), {1}: (1, {}), {2}: (2, {}), {3}: (5, {}), {4}... | custom-call | flops 3000000000 | bytes 3000000 | tf_op jit(solution)/shard_map/border_y/pallas_call | solution.py:288
  29.4 1.9 %contract_near.1 = (f32[128,384]{1,0:T(8,128)S(1)}, f32[128,384]{1,0:T(8,128)S(1)}) custom-call(bf16[4,64,6144]{2,1,0:T(8,128)(2,1)S(1)} %get-tuple-element.49.w_ref, bf16[384,6144]{1,0:T(8,128)(2,1)S(1)} %right_side.1.right_ref), custom_call_target="tpu_custom_call" | custom-call | flops 1207959552 | bytes 4000000 | tf_op jit(solution)/shard_map/contract_near/pallas_call | solution.py:360
  31.3 2.4 %collective-permute-start.6 = (f32[128,384]{1,0:T(8,128)S(1)}, f32[128,384]{1,0:T(8,128)S(1)}, u32[]{:S(2)}, u32[]{:S(2)}) collective-permute-start(f32[128,384]{1,0:T(8,128)S(1)} %get-tuple-element.52), channel_id=1, source_target_pairs={{0,32},{32,0},{64,96},{96,64},{1,33},{33,1},{65,97},{97,65},{2,34}... | collective-permute-start | bytes 589832 | tf_op jit(solution)/shard_map/ppermute | solution.py:440
  33.7 1.5 %contract_far.1 = (f32[128,128]{1,0:T(8,128)S(1)}, f32[128,128]{1,0:T(8,128)S(1)}) custom-call(bf16[4,64,6144]{2,1,0:T(8,128)(2,1)S(1)} %get-tuple-element.49.w_ref, bf16[1536,128]{1,0:T(8,128)(2,1)S(1)} %collective-permute-done.7.refs_0_, bf16[1536,128]{1,0:T(8,128)(2,1)S(1)} %collective-permute-done.8.refs_1_), custom_call_target="tpu_custom_call" | custom-call | flops 402653184 | bytes 4000000 | tf_op jit(solution)/shard_map/contract_far/pallas_call | solution.py:378
  35.2 0.1 collective-permute-start.9
  35.3 1.2 %collective-permute-done.9 = f32[128,128]{1,0:T(8,128)S(1)} collective-permute-done((f32[128,128]{1,0:T(8,128)S(1)}, f32[128,128]{1,0:T(8,128)S(1)}, u32[]{:S(2)}, u32[]{:S(2)}) %collective-permute-start.9) | collective-permute-done | bytes 65568 | tf_op jit(solution)/shard_map/ppermute | solution.py:440
  36.5 2.4 %collective-permute-start.12 = (bf16[128,512]{1,0:T(8,128)(2,1)S(1)}, bf16[128,512]{1,0:T(8,128)(2,1)S(1)}, u32[]{:S(2)}, u32[]{:S(2)}) collective-permute-start(bf16[128,512]{1,0:T(8,128)(2,1)S(1)} %pad_maximum_fusion), channel_id=1, source_target_pairs={{0,16},{4,20},{8,24},{12,28},{16,0},{20,4},{24,8},{28,12},{32,40},... | collective-permute-start | bytes 393224 | tf_op jit(solution)/shard_map/ppermute | solution.py:453
  39.0 0.9 %collective-permute-start.11 = (bf16[128,512]{1,0:T(8,128)(2,1)S(1)}, bf16[128,512]{1,0:T(8,128)(2,1)S(1)}, u32[]{:S(2)}, u32[]{:S(2)}) collective-permute-start(bf16[128,512]{1,0:T(8,128)(2,1)S(1)} %pad_maximum_fusion), channel_id=1, source_target_pairs={{0,80},{4,84},{8,88},{12,92},{16,64},{20,68},{24,72},{28,76},{32,4... | collective-permute-start | bytes 393224 | tf_op jit(solution)/shard_map/ppermute | solution.py:453
  39.8 2.4 %collective-permute-done.12 = bf16[128,512]{1,0:T(8,128)(2,1)S(1)} collective-permute-done((bf16[128,512]{1,0:T(8,128)(2,1)S(1)}, bf16[128,512]{1,0:T(8,128)(2,1)S(1)}, u32[]{:S(2)}, u32[]{:S(2)}) %collective-permute-start.12) | collective-permute-done | bytes 131104 | tf_op jit(solution)/shard_map/ppermute | solution.py:453
  42.2 1.8 %collective-permute-done.11 = bf16[128,512]{1,0:T(8,128)(2,1)S(1)} collective-permute-done((bf16[128,512]{1,0:T(8,128)(2,1)S(1)}, bf16[128,512]{1,0:T(8,128)(2,1)S(1)}, u32[]{:S(2)}, u32[]{:S(2)}) %collective-permute-start.11) | collective-permute-done | bytes 131104 | tf_op jit(solution)/shard_map/ppermute | solution.py:453
  44.1 3.7 %collective-permute-start.15 = (bf16[128,512]{1,0:T(8,128)(2,1)S(1)}, bf16[128,512]{1,0:T(8,128)(2,1)S(1)}, u32[]{:S(2)}, u32[]{:S(2)}) collective-permute-start(bf16[128,512]{1,0:T(8,128)(2,1)S(1)} %add_convert_fusion), channel_id=1, source_target_pairs={{0,8},{4,12},{8,0},{12,4},{16,24},{20,28},{24,16},{28,20},{32,48},... | collective-permute-start | bytes 393224 | tf_op jit(solution)/shard_map/ppermute | solution.py:453
  47.8 0.4 collective-permute-start.14
  48.2 0.3 collective-permute-start.13
  48.5 1.6 %collective-permute-done.15 = bf16[128,512]{1,0:T(8,128)(2,1)S(1)} collective-permute-done((bf16[128,512]{1,0:T(8,128)(2,1)S(1)}, bf16[128,512]{1,0:T(8,128)(2,1)S(1)}, u32[]{:S(2)}, u32[]{:S(2)}) %collective-permute-start.15) | collective-permute-done | bytes 131104 | tf_op jit(solution)/shard_map/ppermute | solution.py:453
  50.1 2.7 %collective-permute-done.14 = bf16[128,512]{1,0:T(8,128)(2,1)S(1)} collective-permute-done((bf16[128,512]{1,0:T(8,128)(2,1)S(1)}, bf16[128,512]{1,0:T(8,128)(2,1)S(1)}, u32[]{:S(2)}, u32[]{:S(2)}) %collective-permute-start.14) | collective-permute-done | bytes 131104 | tf_op jit(solution)/shard_map/ppermute | solution.py:453
  52.9 3.2 %collective-permute-start.16 = (f32[128,512]{1,0:T(8,128)S(1)}, f32[128,512]{1,0:T(8,128)S(1)}, u32[]{:S(2)}, u32[]{:S(2)}) collective-permute-start(f32[128,512]{1,0:T(8,128)S(1)} %add_add_fusion.rows_ref), channel_id=1, source_target_pairs={{0,32},{32,0},{64,96},{96,64},{1,33},{33,1},{65,97},{97,65},{2,34}... | collective-permute-start | bytes 786440 | tf_op jit(solution)/shard_map/ppermute | solution.py:440
  56.1 1.4 %finish_mine.1.refs_0_ = f32[4,2,64,256]{3,2,1,0:T(8,128)} custom-call(s32[3]{0:T(128)S(1)} %copy-done, f32[128,512]{1,0:T(8,128)S(1)} %add_add_fusion.rows_ref), custom_call_target="tpu_custom_call" | custom-call | flops 200000 | bytes 1000000 | tf_op jit(solution)/shard_map/finish_mine/pallas_call | solution.py:425
  57.6 1.4 %finish_other.1 = f32[4,2,64,256]{3,2,1,0:T(8,128)} custom-call(s32[3]{0:T(128)S(1)} %copy-done, f32[128,512]{1,0:T(8,128)S(1)} %collective-permute-done.16.rows_ref, f32[4,2,64,256]{3,2,1,0:T(8,128)} %finish_mine.1.refs_0_), custom_call_target="tpu_custom_call", output_to_operand_aliasing={{}: (2, {})} | custom-call | flops 200000 | bytes 1000000 | tf_op jit(solution)/shard_map/finish_other/pallas_call | solution.py:425
  (28 shorter events, 0.3 us)
Async XLA Ops:
  0.0 13.3 %copy-start.4 = (s32[3]{0:T(128)S(1)}, s32[3]{0:T(128)}, u32[]{:S(2)}) copy-start(s32[3]{0:T(128)} %momentum_ref.1) | copy-start | bytes 40
  0.0 20.9 %collective-permute-start.3 = (bf16[3072,128]{1,0:T(8,128)(2,1)}, bf16[3072,128]{1,0:T(8,128)(2,1)S(1)}, u32[]{:S(2)}, u32[]{:S(2)}) collective-permute-start(bf16[3072,128]{1,0:T(8,128)(2,1)} %bitcast.2), channel_id=1, source_target_pairs={{0,1},{1,2},{2,3},{3,0},{4,5},{5,6},{6,7},{7,4},{8,9},{9,10},{10,1... | collective-permute-start | bytes 2359304 | tf_op jit(solution)/shard_map/ppermute | solution.py:440
  2.1 18.9 %collective-permute-start.2 = (bf16[3072,128]{1,0:T(8,128)(2,1)}, bf16[3072,128]{1,0:T(8,128)(2,1)S(1)}, u32[]{:S(2)}, u32[]{:S(2)}) collective-permute-start(bf16[3072,128]{1,0:T(8,128)(2,1)} %bitcast.3), channel_id=1, source_target_pairs={{0,3},{1,0},{2,1},{3,2},{4,7},{5,4},{6,5},{7,6},{8,11},{9,8},{10,9... | collective-permute-start | bytes 2359304 | tf_op jit(solution)/shard_map/ppermute | solution.py:440
  3.6 1.2 %copy-start.1 = (bf16[64,3,8,2,128]{4,3,2,1,0:T(2,128)(2,1)S(1)}, bf16[64,3,8,2,128]{4,3,2,1,0:T(2,128)(2,1)}, u32[]{:S(2)}) copy-start(bf16[64,3,8,2,128]{4,3,2,1,0:T(2,128)(2,1)} %param.4) | copy-start | bytes 2359300
  4.8 0.9 %copy-start.3 = (bf16[3,3,3,8,2,128]{5,4,3,2,1,0:T(2,128)(2,1)S(1)}, bf16[3,3,3,8,2,128]{5,4,3,2,1,0:T(2,128)(2,1)}, u32[]{:S(2)}) copy-start(bf16[3,3,3,8,2,128]{5,4,3,2,1,0:T(2,128)(2,1)} %param.5) | copy-start | bytes 331780
  5.7 7.6 %copy-start.2 = (bf16[64,3,8,2,128]{4,3,2,1,0:T(2,128)(2,1)S(1)}, bf16[64,3,8,2,128]{4,3,2,1,0:T(2,128)(2,1)}, u32[]{:S(2)}) copy-start(bf16[64,3,8,2,128]{4,3,2,1,0:T(2,128)(2,1)} %param.4) | copy-start | bytes 2359300
  6.3 11.9 %collective-permute-start = (bf16[6,64,128]{2,1,0:T(8,128)(2,1)S(1)}, bf16[6,64,128]{2,1,0:T(8,128)(2,1)S(1)}, u32[]{:S(2)}, u32[]{:S(2)}) collective-permute-start(bf16[6,64,128]{2,1,0:T(8,128)(2,1)S(1)} %get-tuple-element.38), channel_id=1, source_target_pairs={{0,96},{32,0},{64,32},{96,64},{1,97},{33,1},{65,33},{97,65},{2,98}... | collective-permute-start | bytes 294920 | tf_op jit(solution)/shard_map/ppermute | solution.py:440
  7.4 20.3 %collective-permute-start.4 = (bf16[24,64,128]{2,1,0:T(8,128)(2,1)S(1)}, bf16[24,64,128]{2,1,0:T(8,128)(2,1)S(1)}, u32[]{:S(2)}, u32[]{:S(2)}) collective-permute-start(bf16[24,64,128]{2,1,0:T(8,128)(2,1)S(1)} %get-tuple-element.47), channel_id=1, source_target_pairs={{0,28},{4,0},{8,4},{12,8},{16,12},{20,16},{24,20},{28,24},{1,29},{... | collective-permute-start | bytes 1179656 | tf_op jit(solution)/shard_map/ppermute | solution.py:440
  13.2 14.4 %collective-permute-start.5 = (bf16[26,64,128]{2,1,0:T(8,128)(2,1)S(1)}, bf16[26,64,128]{2,1,0:T(8,128)(2,1)S(1)}, u32[]{:S(2)}, u32[]{:S(2)}) collective-permute-start(bf16[26,64,128]{2,1,0:T(8,128)(2,1)S(1)} %get-tuple-element.48), channel_id=1, source_target_pairs={{0,4},{4,8},{8,12},{12,16},{16,20},{20,24},{24,28},{28,0},{1,5},{5... | collective-permute-start | bytes 1277960 | tf_op jit(solution)/shard_map/ppermute | solution.py:440
  18.2 7.9 %collective-permute-start.1 = (bf16[7,64,128]{2,1,0:T(8,128)(2,1)S(1)}, bf16[7,64,128]{2,1,0:T(8,128)(2,1)S(1)}, u32[]{:S(2)}, u32[]{:S(2)}) collective-permute-start(bf16[7,64,128]{2,1,0:T(8,128)(2,1)S(1)} %get-tuple-element.40), channel_id=1, source_target_pairs={{0,32},{32,64},{64,96},{96,0},{1,33},{33,65},{65,97},{97,1},{2,34}... | collective-permute-start | bytes 344072 | tf_op jit(solution)/shard_map/ppermute | solution.py:440
  20.9 12.8 %collective-permute-start.7 = (bf16[1536,128]{1,0:T(8,128)(2,1)S(1)}, bf16[1536,128]{1,0:T(8,128)(2,1)S(1)}, u32[]{:S(2)}, u32[]{:S(2)}) collective-permute-start(bf16[1536,128]{1,0:T(8,128)(2,1)S(1)} %slice.8), channel_id=1, source_target_pairs={{0,1},{1,2},{2,3},{3,0},{4,5},{5,6},{6,7},{7,4},{8,9},{9,10},{10,1... | collective-permute-start | bytes 1179656 | tf_op jit(solution)/shard_map/ppermute | solution.py:440
  21.0 12.7 %collective-permute-start.8 = (bf16[1536,128]{1,0:T(8,128)(2,1)S(1)}, bf16[1536,128]{1,0:T(8,128)(2,1)S(1)}, u32[]{:S(2)}, u32[]{:S(2)}) collective-permute-start(bf16[1536,128]{1,0:T(8,128)(2,1)S(1)} %slice.9), channel_id=1, source_target_pairs={{0,3},{1,0},{2,1},{3,2},{4,7},{5,4},{6,5},{7,6},{8,11},{9,8},{10,9... | collective-permute-start | bytes 1179656 | tf_op jit(solution)/shard_map/ppermute | solution.py:440
  31.3 24.8 %copy-start = (s32[3]{0:T(128)S(1)}, s32[3]{0:T(128)}, u32[]{:S(2)}) copy-start(s32[3]{0:T(128)} %dirs_ref.3) | copy-start | bytes 40
  31.3 4.0 %collective-permute-start.6 = (f32[128,384]{1,0:T(8,128)S(1)}, f32[128,384]{1,0:T(8,128)S(1)}, u32[]{:S(2)}, u32[]{:S(2)}) collective-permute-start(f32[128,384]{1,0:T(8,128)S(1)} %get-tuple-element.52), channel_id=1, source_target_pairs={{0,32},{32,0},{64,96},{96,64},{1,33},{33,1},{65,97},{97,65},{2,34}... | collective-permute-start | bytes 589832 | tf_op jit(solution)/shard_map/ppermute | solution.py:440
  35.2 1.3 %collective-permute-start.9 = (f32[128,128]{1,0:T(8,128)S(1)}, f32[128,128]{1,0:T(8,128)S(1)}, u32[]{:S(2)}, u32[]{:S(2)}) collective-permute-start(f32[128,128]{1,0:T(8,128)S(1)} %get-tuple-element.54), channel_id=1, source_target_pairs={{0,32},{32,0},{64,96},{96,64},{1,33},{33,1},{65,97},{97,65},{2,34}... | collective-permute-start | bytes 196616 | tf_op jit(solution)/shard_map/ppermute | solution.py:440
  36.5 5.7 %collective-permute-start.12 = (bf16[128,512]{1,0:T(8,128)(2,1)S(1)}, bf16[128,512]{1,0:T(8,128)(2,1)S(1)}, u32[]{:S(2)}, u32[]{:S(2)}) collective-permute-start(bf16[128,512]{1,0:T(8,128)(2,1)S(1)} %pad_maximum_fusion), channel_id=1, source_target_pairs={{0,16},{4,20},{8,24},{12,28},{16,0},{20,4},{24,8},{28,12},{32,40},... | collective-permute-start | bytes 393224 | tf_op jit(solution)/shard_map/ppermute | solution.py:453
  39.0 5.0 %collective-permute-start.11 = (bf16[128,512]{1,0:T(8,128)(2,1)S(1)}, bf16[128,512]{1,0:T(8,128)(2,1)S(1)}, u32[]{:S(2)}, u32[]{:S(2)}) collective-permute-start(bf16[128,512]{1,0:T(8,128)(2,1)S(1)} %pad_maximum_fusion), channel_id=1, source_target_pairs={{0,80},{4,84},{8,88},{12,92},{16,64},{20,68},{24,72},{28,76},{32,4... | collective-permute-start | bytes 393224 | tf_op jit(solution)/shard_map/ppermute | solution.py:453
  39.8 4.2 %collective-permute-start.10 = (bf16[128,512]{1,0:T(8,128)(2,1)S(1)}, bf16[128,512]{1,0:T(8,128)(2,1)S(1)}, u32[]{:S(2)}, u32[]{:S(2)}) collective-permute-start(bf16[128,512]{1,0:T(8,128)(2,1)S(1)} %pad_maximum_fusion), channel_id=1, source_target_pairs={{0,64},{4,68},{8,72},{12,76},{16,80},{20,84},{24,88},{28,92},{32,3... | collective-permute-start | bytes 393224 | tf_op jit(solution)/shard_map/ppermute | solution.py:453
  44.1 6.0 %collective-permute-start.15 = (bf16[128,512]{1,0:T(8,128)(2,1)S(1)}, bf16[128,512]{1,0:T(8,128)(2,1)S(1)}, u32[]{:S(2)}, u32[]{:S(2)}) collective-permute-start(bf16[128,512]{1,0:T(8,128)(2,1)S(1)} %add_convert_fusion), channel_id=1, source_target_pairs={{0,8},{4,12},{8,0},{12,4},{16,24},{20,28},{24,16},{28,20},{32,48},... | collective-permute-start | bytes 393224 | tf_op jit(solution)/shard_map/ppermute | solution.py:453
  47.8 5.1 %collective-permute-start.14 = (bf16[128,512]{1,0:T(8,128)(2,1)S(1)}, bf16[128,512]{1,0:T(8,128)(2,1)S(1)}, u32[]{:S(2)}, u32[]{:S(2)}) collective-permute-start(bf16[128,512]{1,0:T(8,128)(2,1)S(1)} %add_convert_fusion), channel_id=1, source_target_pairs={{0,12},{4,8},{8,4},{12,0},{16,28},{20,24},{24,20},{28,16},{32,112}... | collective-permute-start | bytes 393224 | tf_op jit(solution)/shard_map/ppermute | solution.py:453
  48.2 4.6 %collective-permute-start.13 = (bf16[128,512]{1,0:T(8,128)(2,1)S(1)}, bf16[128,512]{1,0:T(8,128)(2,1)S(1)}, u32[]{:S(2)}, u32[]{:S(2)}) collective-permute-start(bf16[128,512]{1,0:T(8,128)(2,1)S(1)} %add_convert_fusion), channel_id=1, source_target_pairs={{0,4},{4,0},{8,12},{12,8},{16,20},{20,16},{24,28},{28,24},{32,96},... | collective-permute-start | bytes 393224 | tf_op jit(solution)/shard_map/ppermute | solution.py:453
  52.9 4.6 %collective-permute-start.16 = (f32[128,512]{1,0:T(8,128)S(1)}, f32[128,512]{1,0:T(8,128)S(1)}, u32[]{:S(2)}, u32[]{:S(2)}) collective-permute-start(f32[128,512]{1,0:T(8,128)S(1)} %add_add_fusion.rows_ref), channel_id=1, source_target_pairs={{0,32},{32,0},{64,96},{96,64},{1,33},{33,1},{65,97},{97,65},{2,34}... | collective-permute-start | bytes 786440 | tf_op jit(solution)/shard_map/ppermute | solution.py:440
